TPU v7x, 32 devices: a whole 2x2x4 slice. The times are simulated.
32 devices in a mesh: groups: 1, row: 8 (over z, y), col: 4 (over x, core), half: 1.
Axes of the slice: x: 2, y: 2, z: 4, core: 2. Of those that a mesh axis runs over, the one named last changes fastest.
Arguments:
- tokens: bfloat16 [4096, 1024], P(('groups', 'row', 'col'), 'half'), may hold values from -6 to 6
- expert_ids: int32 [4096, 8], P(('groups', 'row', 'col')), may hold values from 0 to 31, as said below
- gates: float32 [4096, 8], P(('groups', 'row', 'col')), may hold values from 0.02 to 0.4
- w_gate: bfloat16 [32, 1024, 512], P(('row', 'col'), None, 'half'), may hold values from -0.1875 to 0.1875
- w_up: bfloat16 [32, 1024, 512], P(('row', 'col'), None, 'half'), may hold values from -0.1875 to 0.1875
- w_down: bfloat16 [32, 512, 1024], P(('row', 'col'), 'half'), may hold values from -0.25 to 0.25
- grad_out: bfloat16 [4096, 1024], P(('groups', 'row', 'col'), 'half'), may hold values from -6 to 6
Outputs:
- mixed: bfloat16 [4096, 1024], P(('groups', 'row', 'col'), 'half')
- grad_tokens: bfloat16 [4096, 1024], P(('groups', 'row', 'col'), 'half')
- grad_gates: float32 [4096, 8], P(('groups', 'row', 'col'))
- grad_w_gate: bfloat16 [32, 1024, 512], P(('groups', 'row', 'col'), None, 'half')
- grad_w_up: bfloat16 [32, 1024, 512], P(('groups', 'row', 'col'), None, 'half')
- grad_w_down: bfloat16 [32, 512, 1024], P(('groups', 'row', 'col'), 'half')
Inputs may be any that keep to these rules, and one draw needn't show every extreme that they name: `expert_ids`: the 8 experts of a token are distinct. Among the 128 tokens of each aligned block (the tokens of one index of row and col) no expert is named more than 48 times, and one expert, the same for all blocks, is named exactly 48 times in every block.
All inputs are finite; a program needn't handle non-finite values.
Results may differ from a plain program's by a relative error of at most 0.0071.
Values may be sent and summed in bfloat16 or wider, within the bound.
No kernel may reach another device: no remote copies, remote signals or barrier semaphores. Data moves between devices by JAX's collectives and lax.ppermute only.
A program may use at most 128 MiB of HBM per device.

v0:
```python
import jax
import jax.numpy as jnp
from jax import lax
from jax.sharding import PartitionSpec as P


def padded_rows(source, slot_token):
    extended = jnp.concatenate([source, jnp.zeros((1, source.shape[1]), source.dtype)])
    return extended[slot_token]


def dispatch_rows(x_block, grad_block):
    return (
        lax.all_to_all(x_block, ("row", "col"), split_axis=0, concat_axis=0, tiled=True),
        lax.all_to_all(grad_block, ("row", "col"), split_axis=0, concat_axis=0, tiled=True),
    )


def return_outputs(block):
    return lax.all_to_all(block, ("row", "col"), split_axis=0, concat_axis=0, tiled=True)


def return_grads(block):
    return lax.all_to_all(block, ("row", "col"), split_axis=0, concat_axis=0, tiled=True)


def partner_total(moved):
    return jnp.sum(moved.astype(jnp.float32), 1).astype(jnp.bfloat16)


def local(tokens, expert_ids, gates, w_gate, w_up, w_down, grad_out):
    token_count, top_count = expert_ids.shape
    expert_count = lax.axis_size("row") * lax.axis_size("col")
    half_count = lax.axis_size("half")
    average = token_count * top_count // expert_count
    capacity = min(token_count, average + average // 2)
    entry_count = token_count * top_count
    flat_ids = expert_ids.reshape(entry_count)
    expert_range = jnp.arange(expert_count, dtype=jnp.int32)
    entry_hot = (expert_ids[:, :, None] == expert_range[None, None, :]).astype(jnp.float32)
    token_hot = jnp.sum(entry_hot, 1).astype(jnp.bfloat16)
    token_range = jnp.arange(token_count, dtype=jnp.int32)
    lower = (token_range[:, None] > token_range[None, :]).astype(jnp.bfloat16)
    before = jnp.dot(lower, token_hot, preferred_element_type=jnp.float32)
    earlier = jnp.sum(before[:, None, :] * entry_hot, 2).reshape(entry_count).astype(jnp.int32)
    position = flat_ids * capacity + earlier
    slot_entry = (
        jnp.full((expert_count * capacity,), entry_count, jnp.int32)
        .at[position]
        .set(jnp.arange(entry_count, dtype=jnp.int32))
    )
    slot_token = slot_entry // top_count
    gate_flat = jnp.concatenate([gates.reshape(entry_count), jnp.zeros((1,), jnp.float32)])
    slot_gate = gate_flat[slot_entry]
    x_source = lax.all_gather(tokens, "half", axis=1, tiled=True)
    dy_source = lax.all_gather(grad_out, "half", axis=1, tiled=True)
    x_send = padded_rows(x_source, slot_token)
    grad_send = (
        slot_gate[:, None] * padded_rows(dy_source, slot_token).astype(jnp.float32)
    ).astype(jnp.bfloat16)
    block_shape = (expert_count, capacity, x_send.shape[1])
    x_recv, grad_recv = dispatch_rows(x_send.reshape(block_shape), grad_send.reshape(block_shape))
    width = x_recv.shape[2]
    own_width = width // half_count
    row_total = expert_count * capacity
    x_rows = x_recv.reshape(row_total, width)
    grad_rows = grad_recv.reshape(row_total, width)
    gate_mat = w_gate[0]
    up_mat = w_up[0]
    down_mat = w_down[0]
    pre_gate = jnp.dot(x_rows, gate_mat, preferred_element_type=jnp.float32)
    pre_up = jnp.dot(x_rows, up_mat, preferred_element_type=jnp.float32)
    sigmoid_gate = jax.nn.sigmoid(pre_gate)
    act = (pre_gate * sigmoid_gate * pre_up).astype(jnp.bfloat16)
    partial_out = jnp.dot(act, down_mat, preferred_element_type=jnp.float32).astype(jnp.bfloat16)
    out_back = return_outputs(partial_out.reshape(expert_count, capacity, width))
    contract_last = (((1,), (1,)), ((), ()))
    contract_rows = (((0,), (0,)), ((), ()))
    grad_act = lax.dot_general(
        grad_rows, down_mat, contract_last, preferred_element_type=jnp.float32
    )
    grad_pre_gate = (
        grad_act * pre_up * sigmoid_gate * (1.0 + pre_gate * (1.0 - sigmoid_gate))
    ).astype(jnp.bfloat16)
    grad_pre_up = (grad_act * pre_gate * sigmoid_gate).astype(jnp.bfloat16)
    partial_grad = lax.dot_general(
        grad_pre_gate, gate_mat, contract_last, preferred_element_type=jnp.float32
    )
    partial_grad = (
        partial_grad
        + lax.dot_general(grad_pre_up, up_mat, contract_last, preferred_element_type=jnp.float32)
    ).astype(jnp.bfloat16)
    grad_back = return_grads(partial_grad.reshape(expert_count, capacity, width))
    grad_gate_mat = lax.dot_general(
        x_rows, grad_pre_gate, contract_rows, preferred_element_type=jnp.float32
    )
    grad_up_mat = lax.dot_general(
        x_rows, grad_pre_up, contract_rows, preferred_element_type=jnp.float32
    )
    grad_down_mat = lax.dot_general(
        act, grad_rows, contract_rows, preferred_element_type=jnp.float32
    )
    back_width = out_back.shape[2]
    routed_out = out_back.reshape(row_total, back_width)[position]
    routed_grad = grad_back.reshape(row_total, back_width)[position]
    split_shape = (entry_count, half_count, own_width)
    moved_out, moved_grad = (
        lax.all_to_all(
            routed_out.reshape(split_shape), "half", split_axis=1, concat_axis=1, tiled=True
        ),
        lax.all_to_all(
            routed_grad.reshape(split_shape), "half", split_axis=1, concat_axis=1, tiled=True
        ),
    )
    expert_out = partner_total(moved_out)
    expert_grad = partner_total(moved_grad)
    expert_out = expert_out.reshape(token_count, top_count, own_width).astype(jnp.float32)
    expert_grad = expert_grad.reshape(token_count, top_count, own_width).astype(jnp.float32)
    mixed = jnp.sum(gates[:, :, None] * expert_out, 1).astype(jnp.bfloat16)
    gate_terms = jnp.sum(grad_out.astype(jnp.float32)[:, None, :] * expert_out, 2)
    grad_gates = lax.psum(gate_terms, "half")
    grad_tokens = jnp.sum(expert_grad, 1).astype(jnp.bfloat16)
    return (
        mixed,
        grad_tokens,
        grad_gates,
        grad_gate_mat.astype(jnp.bfloat16)[None],
        grad_up_mat.astype(jnp.bfloat16)[None],
        grad_down_mat.astype(jnp.bfloat16)[None],
    )


def solution(mesh):
    return jax.shard_map(
        local,
        mesh=mesh,
        in_specs=(
            P(("groups", "row", "col"), "half"),
            P(("groups", "row", "col"), None),
            P(("groups", "row", "col"), None),
            P(("row", "col"), None, "half"),
            P(("row", "col"), None, "half"),
            P(("row", "col"), "half", None),
            P(("groups", "row", "col"), "half"),
        ),
        out_specs=(
            P(("groups", "row", "col"), "half"),
            P(("groups", "row", "col"), "half"),
            P(("groups", "row", "col"), None),
            P(("groups", "row", "col"), None, "half"),
            P(("groups", "row", "col"), None, "half"),
            P(("groups", "row", "col"), "half", None),
        ),
        check_vma=False,
    )
```

profile of v0, /device:TPU:0, one launch (start us, length us, event | category | flops | bytes accessed | tf_op | source)
XLA Modules:
  0.0 339.5 jit_solution(14498442923576251223)
XLA Ops:
  3.2 4.3 %scatter_custom_fusion = s32[1536]{0:T(1024)S(1)} fusion(s32[1024]{0:T(1024)S(1)} %bitcast.57, s32[1024]{0:T(1024)S(1)} %iota.14, s32[]{:T(128)} %constant.11.clone.1), kind=kCustom, calls=%fused_computation.55 | custom fusion | bytes 6148 | tf_op jit(solution)/shard_map/scatter | solution.py:50
  8.6 5.8 %gather_fusion = bf16[1536,1024]{1,0:T(8,128)(2,1)} fusion(bf16[129,1024]{1,0:T(8,128)(2,1)S(1)} %concatenate.9, s32[2048]{0:T(1024)S(1)} %get-tuple-element.26), kind=kCustom, calls=%fused_computation | custom fusion | bytes 6297600 | tf_op jit(solution)/shard_map/gather | solution.py:9
  14.4 7.4 %all-to-all-start = ((bf16[32,48,1024]{2,1,0:T(8,128)(2,1)}), bf16[32,48,1024]{2,1,0:T(8,128)(2,1)}, u32[]{:S(2)}, u32[]{:S(2)}) async-start(bf16[32,48,1024]{2,1,0:T(8,128)(2,1)} %bitcast.54), calls=%async_computation | async-start | bytes 6291456 | tf_op jit(solution)/shard_map/all_to_all | solution.py:14
  22.0 8.4 %gather_fusion.2 = f32[1536]{0:T(1024)S(1)} fusion(f32[1025]{0:T(1024)S(1)} %pad_maximum_fusion, s32[2048]{0:T(1024)S(1)} %get-tuple-element.25), kind=kCustom, calls=%fused_computation.2 | custom fusion | bytes 18432 | tf_op jit(solution)/shard_map/gather | solution.py:54
  30.5 5.8 %gather_fusion.3 = bf16[1536,1024]{1,0:T(8,128)(2,1)} fusion(bf16[129,1024]{1,0:T(8,128)(2,1)S(1)} %concatenate.11, s32[2048]{0:T(1024)S(1)} %get-tuple-element.26), kind=kCustom, calls=%fused_computation.3 | custom fusion | bytes 6297600 | tf_op jit(solution)/shard_map/gather | solution.py:9
  36.3 4.2 %fusion = bf16[32,48,1024]{2,1,0:T(8,128)(2,1)} fusion(bf16[32,48,1024]{2,1,0:T(8,128)(2,1)} %bitcast.55, f32[32,48]{1,0:T(8,128)S(1)} %mul.85), kind=kLoop, calls=%fused_computation.7 | loop fusion | flops 4718592 | bytes 6297600 | tf_op jit(solution)/shard_map/convert_element_type | solution.py:60
  40.5 52.8 %all-to-all-done = bf16[32,48,1024]{2,1,0:T(8,128)(2,1)} async-done(((bf16[32,48,1024]{2,1,0:T(8,128)(2,1)}), bf16[32,48,1024]{2,1,0:T(8,128)(2,1)}, u32[]{:S(2)}, u32[]{:S(2)}) %all-to-all-start) | async-done | bytes 3145760 | tf_op jit(solution)/shard_map/all_to_all | solution.py:14
  93.2 4.0 %all-to-all-start.2 = ((bf16[32,48,1024]{2,1,0:T(8,128)(2,1)}), bf16[32,48,1024]{2,1,0:T(8,128)(2,1)}, u32[]{:S(2)}, u32[]{:S(2)}) async-start(bf16[32,48,1024]{2,1,0:T(8,128)(2,1)} %fusion), calls=%async_computation.2 | async-start | bytes 6291456 | tf_op jit(solution)/shard_map/all_to_all | solution.py:15
  97.3 5.4 %fusion.10 = f32[1536,512]{1,0:T(8,128)} fusion(bf16[1536,1024]{1,0:T(8,128)(2,1)} %bitcast.2, bf16[1,1024,512]{2,1,0:T(8,128)(2,1)S(1)} %copy-done.1), kind=kOutput, calls=%fused_computation.29 | convolution fusion | flops 1610612736 | bytes 7340032 | tf_op jit(solution)/shard_map/dot_general | solution.py:72
  102.7 5.3 %fusion.14 = f32[1536,512]{1,0:T(8,128)} fusion(bf16[1536,1024]{1,0:T(8,128)(2,1)} %bitcast.2, bf16[1,1024,512]{2,1,0:T(8,128)(2,1)S(1)} %copy-done.5), kind=kOutput, calls=%fused_computation.33 | convolution fusion | flops 1610612736 | bytes 7340032 | tf_op jit(solution)/shard_map/dot_general | solution.py:71
  108.1 60.7 %all-to-all-done.2 = bf16[32,48,1024]{2,1,0:T(8,128)(2,1)} async-done(((bf16[32,48,1024]{2,1,0:T(8,128)(2,1)}), bf16[32,48,1024]{2,1,0:T(8,128)(2,1)}, u32[]{:S(2)}, u32[]{:S(2)}) %all-to-all-start.2) | async-done | bytes 3145760 | tf_op jit(solution)/shard_map/all_to_all | solution.py:15
  168.7 6.9 %multiply_convert_fusion = (bf16[1536,512]{1,0:T(8,128)(2,1)S(1)}, bf16[1536,512]{1,0:T(8,128)(2,1)}, bf16[1536,512]{1,0:T(8,128)(2,1)S(1)}) fusion(f32[1536,512]{1,0:T(8,128)} %fusion.14, f32[1536,512]{1,0:T(8,128)} %fusion.10, bf16[1536,1024]{1,0:T(8,128)(2,1)} %bitcast.10, bf16[1,512,1024]{2,1,0:T(8,128)(2,1)S(1)} %copy-done), kind=kOutput, calls=%fused_computation.14 | convolution fusion | flops 1623195648 | bytes 15204352 | tf_op jit(solution)/shard_map/dot_general | solution.py:79
  175.6 3.5 %convolution_convert_fusion = bf16[1536,1024]{1,0:T(8,128)(2,1)} fusion(bf16[1536,512]{1,0:T(8,128)(2,1)S(1)} %get-tuple-element.22, bf16[1,512,1024]{2,1,0:T(8,128)(2,1)S(1)} %copy-done), kind=kOutput, calls=%fused_computation.13 | convolution fusion | flops 1612185600 | bytes 5767168 | tf_op jit(solution)/shard_map/dot_general | solution.py:75
  179.1 4.2 %all-to-all-start.1 = ((bf16[32,48,1024]{2,1,0:T(8,128)(2,1)}), bf16[32,48,1024]{2,1,0:T(8,128)(2,1)}, u32[]{:S(2)}, u32[]{:S(2)}) async-start(bf16[32,48,1024]{2,1,0:T(8,128)(2,1)} %bitcast.56), calls=%async_computation.1 | async-start | bytes 6291456 | tf_op jit(solution)/shard_map/all_to_all | solution.py:20
  183.3 3.7 %fusion.12 = f32[1536,1024]{1,0:T(8,128)S(1)} fusion(bf16[1536,512]{1,0:T(8,128)(2,1)} %get-tuple-element.21, bf16[1,1024,512]{2,1,0:T(8,128)(2,1)} %param.10), kind=kOutput, calls=%fused_computation.31 | convolution fusion | flops 1610612736 | bytes 8912896 | tf_op jit(solution)/shard_map/dot_general | solution.py:86
  187.0 3.7 %add_convert_fusion = bf16[1536,1024]{1,0:T(8,128)(2,1)} fusion(f32[1536,1024]{1,0:T(8,128)S(1)} %fusion.12, bf16[1536,512]{1,0:T(8,128)(2,1)S(1)} %get-tuple-element.20, bf16[1,1024,512]{2,1,0:T(8,128)(2,1)S(1)} %copy-done.2), kind=kOutput, calls=%fused_computation.8 | convolution fusion | flops 1613758464 | bytes 12058624 | tf_op jit(solution)/shard_map/dot_general | solution.py:91
  190.7 64.0 %all-to-all-done.1 = bf16[32,48,1024]{2,1,0:T(8,128)(2,1)} async-done(((bf16[32,48,1024]{2,1,0:T(8,128)(2,1)}), bf16[32,48,1024]{2,1,0:T(8,128)(2,1)}, u32[]{:S(2)}, u32[]{:S(2)}) %all-to-all-start.1) | async-done | bytes 3145760 | tf_op jit(solution)/shard_map/all_to_all | solution.py:20
  254.7 4.0 %all-to-all-start.3 = ((bf16[32,48,1024]{2,1,0:T(8,128)(2,1)}), bf16[32,48,1024]{2,1,0:T(8,128)(2,1)}, u32[]{:S(2)}, u32[]{:S(2)}) async-start(bf16[32,48,1024]{2,1,0:T(8,128)(2,1)} %bitcast.53), calls=%async_computation.3 | async-start | bytes 6291456 | tf_op jit(solution)/shard_map/all_to_all | solution.py:24
  259.5 5.1 %fusion.5 = bf16[1,512,1024]{2,1,0:T(8,128)(2,1)} fusion(bf16[1536,512]{1,0:T(8,128)(2,1)} %copy-done.7, bf16[1536,1024]{1,0:T(8,128)(2,1)} %bitcast.10), kind=kOutput, calls=%fused_computation.24 | convolution fusion | flops 1611137024 | bytes 5767168 | tf_op jit(solution)/shard_map/dot_general | solution.py:100
  264.7 4.8 %fusion.4 = bf16[1,1024,512]{2,1,0:T(8,128)(2,1)} fusion(bf16[1536,1024]{1,0:T(8,128)(2,1)} %bitcast.2, bf16[1536,512]{1,0:T(8,128)(2,1)S(1)} %get-tuple-element.20), kind=kOutput, calls=%fused_computation.23 | convolution fusion | flops 1611137024 | bytes 5767168 | tf_op jit(solution)/shard_map/dot_general | solution.py:97
  269.5 4.7 %fusion.3 = bf16[1,1024,512]{2,1,0:T(8,128)(2,1)} fusion(bf16[1536,1024]{1,0:T(8,128)(2,1)} %bitcast.2, bf16[1536,512]{1,0:T(8,128)(2,1)S(1)} %copy-done.6), kind=kOutput, calls=%fused_computation.22 | convolution fusion | flops 1611137024 | bytes 5767168 | tf_op jit(solution)/shard_map/dot_general | solution.py:94
  274.2 7.3 %gather_fusion.1 = bf16[1024,1024]{1,0:T(8,128)(2,1)S(1)} fusion(bf16[1536,1024]{1,0:T(8,128)(2,1)} %bitcast.7, s32[1024]{0:T(1024)S(1)} %broadcast_clamp_fusion), kind=kCustom, calls=%fused_computation.1 | custom fusion | bytes 4198400 | tf_op jit(solution)/shard_map/gather | solution.py:104
  285.5 44.6 %all-to-all-done.3 = bf16[32,48,1024]{2,1,0:T(8,128)(2,1)} async-done(((bf16[32,48,1024]{2,1,0:T(8,128)(2,1)}), bf16[32,48,1024]{2,1,0:T(8,128)(2,1)}, u32[]{:S(2)}, u32[]{:S(2)}) %all-to-all-start.3) | async-done | bytes 3145760 | tf_op jit(solution)/shard_map/all_to_all | solution.py:24
  330.1 7.3 %gather_fusion.4 = bf16[1024,1024]{1,0:T(8,128)(2,1)S(1)} fusion(bf16[1536,1024]{1,0:T(8,128)(2,1)} %bitcast.12, s32[1024]{0:T(1024)S(1)} %broadcast_clamp_fusion), kind=kCustom, calls=%fused_computation.4 | custom fusion | bytes 4198400 | tf_op jit(solution)/shard_map/gather | solution.py:105
  (37 shorter events, 11.0 us)
Async XLA Ops:
  0.6 168.1 %copy-start = (bf16[1,512,1024]{2,1,0:T(8,128)(2,1)S(1)}, bf16[1,512,1024]{2,1,0:T(8,128)(2,1)}, u32[]{:S(2)}) copy-start(bf16[1,512,1024]{2,1,0:T(8,128)(2,1)} %param.12) | copy-start | bytes 3145732
  14.4 7.4 %copy-start.4 = (f32[128,8]{0,1:T(8,128)S(1)}, f32[128,8]{0,1:T(8,128)}, u32[]{:S(2)}) copy-start(f32[128,8]{0,1:T(8,128)} %param.9) | copy-start | bytes 12292
  14.4 78.9 %all-to-all-start = ((bf16[32,48,1024]{2,1,0:T(8,128)(2,1)}), bf16[32,48,1024]{2,1,0:T(8,128)(2,1)}, u32[]{:S(2)}, u32[]{:S(2)}) async-start(bf16[32,48,1024]{2,1,0:T(8,128)(2,1)} %bitcast.54), calls=%async_computation | async-start | bytes 6291456 | tf_op jit(solution)/shard_map/all_to_all | solution.py:14
  22.0 8.5 %copy-start.3 = (bf16[128,1024]{1,0:T(8,128)(2,1)S(1)}, bf16[128,1024]{1,0:T(8,128)(2,1)}, u32[]{:S(2)}) copy-start(bf16[128,1024]{1,0:T(8,128)(2,1)} %param.13) | copy-start | bytes 786436
  40.5 56.8 %copy-start.1 = (bf16[1,1024,512]{2,1,0:T(8,128)(2,1)S(1)}, bf16[1,1024,512]{2,1,0:T(8,128)(2,1)}, u32[]{:S(2)}) copy-start(bf16[1,1024,512]{2,1,0:T(8,128)(2,1)} %param.11) | copy-start | bytes 3145732
  93.2 75.5 %all-to-all-start.2 = ((bf16[32,48,1024]{2,1,0:T(8,128)(2,1)}), bf16[32,48,1024]{2,1,0:T(8,128)(2,1)}, u32[]{:S(2)}, u32[]{:S(2)}) async-start(bf16[32,48,1024]{2,1,0:T(8,128)(2,1)} %fusion), calls=%async_computation.2 | async-start | bytes 6291456 | tf_op jit(solution)/shard_map/all_to_all | solution.py:15
  97.3 5.4 %copy-start.5 = (bf16[1,1024,512]{2,1,0:T(8,128)(2,1)S(1)}, bf16[1,1024,512]{2,1,0:T(8,128)(2,1)}, u32[]{:S(2)}) copy-start(bf16[1,1024,512]{2,1,0:T(8,128)(2,1)} %param.10) | copy-start | bytes 3145732
  175.6 3.5 %copy-start.7 = (bf16[1536,512]{1,0:T(8,128)(2,1)}, bf16[1536,512]{1,0:T(8,128)(2,1)S(1)}, u32[]{:S(2)}) copy-start(bf16[1536,512]{1,0:T(8,128)(2,1)S(1)} %get-tuple-element.22) | copy-start | bytes 4718596
  179.1 75.6 %all-to-all-start.1 = ((bf16[32,48,1024]{2,1,0:T(8,128)(2,1)}), bf16[32,48,1024]{2,1,0:T(8,128)(2,1)}, u32[]{:S(2)}, u32[]{:S(2)}) async-start(bf16[32,48,1024]{2,1,0:T(8,128)(2,1)} %bitcast.56), calls=%async_computation.1 | async-start | bytes 6291456 | tf_op jit(solution)/shard_map/all_to_all | solution.py:20
  183.3 3.7 %copy-start.2 = (bf16[1,1024,512]{2,1,0:T(8,128)(2,1)S(1)}, bf16[1,1024,512]{2,1,0:T(8,128)(2,1)}, u32[]{:S(2)}) copy-start(bf16[1,1024,512]{2,1,0:T(8,128)(2,1)} %param.11) | copy-start | bytes 3145732
  254.7 75.4 %all-to-all-start.3 = ((bf16[32,48,1024]{2,1,0:T(8,128)(2,1)}), bf16[32,48,1024]{2,1,0:T(8,128)(2,1)}, u32[]{:S(2)}, u32[]{:S(2)}) async-start(bf16[32,48,1024]{2,1,0:T(8,128)(2,1)} %bitcast.53), calls=%async_computation.3 | async-start | bytes 6291456 | tf_op jit(solution)/shard_map/all_to_all | solution.py:24
  264.7 4.8 %copy-start.6 = (bf16[1536,512]{1,0:T(8,128)(2,1)S(1)}, bf16[1536,512]{1,0:T(8,128)(2,1)}, u32[]{:S(2)}) copy-start(bf16[1536,512]{1,0:T(8,128)(2,1)} %get-tuple-element.21) | copy-start | bytes 4718596
where the time goes:
time: 340 us
  waiting for transfers between devices  222 us (65%)
  matrix products  43.2 us (13%)
  local copies, waits for them, and re-layouts  41 us (12%)
  starting transfers between devices  19.7 us (6%)
  other arithmetic  12.8 us (4%)
    all_to_all x1, waiting for transfers between devices, return_outputs(): lax.all_to_all(block, ('row', 'col'), split_axis=0, concat_axis=0, tiled=...  64 us
    all_to_all x1, waiting for transfers between devices, dispatch_rows(): lax.all_to_all(grad_block, ('row', 'col'), split_axis=0, concat_axis=0, t...  60.7 us
    all_to_all x1, waiting for transfers between devices, dispatch_rows(): lax.all_to_all(x_block, ('row', 'col'), split_axis=0, concat_axis=0, tile...  52.8 us
    all_to_all x1, waiting for transfers between devices, return_grads(): lax.all_to_all(block, ('row', 'col'), split_axis=0, concat_axis=0, tiled=...  44.6 us
    gather x2, local copies, waits for them, and re-layouts, padded_rows(): return extended[slot_token]  11.6 us
    gather x1, local copies, waits for them, and re-layouts, local(): slot_gate = gate_flat[slot_entry]  8.39 us
    all_to_all x1, starting transfers between devices, dispatch_rows(): lax.all_to_all(x_block, ('row', 'col'), split_axis=0, concat_axis=0, tile...  7.41 us
    gather x1, local copies, waits for them, and re-layouts, local(): routed_grad = grad_back.reshape(row_total, back_width)[position]  7.27 us
  transfers between devices with their start and end apart: 4, of which 4 were waited for; matrix products, arithmetic and copies ran while one was open for 19% of the time, Pallas kernels for 0%

commit v1 on v0

--- a/solution.py
+++ b/solution.py
@@ -1,6 +1,10 @@
+import functools
+
 import jax
 import jax.numpy as jnp
 from jax import lax
+from jax.experimental import pallas as pl
+from jax.experimental.pallas import tpu as pltpu
 from jax.sharding import PartitionSpec as P
 
 
@@ -28,7 +32,7 @@
     return jnp.sum(moved.astype(jnp.float32), 1).astype(jnp.bfloat16)
 
 
-def local(tokens, expert_ids, gates, w_gate, w_up, w_down, grad_out):
+def local_exchange(tokens, expert_ids, gates, w_gate, w_up, w_down, grad_out):
     token_count, top_count = expert_ids.shape
     expert_count = lax.axis_size("row") * lax.axis_size("col")
     half_count = lax.axis_size("half")
@@ -130,9 +134,269 @@
     )
 
 
+META = 16
+LEADING = (((0,), (0,)), ((), ()))
+TRAILING = (((1,), (1,)), ((), ()))
+CHIPS = 4
+VMEM = pl.BlockSpec(memory_space=pltpu.VMEM)
+SMEM = pl.BlockSpec(memory_space=pltpu.SMEM)
+
+
+def plane_fits(mesh):
+    size = mesh.shape
+    return size["groups"] == 1 and size["half"] == 1 and size["col"] == 4 and size["row"] % 2 == 0 and size["row"] <= 32
+
+
+def dot(left, right, dims=(((1,), (0,)), ((), ()))):
+    return lax.dot_general(left, right, dims, preferred_element_type=jnp.float32)
+
+
+def call(kernel, name, outs, in_specs, flops=0, moved=0, grid=()):
+    return pl.pallas_call(
+        kernel,
+        out_shape=outs,
+        grid=grid,
+        in_specs=in_specs,
+        out_specs=[VMEM] * len(outs),
+        compiler_params=pltpu.CompilerParams(vmem_limit_bytes=56 * 1024 * 1024),
+        cost_estimate=pl.CostEstimate(flops=flops, bytes_accessed=moved, transcendentals=0),
+        name=name,
+    )
+
+
+def split_parts(value):
+    first = value.astype(jnp.bfloat16)
+    rest = value - first.astype(jnp.float32)
+    second = rest.astype(jnp.bfloat16)
+    third = (rest - second.astype(jnp.float32)).astype(jnp.bfloat16)
+    return first, second, third
+
+
+def store_meta(ref, pieces):
+    tokens = pieces[0].shape[1]
+    base = ref.shape[0] - META
+    ref[base:, :] = jnp.zeros((META, ref.shape[1]), jnp.bfloat16)
+    for number, piece in enumerate(pieces):
+        piece = piece.astype(jnp.float32)
+        missing = META - piece.shape[0]
+        if missing:
+            piece = jnp.concatenate([piece, jnp.zeros((missing, tokens), jnp.float32)], 0)
+        ref[base:, number * tokens : (number + 1) * tokens] = piece.astype(jnp.bfloat16)
+
+
+def load_meta(ref, tokens, number):
+    base = ref.shape[0] - META
+    return ref[base:, number * tokens : (number + 1) * tokens].astype(jnp.float32)
+
+
+def join_kernel(tokens_ref, grad_ref, ids_ref, gates_ref, block_ref):
+    tokens = tokens_ref.shape[0]
+    block_ref[:tokens, :] = tokens_ref[...]
+    block_ref[tokens : 2 * tokens, :] = grad_ref[...]
+    store_meta(block_ref, (ids_ref[...].astype(jnp.float32).astype(jnp.bfloat16),) + split_parts(gates_ref[...]))
+
+
+def selection(table_ref, block_ref, tokens, capacity, top):
+    ids = load_meta(block_ref, tokens, 0)
+    gates = load_meta(block_ref, tokens, 1) + load_meta(block_ref, tokens, 2) + load_meta(block_ref, tokens, 3)
+    experts = [table_ref[place].astype(jnp.float32) for place in range(2 * CHIPS)]
+    live = lax.broadcasted_iota(jnp.int32, ids.shape, 0) < top
+    named = [(ids == expert) & live for expert in experts]
+    hits = jnp.concatenate([jnp.sum(jnp.where(hit, 1.0, 0.0), 0, keepdims=True) for hit in named], 0)
+    weights = [jnp.sum(jnp.where(hit, gates, 0.0), 0, keepdims=True) for hit in named]
+    row = lax.broadcasted_iota(jnp.int32, (tokens, tokens), 0)
+    column = lax.broadcasted_iota(jnp.int32, (tokens, tokens), 1)
+    earlier = dot(hits.astype(jnp.bfloat16), jnp.where(row < column, 1.0, 0.0).astype(jnp.bfloat16))
+    slot = lax.broadcasted_iota(jnp.int32, (capacity, tokens), 0).astype(jnp.float32)
+    chosen = [
+        jnp.where((slot == earlier[place : place + 1]) & (hits[place : place + 1] > 0.0), 1.0, 0.0)
+        for place in range(2 * CHIPS)
+    ]
+    return chosen, weights, named
+
+
+def pack_kernel(tokens, capacity, top, table_ref, block_ref, *out_refs):
+    chosen, weights, _ = selection(table_ref, block_ref, tokens, capacity, top)
+    stacked = jnp.concatenate(chosen, 0).astype(jnp.bfloat16)
+    slot_gate = jnp.concatenate(
+        [jnp.sum(pick * weight, 1, keepdims=True) for pick, weight in zip(chosen, weights)], 0
+    )
+    rows = dot(stacked, block_ref[:tokens, :]).astype(jnp.bfloat16)
+    grads = (slot_gate * dot(stacked, block_ref[tokens : 2 * tokens, :])).astype(jnp.bfloat16)
+    for place in range(2 * CHIPS):
+        part = slice(place * capacity, (place + 1) * capacity)
+        out_refs[place // 2][place % 2, :capacity, :] = rows[part]
+        out_refs[place // 2][place % 2, capacity:, :] = grads[part]
+
+
+def expert_kernel(capacity, *refs):
+    own_refs, partner_ref = refs[:CHIPS], refs[CHIPS]
+    gate_ref, up_ref, down_ref = refs[CHIPS + 1 : CHIPS + 4]
+    own_out, partner_out, rows_ref, grads_ref, act_ref, pre_gate_ref, pre_up_ref = refs[CHIPS + 4 :]
+    pieces = [ref[0] for ref in own_refs] + [partner_ref[chip] for chip in range(CHIPS)]
+    rows = jnp.concatenate([piece[:capacity] for piece in pieces], 0)
+    grads = jnp.concatenate([piece[capacity:] for piece in pieces], 0)
+    rows_ref[...] = rows
+    grads_ref[...] = grads
+    pre_gate = dot(rows, gate_ref[...])
+    pre_up = dot(rows, up_ref[...])
+    sigmoid_gate = jax.nn.sigmoid(pre_gate)
+    act = (pre_gate * sigmoid_gate * pre_up).astype(jnp.bfloat16)
+    act_ref[...] = act
+    out = dot(act, down_ref[...]).astype(jnp.bfloat16)
+    grad_act = dot(grads, down_ref[...], TRAILING)
+    grad_pre_gate = (
+        grad_act * pre_up * sigmoid_gate * (1.0 + pre_gate * (1.0 - sigmoid_gate))
+    ).astype(jnp.bfloat16)
+    grad_pre_up = (grad_act * pre_gate * sigmoid_gate).astype(jnp.bfloat16)
+    pre_gate_ref[...] = grad_pre_gate
+    pre_up_ref[...] = grad_pre_up
+    grad_in = (dot(grad_pre_gate, gate_ref[...], TRAILING) + dot(grad_pre_up, up_ref[...], TRAILING)).astype(
+        jnp.bfloat16
+    )
+    for number in range(2 * CHIPS):
+        part = slice(number * capacity, (number + 1) * capacity)
+        target = own_out if number < CHIPS else partner_out
+        target[number % CHIPS, :capacity, :] = out[part]
+        target[number % CHIPS, capacity:, :] = grad_in[part]
+
+
+def merge_kernel(tokens, capacity, top, table_ref, block_ref, own_ref, swapped_ref, *refs):
+    back_refs, result_ref = refs[:-1], refs[-1]
+    chosen, weights, named = selection(table_ref, block_ref, tokens, capacity, top)
+    pieces = [own_ref[0], swapped_ref[0]] + [ref[core] for ref in back_refs for core in range(2)]
+    out = jnp.concatenate([piece[:capacity] for piece in pieces], 0)
+    grad = jnp.concatenate([piece[capacity:] for piece in pieces], 0)
+    stacked = jnp.concatenate(chosen, 0).astype(jnp.bfloat16)
+    weighted = jnp.concatenate([pick * weight for pick, weight in zip(chosen, weights)], 0)
+    high, low, _ = split_parts(weighted)
+    result_ref[:tokens, :] = (dot(high, out, LEADING) + dot(low, out, LEADING)).astype(jnp.bfloat16)
+    result_ref[tokens : 2 * tokens, :] = dot(stacked, grad, LEADING).astype(jnp.bfloat16)
+    source = dot(stacked, block_ref[tokens : 2 * tokens, :])
+    terms = jnp.sum(source * out.astype(jnp.float32), 1, keepdims=True)
+    total = jnp.zeros(named[0].shape, jnp.float32)
+    for place in range(2 * CHIPS):
+        part = slice(place * capacity, (place + 1) * capacity)
+        per_token = jnp.sum(chosen[place] * terms[part], 0, keepdims=True)
+        total = total + jnp.where(named[place], per_token, 0.0)
+    store_meta(result_ref, split_parts(total))
+
+
+def total_kernel(*refs):
+    parts, (mixed_ref, grad_ref, gates_ref) = refs[:-3], refs[-3:]
+    tokens = mixed_ref.shape[0]
+    mixed = parts[0][:tokens, :].astype(jnp.float32)
+    grad = parts[0][tokens : 2 * tokens, :].astype(jnp.float32)
+    for part in parts[1:]:
+        mixed = mixed + part[:tokens, :].astype(jnp.float32)
+        grad = grad + part[tokens : 2 * tokens, :].astype(jnp.float32)
+    mixed_ref[...] = mixed.astype(jnp.bfloat16)
+    grad_ref[...] = grad.astype(jnp.bfloat16)
+    gates = sum(load_meta(part, tokens, number) for part in parts for number in range(3))
+    gates_ref[...] = gates[: gates_ref.shape[0]]
+
+
+def weight_kernel(*refs):
+    parts, (gate_ref, up_ref, down_ref) = refs[:-3], refs[-3:]
+    steps = [parts[number : number + 5] for number in range(0, len(parts), 5)]
+    gate_ref[...] = sum(dot(rows[...], gate[...], LEADING) for rows, _, _, gate, _ in steps).astype(jnp.bfloat16)
+    up_ref[...] = sum(dot(rows[...], up[...], LEADING) for rows, _, _, _, up in steps).astype(jnp.bfloat16)
+    down_ref[...] = sum(dot(act[...], grads[...], LEADING) for _, grads, act, _, _ in steps).astype(jnp.bfloat16)
+
+
+def local_plane(tokens, expert_ids, gates, w_gate, w_up, w_down, grad_out):
+    token_count, top_count = expert_ids.shape
+    width = tokens.shape[1]
+    hidden = w_gate.shape[2]
+    axes = ("row", "col")
+    plane = 2 * CHIPS
+    device_count = lax.axis_size("row") * lax.axis_size("col")
+    levels = device_count // plane
+    average = token_count * top_count // device_count
+    capacity = -(-min(token_count, average + average // 2) // 16) * 16
+    me = lax.axis_index("row") * lax.axis_size("col") + lax.axis_index("col")
+    table = (me // plane) * plane + jnp.bitwise_xor(me % plane, jnp.arange(plane, dtype=jnp.int32))
+    bf16 = functools.partial(jax.ShapeDtypeStruct, dtype=jnp.bfloat16)
+
+    def flip(value, mask):
+        pairs = [(device, device ^ mask) for device in range(device_count)]
+        return lax.ppermute(value, axes, pairs)
+
+    def climb(value, step):
+        pairs = [(device, (device + step * plane) % device_count) for device in range(device_count)]
+        return lax.ppermute(value, axes, pairs)
+
+    block_rows = 2 * token_count + META
+    row_total = plane * capacity
+    pair = bf16((2, 2 * capacity, width))
+    quad = bf16((CHIPS, 2 * capacity, width))
+    (block,) = call(join_kernel, "join", [bf16((block_rows, width))], [VMEM] * 4, 0, 4 * block_rows * width)(
+        tokens, grad_out, expert_ids.T, gates.T
+    )
+    order = [0] + sorted(range(1, levels), key=lambda step: min(step, levels - step))
+    blocks = {step: climb(block, step) if step else block for step in order}
+    pack = call(
+        functools.partial(pack_kernel, token_count, capacity, top_count),
+        "pack",
+        [pair] * CHIPS,
+        [SMEM, VMEM],
+        4 * row_total * token_count * width,
+        2 * (block_rows + 2 * row_total) * width,
+    )
+    first = pl.BlockSpec((1, 2 * capacity, width), lambda step: (0, 0, 0), memory_space=pltpu.VMEM)
+    expert = call(
+        functools.partial(expert_kernel, capacity),
+        "expert",
+        [quad, quad, bf16((row_total, width)), bf16((row_total, width))] + [bf16((row_total, hidden))] * 3,
+        [first] * CHIPS + [VMEM] * 4,
+        12 * row_total * width * hidden,
+        2 * (6 * row_total * width + 3 * row_total * hidden + 3 * width * hidden),
+        (1,),
+    )
+    merge = call(
+        functools.partial(merge_kernel, token_count, capacity, top_count),
+        "merge",
+        [bf16((block_rows, width))],
+        [SMEM, VMEM, first, first] + [VMEM] * (CHIPS - 1),
+        8 * row_total * token_count * width,
+        2 * (2 * block_rows + 2 * row_total) * width,
+        (1,),
+    )
+    saved = []
+    finished = {}
+    for step in order:
+        packed = pack(table, blocks[step])
+        arrived = [packed[0]] + [flip(packed[chip], 2 * chip) for chip in range(1, CHIPS)]
+        swapped = flip(jnp.stack([part[1] for part in arrived]), 1)
+        own_out, partner_out, *kept = expert(*arrived, swapped, w_gate[0], w_up[0], w_down[0])
+        saved.append(kept)
+        back = flip(partner_out, 1)
+        home = [flip(jnp.stack([own_out[chip], back[chip]]), 2 * chip) for chip in range(1, CHIPS)]
+        (merged,) = merge(table, blocks[step], own_out, back, *home)
+        finished[step] = climb(merged, levels - step) if step else merged
+    half_block = bf16((token_count, width))
+    mixed, grad_tokens, grad_gates = call(
+        total_kernel,
+        "total",
+        [half_block, half_block, jax.ShapeDtypeStruct((top_count, token_count), jnp.float32)],
+        [VMEM] * levels,
+        0,
+        2 * (levels + 1) * block_rows * width,
+    )(*[finished[step] for step in order])
+    grad_gate_mat, grad_up_mat, grad_down_mat = call(
+        weight_kernel,
+        "weight",
+        [bf16((width, hidden)), bf16((width, hidden)), bf16((hidden, width))],
+        [VMEM] * (5 * levels),
+        6 * levels * row_total * width * hidden,
+        2 * levels * row_total * (2 * width + 3 * hidden) + 6 * width * hidden,
+    )(*[value for kept in saved for value in kept])
+    return mixed, grad_tokens, grad_gates.T, grad_gate_mat[None], grad_up_mat[None], grad_down_mat[None]
+
+
 def solution(mesh):
     return jax.shard_map(
-        local,
+        local_plane if plane_fits(mesh) else local_exchange,
         mesh=mesh,
         in_specs=(
             P(("groups", "row", "col"), "half"),

time: 340 us -> 234 us (0.69)
  waiting for transfers between devices: 222 us -> 98 us
  Pallas kernels: 0 us -> 68.2 us
  matrix products: 43.2 us -> 0 us
  starting transfers between devices: 19.7 us -> 46.5 us
  local copies, waits for them, and re-layouts: 41 us -> 18.2 us
  other arithmetic: 12.8 us -> 1.38 us
    all_to_all x4 -> x0, waiting for transfers between devices: 222 us -> none  [the longest x1 64 us: return_outputs(): lax.all_to_all(block, ('row', 'col'), split_axis=0, concat_axis=0, tiled=...]
    ppermute x0 -> x38, waiting for transfers between devices: none -> 98 us  [the longest x32 53.8 us: flip(): return lax.ppermute(value, axes, pairs)]
    pallas_call x0 -> x15, Pallas kernels: none -> 68.2 us  [the longest x4 26.9 us: local_plane(): expert(*arrived, swapped, w_gate[0], w_up[0], w_down[0])]
    ppermute x0 -> x38, starting transfers between devices: none -> 46.5 us  [the longest x32 34.9 us: flip(): return lax.ppermute(value, axes, pairs)]
    dot_general x10 -> x0, matrix products: 43.2 us -> none  [the longest x1 6.85 us: local(): lax.dot_general(grad_rows, down_mat, contract_last, preferred_element_typ...]
    gather x5 -> x0, local copies, waits for them, and re-layouts: 34.5 us -> none  [the longest x2 11.6 us: padded_rows(): return extended[slot_token]]
    all_to_all x4 -> x0, starting transfers between devices: 19.7 us -> none  [the longest x1 7.41 us: dispatch_rows(): lax.all_to_all(x_block, ('row', 'col'), split_axis=0, concat_axis=0, tile...]
    unnamed x18 -> x96, local copies, waits for them, and re-layouts: 0.8 us -> 12.7 us
  transfers between devices with their start and end apart: 4 -> 38, of which waited for: 4 -> 12; matrix products, arithmetic and copies ran while one was open for 19% -> 1% of each run, Pallas kernels for 0% -> 27%
where the time goes in v1:
time: 234 us
  waiting for transfers between devices  98 us (42%)
  Pallas kernels  68.2 us (29%)
  starting transfers between devices  46.5 us (20%)
  local copies, waits for them, and re-layouts  18.2 us (8%)
    ppermute x32, waiting for transfers between devices, flip(): return lax.ppermute(value, axes, pairs)  53.8 us
    ppermute x6, waiting for transfers between devices, climb(): return lax.ppermute(value, axes, pairs)  44.2 us
    ppermute x32, starting transfers between devices, flip(): return lax.ppermute(value, axes, pairs)  34.9 us
    pallas_call x4, Pallas kernels, local_plane(): expert(*arrived, swapped, w_gate[0], w_up[0], w_down[0])  26.9 us
    pallas_call x4, Pallas kernels, local_plane(): merged, = merge(table, blocks[step], own_out, back, *home)  13.8 us
    unnamed x96, local copies, waits for them, and re-layouts  12.7 us
    pallas_call x1, Pallas kernels, local_plane(): call(weight_kernel, 'weight', [bf16((width, hidden)), bf16((width, hidden...  11.8 us
    ppermute x6, starting transfers between devices, climb(): return lax.ppermute(value, axes, pairs)  11.6 us
  transfers between devices with their start and end apart: 38, of which 12 were waited for; matrix products, arithmetic and copies ran while one was open for 1% of the time, Pallas kernels for 27%

profile of v1, /device:TPU:0, one launch (start us, length us, event | category | flops | bytes accessed | tf_op | source)
XLA Modules:
  0.0 233.5 jit_solution(6568142410465403474)
XLA Ops:
  2.5 3.0 %collective-permute-start.8 = (bf16[272,1024]{1,0:T(8,128)(2,1)}, bf16[272,1024]{1,0:T(8,128)(2,1)S(1)}, u32[]{:S(2)}, u32[]{:S(2)}) collective-permute-start(bf16[272,1024]{1,0:T(8,128)(2,1)} %join.1.block_ref), channel_id=1, source_target_pairs={{0,8},{1,9},{2,10},{3,11},{4,12},{5,13},{6,14},{7,15},{8,16},{9,17... | collective-permute-start | bytes 1671176 | tf_op jit(solution)/shard_map/ppermute | solution.py:327
  14.9 6.4 %collective-permute-done.8.block_ref = bf16[272,1024]{1,0:T(8,128)(2,1)S(1)} collective-permute-done((bf16[272,1024]{1,0:T(8,128)(2,1)}, bf16[272,1024]{1,0:T(8,128)(2,1)S(1)}, u32[]{:S(2)}, u32[]{:S(2)}) %collective-permute-start.8) | collective-permute-done | bytes 557088 | tf_op jit(solution)/shard_map/ppermute | solution.py:327
  24.0 2.9 %pack.5 = (bf16[2,96,1024]{2,1,0:T(8,128)(2,1)}, bf16[2,96,1024]{2,1,0:T(8,128)(2,1)}, bf16[2,96,1024]{2,1,0:T(8,128)(2,1)}, bf16[2,96,1024]{2,1,0:T(8,128)(2,1)}) custom-call(s32[8]{0:T(128)} %xor_add_fusion.table_ref, bf16[272,1024]{1,0:T(8,128)(2,1)} %copy-done.16), custom_call_target="tpu_custom_call" | custom-call | flops 201326592 | bytes 2129920 | tf_op jit(solution)/shard_map/pack/pallas_call | solution.py:368
  27.4 4.3 %collective-permute-done.18.block_ref = bf16[272,1024]{1,0:T(8,128)(2,1)S(1)} collective-permute-done((bf16[272,1024]{1,0:T(8,128)(2,1)}, bf16[272,1024]{1,0:T(8,128)(2,1)S(1)}, u32[]{:S(2)}, u32[]{:S(2)}) %collective-permute-start.18) | collective-permute-done | bytes 557088 | tf_op jit(solution)/shard_map/ppermute | solution.py:327
  33.3 2.8 %pack.6 = (bf16[2,96,1024]{2,1,0:T(8,128)(2,1)}, bf16[2,96,1024]{2,1,0:T(8,128)(2,1)}, bf16[2,96,1024]{2,1,0:T(8,128)(2,1)}, bf16[2,96,1024]{2,1,0:T(8,128)(2,1)}) custom-call(s32[8]{0:T(128)} %xor_add_fusion.table_ref, bf16[272,1024]{1,0:T(8,128)(2,1)} %copy-done.15), custom_call_target="tpu_custom_call" | custom-call | flops 201326592 | bytes 2129920 | tf_op jit(solution)/shard_map/pack/pallas_call | solution.py:368
  38.4 17.9 %collective-permute-done.28.block_ref = bf16[272,1024]{1,0:T(8,128)(2,1)S(1)} collective-permute-done((bf16[272,1024]{1,0:T(8,128)(2,1)S(1)}, bf16[272,1024]{1,0:T(8,128)(2,1)S(1)}, u32[]{:S(2)}, u32[]{:S(2)}) %collective-permute-start.28) | collective-permute-done | bytes 557088 | tf_op jit(solution)/shard_map/ppermute | solution.py:327
  61.5 2.8 %pack.7 = (bf16[2,96,1024]{2,1,0:T(8,128)(2,1)}, bf16[2,96,1024]{2,1,0:T(8,128)(2,1)}, bf16[2,96,1024]{2,1,0:T(8,128)(2,1)}, bf16[2,96,1024]{2,1,0:T(8,128)(2,1)}) custom-call(s32[8]{0:T(128)} %xor_add_fusion.table_ref, bf16[272,1024]{1,0:T(8,128)(2,1)} %copy-done.17), custom_call_target="tpu_custom_call" | custom-call | flops 201326592 | bytes 2129920 | tf_op jit(solution)/shard_map/pack/pallas_call | solution.py:368
  66.3 19.0 %collective-permute-done.20.refs_2_ = bf16[2,96,1024]{2,1,0:T(8,128)(2,1)S(1)} collective-permute-done((bf16[2,96,1024]{2,1,0:T(8,128)(2,1)}, bf16[2,96,1024]{2,1,0:T(8,128)(2,1)S(1)}, u32[]{:S(2)}, u32[]{:S(2)}) %collective-permute-start.20) | collective-permute-done | bytes 393248 | tf_op jit(solution)/shard_map/ppermute | solution.py:323
  96.9 6.7 %expert.4 = (bf16[4,96,1024]{2,1,0:T(8,128)(2,1)}, bf16[4,96,1024]{2,1,0:T(8,128)(2,1)}, bf16[384,1024]{1,0:T(8,128)(2,1)}, bf16[384,1024]{1,0:T(8,128)(2,1)}, b...) custom-call(bf16[2,96,1024]{2,1,0:T(8,128)(2,1)} %get-tuple-element.56.refs_0_, ...), custom_call_target="tpu_custom_call" | custom-call | flops 2415919104 | bytes 9043968 | tf_op jit(solution)/shard_map/expert/pallas_call | solution.py:371
  106.2 6.7 %expert.5 = (bf16[4,96,1024]{2,1,0:T(8,128)(2,1)}, bf16[4,96,1024]{2,1,0:T(8,128)(2,1)}, bf16[384,1024]{1,0:T(8,128)(2,1)}, bf16[384,1024]{1,0:T(8,128)(2,1)}, b...) custom-call(bf16[2,96,1024]{2,1,0:T(8,128)(2,1)} %get-tuple-element.62.refs_0_, ...), custom_call_target="tpu_custom_call" | custom-call | flops 2415919104 | bytes 9043968 | tf_op jit(solution)/shard_map/expert/pallas_call | solution.py:371
  113.7 6.7 %expert.6 = (bf16[4,96,1024]{2,1,0:T(8,128)(2,1)}, bf16[4,96,1024]{2,1,0:T(8,128)(2,1)}, bf16[384,1024]{1,0:T(8,128)(2,1)}, bf16[384,1024]{1,0:T(8,128)(2,1)}, b...) custom-call(bf16[2,96,1024]{2,1,0:T(8,128)(2,1)} %get-tuple-element.68.refs_0_, ...), custom_call_target="tpu_custom_call" | custom-call | flops 2415919104 | bytes 9043968 | tf_op jit(solution)/shard_map/expert/pallas_call | solution.py:371
  121.9 6.9 %expert.7 = (bf16[4,96,1024]{2,1,0:T(8,128)(2,1)}, bf16[4,96,1024]{2,1,0:T(8,128)(2,1)}, bf16[384,1024]{1,0:T(8,128)(2,1)}, bf16[384,1024]{1,0:T(8,128)(2,1)}, b...) custom-call(bf16[2,96,1024]{2,1,0:T(8,128)(2,1)} %get-tuple-element.74.refs_0_, ...), custom_call_target="tpu_custom_call" | custom-call | flops 2415919104 | bytes 9043968 | tf_op jit(solution)/shard_map/expert/pallas_call | solution.py:371
  138.4 4.6 %collective-permute-done.14.refs_0_ = bf16[2,96,1024]{2,1,0:T(8,128)(2,1)S(1)} collective-permute-done((bf16[2,96,1024]{2,1,0:T(8,128)(2,1)S(1)}, bf16[2,96,1024]{2,1,0:T(8,128)(2,1)S(1)}, u32[]{:S(2)}, u32[]{:S(2)}) %collective-permute-start.14) | collective-permute-done | bytes 393248 | tf_op jit(solution)/shard_map/ppermute | solution.py:323
  145.5 7.6 %collective-permute-done.15.refs_1_ = bf16[2,96,1024]{2,1,0:T(8,128)(2,1)S(1)} collective-permute-done((bf16[2,96,1024]{2,1,0:T(8,128)(2,1)S(1)}, bf16[2,96,1024]{2,1,0:T(8,128)(2,1)S(1)}, u32[]{:S(2)}, u32[]{:S(2)}) %collective-permute-start.15) | collective-permute-done | bytes 393248 | tf_op jit(solution)/shard_map/ppermute | solution.py:323
  155.1 4.8 %collective-permute-done.24.refs_0_ = bf16[2,96,1024]{2,1,0:T(8,128)(2,1)S(1)} collective-permute-done((bf16[2,96,1024]{2,1,0:T(8,128)(2,1)S(1)}, bf16[2,96,1024]{2,1,0:T(8,128)(2,1)S(1)}, u32[]{:S(2)}, u32[]{:S(2)}) %collective-permute-start.24) | collective-permute-done | bytes 393248 | tf_op jit(solution)/shard_map/ppermute | solution.py:323
  162.5 7.4 %collective-permute-done.25.refs_1_ = bf16[2,96,1024]{2,1,0:T(8,128)(2,1)S(1)} collective-permute-done((bf16[2,96,1024]{2,1,0:T(8,128)(2,1)S(1)}, bf16[2,96,1024]{2,1,0:T(8,128)(2,1)S(1)}, u32[]{:S(2)}, u32[]{:S(2)}) %collective-permute-start.25) | collective-permute-done | bytes 393248 | tf_op jit(solution)/shard_map/ppermute | solution.py:323
  170.7 3.4 %merge.5 = bf16[272,1024]{1,0:T(8,128)(2,1)} custom-call(s32[8]{0:T(128)} %xor_add_fusion.table_ref, bf16[272,1024]{1,0:T(8,128)(2,1)} %copy-done.16, bf16[4,96,1024]{2,1,0:T(8,128)(2,1)} %get-tuple-element.66.own_ref, bf16[4,96,1024]{2,1,0:T(8,128)(2,1)} %copy-done.4, bf16[2,96,1024]{2,1,0:T(8,128)(2,1)} %copy-done.22, bf16[2,96,1024]{2,1,0:T(8,128)(2,1)} %copy-done.23, ...), custom_call_target="tpu_custom_call" | custom-call | flops 402653184 | bytes 2686976 | tf_op jit(solution)/shard_map/merge/pallas_call | solution.py:375
  175.7 3.4 %merge.6 = bf16[272,1024]{1,0:T(8,128)(2,1)} custom-call(s32[8]{0:T(128)} %xor_add_fusion.table_ref, bf16[272,1024]{1,0:T(8,128)(2,1)} %copy-done.15, bf16[4,96,1024]{2,1,0:T(8,128)(2,1)} %get-tuple-element.72.own_ref, bf16[4,96,1024]{2,1,0:T(8,128)(2,1)} %copy-done.6, bf16[2,96,1024]{2,1,0:T(8,128)(2,1)} %copy-done.26, bf16[2,96,1024]{2,1,0:T(8,128)(2,1)} %copy-done.29, ...), custom_call_target="tpu_custom_call" | custom-call | flops 402653184 | bytes 2686976 | tf_op jit(solution)/shard_map/merge/pallas_call | solution.py:375
  179.4 7.4 %collective-permute-done.35.refs_1_ = bf16[2,96,1024]{2,1,0:T(8,128)(2,1)S(1)} collective-permute-done((bf16[2,96,1024]{2,1,0:T(8,128)(2,1)S(1)}, bf16[2,96,1024]{2,1,0:T(8,128)(2,1)S(1)}, u32[]{:S(2)}, u32[]{:S(2)}) %collective-permute-start.35) | collective-permute-done | bytes 393248 | tf_op jit(solution)/shard_map/ppermute | solution.py:323
  186.8 2.9 %collective-permute-start.27 = (bf16[272,1024]{1,0:T(8,128)(2,1)}, bf16[272,1024]{1,0:T(8,128)(2,1)S(1)}, u32[]{:S(2)}, u32[]{:S(2)}) collective-permute-start(bf16[272,1024]{1,0:T(8,128)(2,1)} %merge.6), channel_id=1, source_target_pairs={{0,8},{1,9},{2,10},{3,11},{4,12},{5,13},{6,14},{7,15},{8,16},{9,17... | collective-permute-start | bytes 1671176 | tf_op jit(solution)/shard_map/ppermute | solution.py:327
  190.5 3.4 %merge.7 = bf16[272,1024]{1,0:T(8,128)(2,1)} custom-call(s32[8]{0:T(128)} %xor_add_fusion.table_ref, bf16[272,1024]{1,0:T(8,128)(2,1)} %copy-done.17, bf16[4,96,1024]{2,1,0:T(8,128)(2,1)} %get-tuple-element.78.own_ref, bf16[4,96,1024]{2,1,0:T(8,128)(2,1)} %copy-done.5, bf16[2,96,1024]{2,1,0:T(8,128)(2,1)} %copy-done.28, bf16[2,96,1024]{2,1,0:T(8,128)(2,1)} %copy-done.30, ...), custom_call_target="tpu_custom_call" | custom-call | flops 402653184 | bytes 2686976 | tf_op jit(solution)/shard_map/merge/pallas_call | solution.py:375
  197.9 11.8 %weight.1 = (bf16[1024,512]{1,0:T(8,128)(2,1)}, bf16[1024,512]{1,0:T(8,128)(2,1)}, bf16[512,1024]{1,0:T(8,128)(2,1)}) custom-call(bf16[384,1024]{1,0:T(8,128)(2,1)} %get-tuple-element.83.refs_0_, bf16[384,1024]{1,0:T(8,128)(2,1)} %get-tuple-element.84.refs_1_, bf16[384,512]{1,0:T(8,128)(2,1)} %get-tuple-element.85.refs_2_, ...), custom_call_target="tpu_custom_call" | custom-call | flops 4831838208 | bytes 14155776 | tf_op jit(solution)/shard_map/weight/pallas_call | solution.py:386
  211.2 3.5 %merge.4.refs_0_ = bf16[272,1024]{1,0:T(8,128)(2,1)} custom-call(s32[8]{0:T(128)} %xor_add_fusion.table_ref, bf16[272,1024]{1,0:T(8,128)(2,1)} %join.1.block_ref, bf16[4,96,1024]{2,1,0:T(8,128)(2,1)} %get-tuple-element.60.own_ref, bf16[4,96,1024]{2,1,0:T(8,128)(2,1)} %copy-done, bf16[2,96,1024]{2,1,0:T(8,128)(2,1)} %copy-done.24, ...), custom_call_target="tpu_custom_call" | custom-call | flops 402653184 | bytes 2686976 | tf_op jit(solution)/shard_map/merge/pallas_call | solution.py:375
  214.7 15.5 %collective-permute-done.37.refs_3_ = bf16[272,1024]{1,0:T(8,128)(2,1)S(1)} collective-permute-done((bf16[272,1024]{1,0:T(8,128)(2,1)}, bf16[272,1024]{1,0:T(8,128)(2,1)S(1)}, u32[]{:S(2)}, u32[]{:S(2)}) %collective-permute-start.37) | collective-permute-done | bytes 557088 | tf_op jit(solution)/shard_map/ppermute | solution.py:327
  (211 shorter events, 70.3 us)
Async XLA Ops:
  5.5 26.2 %collective-permute-start.18 = (bf16[272,1024]{1,0:T(8,128)(2,1)}, bf16[272,1024]{1,0:T(8,128)(2,1)S(1)}, u32[]{:S(2)}, u32[]{:S(2)}) collective-permute-start(bf16[272,1024]{1,0:T(8,128)(2,1)} %join.1.block_ref), channel_id=1, source_target_pairs={{0,24},{1,25},{2,26},{3,27},{4,28},{5,29},{6,30},{7,31},{8,0},{9,1... | collective-permute-start | bytes 1671176 | tf_op jit(solution)/shard_map/ppermute | solution.py:327
  12.6 43.7 %collective-permute-start.28 = (bf16[272,1024]{1,0:T(8,128)(2,1)S(1)}, bf16[272,1024]{1,0:T(8,128)(2,1)S(1)}, u32[]{:S(2)}, u32[]{:S(2)}) collective-permute-start(bf16[272,1024]{1,0:T(8,128)(2,1)S(1)} %copy-done.7), channel_id=1, source_target_pairs={{0,16},{1,17},{2,18},{3,19},{4,20},{5,21},{6,22},{7,23},{8,24},{9,... | collective-permute-start | bytes 1671176 | tf_op jit(solution)/shard_map/ppermute | solution.py:327
  26.8 32.1 %collective-permute-start.9 = (bf16[2,96,1024]{2,1,0:T(8,128)(2,1)}, bf16[2,96,1024]{2,1,0:T(8,128)(2,1)S(1)}, u32[]{:S(2)}, u32[]{:S(2)}) collective-permute-start(bf16[2,96,1024]{2,1,0:T(8,128)(2,1)} %get-tuple-element.63), channel_id=1, source_target_pairs={{0,2},{1,3},{2,0},{3,1},{4,6},{5,7},{6,4},{7,5},{8,10},{9,11},{10,... | collective-permute-start | bytes 1179656 | tf_op jit(solution)/shard_map/ppermute | solution.py:323
  31.8 27.3 %collective-permute-start.10 = (bf16[2,96,1024]{2,1,0:T(8,128)(2,1)}, bf16[2,96,1024]{2,1,0:T(8,128)(2,1)S(1)}, u32[]{:S(2)}, u32[]{:S(2)}) collective-permute-start(bf16[2,96,1024]{2,1,0:T(8,128)(2,1)} %get-tuple-element.64), channel_id=1, source_target_pairs={{0,4},{1,5},{2,6},{3,7},{4,0},{5,1},{6,2},{7,3},{8,12},{9,13},{10,... | collective-permute-start | bytes 1179656 | tf_op jit(solution)/shard_map/ppermute | solution.py:323
  36.1 28.2 %collective-permute-start.11 = (bf16[2,96,1024]{2,1,0:T(8,128)(2,1)}, bf16[2,96,1024]{2,1,0:T(8,128)(2,1)S(1)}, u32[]{:S(2)}, u32[]{:S(2)}) collective-permute-start(bf16[2,96,1024]{2,1,0:T(8,128)(2,1)} %get-tuple-element.65), channel_id=1, source_target_pairs={{0,6},{1,7},{2,4},{3,5},{4,2},{5,3},{6,0},{7,1},{8,14},{9,15},{10,... | collective-permute-start | bytes 1179656 | tf_op jit(solution)/shard_map/ppermute | solution.py:323
  37.9 27.7 %collective-permute-start.19 = (bf16[2,96,1024]{2,1,0:T(8,128)(2,1)}, bf16[2,96,1024]{2,1,0:T(8,128)(2,1)S(1)}, u32[]{:S(2)}, u32[]{:S(2)}) collective-permute-start(bf16[2,96,1024]{2,1,0:T(8,128)(2,1)} %get-tuple-element.69), channel_id=1, source_target_pairs={{0,2},{1,3},{2,0},{3,1},{4,6},{5,7},{6,4},{7,5},{8,10},{9,11},{10,... | collective-permute-start | bytes 1179656 | tf_op jit(solution)/shard_map/ppermute | solution.py:323
  56.3 29.0 %collective-permute-start.20 = (bf16[2,96,1024]{2,1,0:T(8,128)(2,1)}, bf16[2,96,1024]{2,1,0:T(8,128)(2,1)S(1)}, u32[]{:S(2)}, u32[]{:S(2)}) collective-permute-start(bf16[2,96,1024]{2,1,0:T(8,128)(2,1)} %get-tuple-element.70), channel_id=1, source_target_pairs={{0,4},{1,5},{2,6},{3,7},{4,0},{5,1},{6,2},{7,3},{8,12},{9,13},{10,... | collective-permute-start | bytes 1179656 | tf_op jit(solution)/shard_map/ppermute | solution.py:323
  58.9 37.1 %collective-permute-start.3 = (bf16[4,96,1024]{2,1,0:T(8,128)(2,1)S(1)}, bf16[4,96,1024]{2,1,0:T(8,128)(2,1)S(1)}, u32[]{:S(2)}, u32[]{:S(2)}) collective-permute-start(bf16[4,96,1024]{2,1,0:T(8,128)(2,1)S(1)} %pad_maximum_fusion), channel_id=1, source_target_pairs={{0,1},{1,0},{2,3},{3,2},{4,5},{5,4},{6,7},{7,6},{8,9},{9,8},{10,11... | collective-permute-start | bytes 2359304 | tf_op jit(solution)/shard_map/ppermute | solution.py:323
  59.8 28.2 %collective-permute-start.21 = (bf16[2,96,1024]{2,1,0:T(8,128)(2,1)S(1)}, bf16[2,96,1024]{2,1,0:T(8,128)(2,1)S(1)}, u32[]{:S(2)}, u32[]{:S(2)}) collective-permute-start(bf16[2,96,1024]{2,1,0:T(8,128)(2,1)S(1)} %copy-done.47), channel_id=1, source_target_pairs={{0,6},{1,7},{2,4},{3,5},{4,2},{5,3},{6,0},{7,1},{8,14},{9,15},{10,... | collective-permute-start | bytes 1179656 | tf_op jit(solution)/shard_map/ppermute | solution.py:323
  64.3 26.0 %collective-permute-start.31 = (bf16[2,96,1024]{2,1,0:T(8,128)(2,1)}, bf16[2,96,1024]{2,1,0:T(8,128)(2,1)S(1)}, u32[]{:S(2)}, u32[]{:S(2)}) collective-permute-start(bf16[2,96,1024]{2,1,0:T(8,128)(2,1)} %get-tuple-element.77), channel_id=1, source_target_pairs={{0,6},{1,7},{2,4},{3,5},{4,2},{5,3},{6,0},{7,1},{8,14},{9,15},{10,... | collective-permute-start | bytes 1179656 | tf_op jit(solution)/shard_map/ppermute | solution.py:323
  65.6 27.2 %collective-permute-start.30 = (bf16[2,96,1024]{2,1,0:T(8,128)(2,1)}, bf16[2,96,1024]{2,1,0:T(8,128)(2,1)S(1)}, u32[]{:S(2)}, u32[]{:S(2)}) collective-permute-start(bf16[2,96,1024]{2,1,0:T(8,128)(2,1)} %get-tuple-element.76), channel_id=1, source_target_pairs={{0,4},{1,5},{2,6},{3,7},{4,0},{5,1},{6,2},{7,3},{8,12},{9,13},{10,... | collective-permute-start | bytes 1179656 | tf_op jit(solution)/shard_map/ppermute | solution.py:323
  96.0 25.0 %collective-permute-start.32 = (bf16[4,96,1024]{2,1,0:T(8,128)(2,1)S(1)}, bf16[4,96,1024]{2,1,0:T(8,128)(2,1)S(1)}, u32[]{:S(2)}, u32[]{:S(2)}) collective-permute-start(bf16[4,96,1024]{2,1,0:T(8,128)(2,1)S(1)} %pad_maximum_fusion.3), channel_id=1, source_target_pairs={{0,1},{1,0},{2,3},{3,2},{4,5},{5,4},{6,7},{7,6},{8,9},{9,8},{10,11... | collective-permute-start | bytes 2359304 | tf_op jit(solution)/shard_map/ppermute | solution.py:323
  103.6 33.1 %collective-permute-start.4 = (bf16[4,96,1024]{2,1,0:T(8,128)(2,1)}, bf16[4,96,1024]{2,1,0:T(8,128)(2,1)S(1)}, u32[]{:S(2)}, u32[]{:S(2)}) collective-permute-start(bf16[4,96,1024]{2,1,0:T(8,128)(2,1)} %get-tuple-element.61), channel_id=1, source_target_pairs={{0,1},{1,0},{2,3},{3,2},{4,5},{5,4},{6,7},{7,6},{8,9},{9,8},{10,11... | collective-permute-start | bytes 2359304 | tf_op jit(solution)/shard_map/ppermute | solution.py:323
  135.2 24.7 %collective-permute-start.24 = (bf16[2,96,1024]{2,1,0:T(8,128)(2,1)S(1)}, bf16[2,96,1024]{2,1,0:T(8,128)(2,1)S(1)}, u32[]{:S(2)}, u32[]{:S(2)}) collective-permute-start(bf16[2,96,1024]{2,1,0:T(8,128)(2,1)S(1)} %pad_maximum_fusion.10), channel_id=1, source_target_pairs={{0,2},{1,3},{2,0},{3,1},{4,6},{5,7},{6,4},{7,5},{8,10},{9,11},{10,... | collective-permute-start | bytes 1179656 | tf_op jit(solution)/shard_map/ppermute | solution.py:323
  136.8 33.2 %collective-permute-start.25 = (bf16[2,96,1024]{2,1,0:T(8,128)(2,1)S(1)}, bf16[2,96,1024]{2,1,0:T(8,128)(2,1)S(1)}, u32[]{:S(2)}, u32[]{:S(2)}) collective-permute-start(bf16[2,96,1024]{2,1,0:T(8,128)(2,1)S(1)} %pad_maximum_fusion.11), channel_id=1, source_target_pairs={{0,4},{1,5},{2,6},{3,7},{4,0},{5,1},{6,2},{7,3},{8,12},{9,13},{10,... | collective-permute-start | bytes 1179656 | tf_op jit(solution)/shard_map/ppermute | solution.py:323
  143.0 31.1 %collective-permute-start.26 = (bf16[2,96,1024]{2,1,0:T(8,128)(2,1)S(1)}, bf16[2,96,1024]{2,1,0:T(8,128)(2,1)S(1)}, u32[]{:S(2)}, u32[]{:S(2)}) collective-permute-start(bf16[2,96,1024]{2,1,0:T(8,128)(2,1)S(1)} %pad_maximum_fusion.12), channel_id=1, source_target_pairs={{0,6},{1,7},{2,4},{3,5},{4,2},{5,3},{6,0},{7,1},{8,14},{9,15},{10,... | collective-permute-start | bytes 1179656 | tf_op jit(solution)/shard_map/ppermute | solution.py:323
  153.1 26.1 %collective-permute-start.34 = (bf16[2,96,1024]{2,1,0:T(8,128)(2,1)S(1)}, bf16[2,96,1024]{2,1,0:T(8,128)(2,1)S(1)}, u32[]{:S(2)}, u32[]{:S(2)}) collective-permute-start(bf16[2,96,1024]{2,1,0:T(8,128)(2,1)S(1)} %pad_maximum_fusion.13), channel_id=1, source_target_pairs={{0,2},{1,3},{2,0},{3,1},{4,6},{5,7},{6,4},{7,5},{8,10},{9,11},{10,... | collective-permute-start | bytes 1179656 | tf_op jit(solution)/shard_map/ppermute | solution.py:323
  153.3 33.5 %collective-permute-start.35 = (bf16[2,96,1024]{2,1,0:T(8,128)(2,1)S(1)}, bf16[2,96,1024]{2,1,0:T(8,128)(2,1)S(1)}, u32[]{:S(2)}, u32[]{:S(2)}) collective-permute-start(bf16[2,96,1024]{2,1,0:T(8,128)(2,1)S(1)} %pad_maximum_fusion.14), channel_id=1, source_target_pairs={{0,4},{1,5},{2,6},{3,7},{4,0},{5,1},{6,2},{7,3},{8,12},{9,13},{10,... | collective-permute-start | bytes 1179656 | tf_op jit(solution)/shard_map/ppermute | solution.py:323
  159.9 29.8 %collective-permute-start.36 = (bf16[2,96,1024]{2,1,0:T(8,128)(2,1)S(1)}, bf16[2,96,1024]{2,1,0:T(8,128)(2,1)S(1)}, u32[]{:S(2)}, u32[]{:S(2)}) collective-permute-start(bf16[2,96,1024]{2,1,0:T(8,128)(2,1)S(1)} %pad_maximum_fusion.15), channel_id=1, source_target_pairs={{0,6},{1,7},{2,4},{3,5},{4,2},{5,3},{6,0},{7,1},{8,14},{9,15},{10,... | collective-permute-start | bytes 1179656 | tf_op jit(solution)/shard_map/ppermute | solution.py:323
  169.9 26.6 %collective-permute-start.5 = (bf16[2,96,1024]{2,1,0:T(8,128)(2,1)S(1)}, bf16[2,96,1024]{2,1,0:T(8,128)(2,1)S(1)}, u32[]{:S(2)}, u32[]{:S(2)}) collective-permute-start(bf16[2,96,1024]{2,1,0:T(8,128)(2,1)S(1)} %pad_maximum_fusion.4), channel_id=1, source_target_pairs={{0,2},{1,3},{2,0},{3,1},{4,6},{5,7},{6,4},{7,5},{8,10},{9,11},{10,... | collective-permute-start | bytes 1179656 | tf_op jit(solution)/shard_map/ppermute | solution.py:323
  174.1 35.5 %collective-permute-start.6 = (bf16[2,96,1024]{2,1,0:T(8,128)(2,1)S(1)}, bf16[2,96,1024]{2,1,0:T(8,128)(2,1)S(1)}, u32[]{:S(2)}, u32[]{:S(2)}) collective-permute-start(bf16[2,96,1024]{2,1,0:T(8,128)(2,1)S(1)} %pad_maximum_fusion.5), channel_id=1, source_target_pairs={{0,4},{1,5},{2,6},{3,7},{4,0},{5,1},{6,2},{7,3},{8,12},{9,13},{10,... | collective-permute-start | bytes 1179656 | tf_op jit(solution)/shard_map/ppermute | solution.py:323
  179.2 35.5 %collective-permute-start.17 = (bf16[272,1024]{1,0:T(8,128)(2,1)S(1)}, bf16[272,1024]{1,0:T(8,128)(2,1)S(1)}, u32[]{:S(2)}, u32[]{:S(2)}) collective-permute-start(bf16[272,1024]{1,0:T(8,128)(2,1)S(1)} %copy-done.18), channel_id=1, source_target_pairs={{0,24},{1,25},{2,26},{3,27},{4,28},{5,29},{6,30},{7,31},{8,0},{9,1... | collective-permute-start | bytes 1671176 | tf_op jit(solution)/shard_map/ppermute | solution.py:327
  186.8 27.9 %collective-permute-start.27 = (bf16[272,1024]{1,0:T(8,128)(2,1)}, bf16[272,1024]{1,0:T(8,128)(2,1)S(1)}, u32[]{:S(2)}, u32[]{:S(2)}) collective-permute-start(bf16[272,1024]{1,0:T(8,128)(2,1)} %merge.6), channel_id=1, source_target_pairs={{0,8},{1,9},{2,10},{3,11},{4,12},{5,13},{6,14},{7,15},{8,16},{9,17... | collective-permute-start | bytes 1671176 | tf_op jit(solution)/shard_map/ppermute | solution.py:327
  193.9 36.3 %collective-permute-start.37 = (bf16[272,1024]{1,0:T(8,128)(2,1)}, bf16[272,1024]{1,0:T(8,128)(2,1)S(1)}, u32[]{:S(2)}, u32[]{:S(2)}) collective-permute-start(bf16[272,1024]{1,0:T(8,128)(2,1)} %merge.7), channel_id=1, source_target_pairs={{0,16},{1,17},{2,18},{3,19},{4,20},{5,21},{6,22},{7,23},{8,24},{9,... | collective-permute-start | bytes 1671176 | tf_op jit(solution)/shard_map/ppermute | solution.py:327
  (69 other events, 655.4 us)

commit v2 on v1

--- a/solution.py
+++ b/solution.py
@@ -138,6 +138,15 @@
 LEADING = (((0,), (0,)), ((), ()))
 TRAILING = (((1,), (1,)), ((), ()))
 CHIPS = 4
+COST = {'join': 1.0, 'pack': 0, 'expert': 0, 'merge': 0, 'weight': 0}
+WHEN = 0
+FAR = 0
+WPOS = 1
+BEHIND = 1
+STRICT = 0
+AHEAD = 1
+WEIGHT_A = 1
+WEIGHT_B = 2
 VMEM = pl.BlockSpec(memory_space=pltpu.VMEM)
 SMEM = pl.BlockSpec(memory_space=pltpu.SMEM)
 
@@ -152,14 +161,19 @@
 
 
 def call(kernel, name, outs, in_specs, flops=0, moved=0, grid=()):
+    used = len(in_specs)
+
+    def ordered(*refs):
+        kernel(*refs[:used], *refs[used + 1 :])
+
     return pl.pallas_call(
-        kernel,
+        ordered,
         out_shape=outs,
         grid=grid,
-        in_specs=in_specs,
+        in_specs=in_specs + [pl.BlockSpec(memory_space=pl.ANY)],
         out_specs=[VMEM] * len(outs),
         compiler_params=pltpu.CompilerParams(vmem_limit_bytes=56 * 1024 * 1024),
-        cost_estimate=pl.CostEstimate(flops=flops, bytes_accessed=moved, transcendentals=0),
+        cost_estimate=pl.CostEstimate(flops=int(flops * COST[name]), bytes_accessed=moved if COST[name] > 0.5 else 0, transcendentals=0),
         name=name,
     )
 
@@ -230,48 +244,47 @@
 
 
 def expert_kernel(capacity, *refs):
-    own_refs, partner_ref = refs[:CHIPS], refs[CHIPS]
-    gate_ref, up_ref, down_ref = refs[CHIPS + 1 : CHIPS + 4]
-    own_out, partner_out, rows_ref, grads_ref, act_ref, pre_gate_ref, pre_up_ref = refs[CHIPS + 4 :]
-    pieces = [ref[0] for ref in own_refs] + [partner_ref[chip] for chip in range(CHIPS)]
-    rows = jnp.concatenate([piece[:capacity] for piece in pieces], 0)
-    grads = jnp.concatenate([piece[capacity:] for piece in pieces], 0)
-    rows_ref[...] = rows
-    grads_ref[...] = grads
-    pre_gate = dot(rows, gate_ref[...])
-    pre_up = dot(rows, up_ref[...])
-    sigmoid_gate = jax.nn.sigmoid(pre_gate)
-    act = (pre_gate * sigmoid_gate * pre_up).astype(jnp.bfloat16)
-    act_ref[...] = act
-    out = dot(act, down_ref[...]).astype(jnp.bfloat16)
-    grad_act = dot(grads, down_ref[...], TRAILING)
-    grad_pre_gate = (
-        grad_act * pre_up * sigmoid_gate * (1.0 + pre_gate * (1.0 - sigmoid_gate))
-    ).astype(jnp.bfloat16)
-    grad_pre_up = (grad_act * pre_gate * sigmoid_gate).astype(jnp.bfloat16)
-    pre_gate_ref[...] = grad_pre_gate
-    pre_up_ref[...] = grad_pre_up
-    grad_in = (dot(grad_pre_gate, gate_ref[...], TRAILING) + dot(grad_pre_up, up_ref[...], TRAILING)).astype(
-        jnp.bfloat16
-    )
-    for number in range(2 * CHIPS):
-        part = slice(number * capacity, (number + 1) * capacity)
-        target = own_out if number < CHIPS else partner_out
-        target[number % CHIPS, :capacity, :] = out[part]
-        target[number % CHIPS, capacity:, :] = grad_in[part]
-
-
-def merge_kernel(tokens, capacity, top, table_ref, block_ref, own_ref, swapped_ref, *refs):
-    back_refs, result_ref = refs[:-1], refs[-1]
+    in_refs, weight_refs, out_refs = refs[:CHIPS], refs[CHIPS : CHIPS + 6], refs[CHIPS + 6 : 2 * CHIPS + 6]
+    rows_ref, grads_ref, act_ref, pre_gate_ref, pre_up_ref = refs[2 * CHIPS + 6 :]
+    for core in range(2):
+        gate_ref, up_ref, down_ref = weight_refs[3 * core : 3 * core + 3]
+        rows = jnp.concatenate([ref[core, :capacity] for ref in in_refs], 0)
+        grads = jnp.concatenate([ref[core, capacity:] for ref in in_refs], 0)
+        rows_ref[core] = rows
+        grads_ref[core] = grads
+        pre_gate = dot(rows, gate_ref[...])
+        pre_up = dot(rows, up_ref[...])
+        sigmoid_gate = jax.nn.sigmoid(pre_gate)
+        act = (pre_gate * sigmoid_gate * pre_up).astype(jnp.bfloat16)
+        act_ref[core] = act
+        out = dot(act, down_ref[...]).astype(jnp.bfloat16)
+        grad_act = dot(grads, down_ref[...], TRAILING)
+        grad_pre_gate = (
+            grad_act * pre_up * sigmoid_gate * (1.0 + pre_gate * (1.0 - sigmoid_gate))
+        ).astype(jnp.bfloat16)
+        grad_pre_up = (grad_act * pre_gate * sigmoid_gate).astype(jnp.bfloat16)
+        pre_gate_ref[core] = grad_pre_gate
+        pre_up_ref[core] = grad_pre_up
+        grad_in = (
+            dot(grad_pre_gate, gate_ref[...], TRAILING) + dot(grad_pre_up, up_ref[...], TRAILING)
+        ).astype(jnp.bfloat16)
+        for chip in range(CHIPS):
+            part = slice(chip * capacity, (chip + 1) * capacity)
+            out_refs[chip][core, :capacity, :] = out[part]
+            out_refs[chip][core, capacity:, :] = grad_in[part]
+
+
+def merge_kernel(tokens, capacity, top, before, table_ref, block_ref, *refs):
+    back_refs, earlier_refs, out_refs = refs[:CHIPS], refs[CHIPS : CHIPS + before], refs[CHIPS + before :]
     chosen, weights, named = selection(table_ref, block_ref, tokens, capacity, top)
-    pieces = [own_ref[0], swapped_ref[0]] + [ref[core] for ref in back_refs for core in range(2)]
+    pieces = [ref[core] for ref in back_refs for core in range(2)]
     out = jnp.concatenate([piece[:capacity] for piece in pieces], 0)
     grad = jnp.concatenate([piece[capacity:] for piece in pieces], 0)
     stacked = jnp.concatenate(chosen, 0).astype(jnp.bfloat16)
     weighted = jnp.concatenate([pick * weight for pick, weight in zip(chosen, weights)], 0)
     high, low, _ = split_parts(weighted)
-    result_ref[:tokens, :] = (dot(high, out, LEADING) + dot(low, out, LEADING)).astype(jnp.bfloat16)
-    result_ref[tokens : 2 * tokens, :] = dot(stacked, grad, LEADING).astype(jnp.bfloat16)
+    mixed = dot(high, out, LEADING) + dot(low, out, LEADING)
+    grad_in = dot(stacked, grad, LEADING)
     source = dot(stacked, block_ref[tokens : 2 * tokens, :])
     terms = jnp.sum(source * out.astype(jnp.float32), 1, keepdims=True)
     total = jnp.zeros(named[0].shape, jnp.float32)
@@ -279,29 +292,35 @@
         part = slice(place * capacity, (place + 1) * capacity)
         per_token = jnp.sum(chosen[place] * terms[part], 0, keepdims=True)
         total = total + jnp.where(named[place], per_token, 0.0)
-    store_meta(result_ref, split_parts(total))
-
-
-def total_kernel(*refs):
-    parts, (mixed_ref, grad_ref, gates_ref) = refs[:-3], refs[-3:]
-    tokens = mixed_ref.shape[0]
-    mixed = parts[0][:tokens, :].astype(jnp.float32)
-    grad = parts[0][tokens : 2 * tokens, :].astype(jnp.float32)
-    for part in parts[1:]:
-        mixed = mixed + part[:tokens, :].astype(jnp.float32)
-        grad = grad + part[tokens : 2 * tokens, :].astype(jnp.float32)
-    mixed_ref[...] = mixed.astype(jnp.bfloat16)
-    grad_ref[...] = grad.astype(jnp.bfloat16)
-    gates = sum(load_meta(part, tokens, number) for part in parts for number in range(3))
-    gates_ref[...] = gates[: gates_ref.shape[0]]
-
-
-def weight_kernel(*refs):
-    parts, (gate_ref, up_ref, down_ref) = refs[:-3], refs[-3:]
-    steps = [parts[number : number + 5] for number in range(0, len(parts), 5)]
-    gate_ref[...] = sum(dot(rows[...], gate[...], LEADING) for rows, _, _, gate, _ in steps).astype(jnp.bfloat16)
-    up_ref[...] = sum(dot(rows[...], up[...], LEADING) for rows, _, _, _, up in steps).astype(jnp.bfloat16)
-    down_ref[...] = sum(dot(act[...], grads[...], LEADING) for _, grads, act, _, _ in steps).astype(jnp.bfloat16)
+    for ref in earlier_refs:
+        mixed = mixed + ref[:tokens, :].astype(jnp.float32)
+        grad_in = grad_in + ref[tokens : 2 * tokens, :].astype(jnp.float32)
+        total = total + sum(load_meta(ref, tokens, number) for number in range(3))
+    if len(out_refs) == 1:
+        out_refs[0][:tokens, :] = mixed.astype(jnp.bfloat16)
+        out_refs[0][tokens : 2 * tokens, :] = grad_in.astype(jnp.bfloat16)
+        store_meta(out_refs[0], split_parts(total))
+    else:
+        out_refs[0][...] = mixed.astype(jnp.bfloat16)
+        out_refs[1][...] = grad_in.astype(jnp.bfloat16)
+        out_refs[2][...] = total[:top]
+
+
+def weight_kernel(levels, *refs):
+    steps = [refs[number : number + 5] for number in range(0, 5 * levels, 5)]
+    gate_mat = sum(dot(rows[0], gate[0], LEADING) for rows, _, _, gate, _ in steps)
+    up_mat = sum(dot(rows[0], up[0], LEADING) for rows, _, _, _, up in steps)
+    down_mat = sum(dot(act[0], grads[0], LEADING) for _, grads, act, _, _ in steps)
+    width, hidden = gate_mat.shape
+    if len(refs) == 5 * levels + 1:
+        refs[-1][:width, :hidden] = gate_mat.astype(jnp.bfloat16)
+        refs[-1][:width, hidden:] = up_mat.astype(jnp.bfloat16)
+        refs[-1][width:, :] = down_mat.astype(jnp.bfloat16)
+        return
+    other_ref, (gate_ref, up_ref, down_ref) = refs[5 * levels], refs[-3:]
+    gate_ref[...] = (gate_mat + other_ref[:width, :hidden].astype(jnp.float32)).astype(jnp.bfloat16)
+    up_ref[...] = (up_mat + other_ref[:width, hidden:].astype(jnp.float32)).astype(jnp.bfloat16)
+    down_ref[...] = (down_mat + other_ref[width:, :].astype(jnp.float32)).astype(jnp.bfloat16)
 
 
 def local_plane(tokens, expert_ids, gates, w_gate, w_up, w_down, grad_out):
@@ -329,12 +348,11 @@
     block_rows = 2 * token_count + META
     row_total = plane * capacity
     pair = bf16((2, 2 * capacity, width))
-    quad = bf16((CHIPS, 2 * capacity, width))
+    half_rows = row_total // 2
     (block,) = call(join_kernel, "join", [bf16((block_rows, width))], [VMEM] * 4, 0, 4 * block_rows * width)(
-        tokens, grad_out, expert_ids.T, gates.T
-    )
-    order = [0] + sorted(range(1, levels), key=lambda step: min(step, levels - step))
-    blocks = {step: climb(block, step) if step else block for step in order}
+        tokens, grad_out, expert_ids.T, gates.T, gates
+    )
+    order = list(range(levels))
     pack = call(
         functools.partial(pack_kernel, token_count, capacity, top_count),
         "pack",
@@ -343,55 +361,97 @@
         4 * row_total * token_count * width,
         2 * (block_rows + 2 * row_total) * width,
     )
-    first = pl.BlockSpec((1, 2 * capacity, width), lambda step: (0, 0, 0), memory_space=pltpu.VMEM)
+    kept_shapes = [bf16((2, half_rows, size)) for size in (width, width, hidden, hidden, hidden)]
     expert = call(
         functools.partial(expert_kernel, capacity),
         "expert",
-        [quad, quad, bf16((row_total, width)), bf16((row_total, width))] + [bf16((row_total, hidden))] * 3,
-        [first] * CHIPS + [VMEM] * 4,
+        [pair] * CHIPS + kept_shapes,
+        [VMEM] * (CHIPS + 6),
         12 * row_total * width * hidden,
-        2 * (6 * row_total * width + 3 * row_total * hidden + 3 * width * hidden),
-        (1,),
-    )
-    merge = call(
-        functools.partial(merge_kernel, token_count, capacity, top_count),
-        "merge",
-        [bf16((block_rows, width))],
-        [SMEM, VMEM, first, first] + [VMEM] * (CHIPS - 1),
-        8 * row_total * token_count * width,
-        2 * (2 * block_rows + 2 * row_total) * width,
-        (1,),
-    )
-    saved = []
-    finished = {}
-    for step in order:
-        packed = pack(table, blocks[step])
-        arrived = [packed[0]] + [flip(packed[chip], 2 * chip) for chip in range(1, CHIPS)]
-        swapped = flip(jnp.stack([part[1] for part in arrived]), 1)
-        own_out, partner_out, *kept = expert(*arrived, swapped, w_gate[0], w_up[0], w_down[0])
-        saved.append(kept)
-        back = flip(partner_out, 1)
-        home = [flip(jnp.stack([own_out[chip], back[chip]]), 2 * chip) for chip in range(1, CHIPS)]
-        (merged,) = merge(table, blocks[step], own_out, back, *home)
-        finished[step] = climb(merged, levels - step) if step else merged
+        2 * (6 * row_total * width + 3 * row_total * hidden + 6 * width * hidden),
+    )
     half_block = bf16((token_count, width))
-    mixed, grad_tokens, grad_gates = call(
-        total_kernel,
-        "total",
-        [half_block, half_block, jax.ShapeDtypeStruct((top_count, token_count), jnp.float32)],
-        [VMEM] * levels,
-        0,
-        2 * (levels + 1) * block_rows * width,
-    )(*[finished[step] for step in order])
-    grad_gate_mat, grad_up_mat, grad_down_mat = call(
-        weight_kernel,
-        "weight",
-        [bf16((width, hidden)), bf16((width, hidden)), bf16((hidden, width))],
-        [VMEM] * (5 * levels),
-        6 * levels * row_total * width * hidden,
-        2 * levels * row_total * (2 * width + 3 * hidden) + 6 * width * hidden,
-    )(*[value for kept in saved for value in kept])
-    return mixed, grad_tokens, grad_gates.T, grad_gate_mat[None], grad_up_mat[None], grad_down_mat[None]
+    results_shapes = [half_block, half_block, jax.ShapeDtypeStruct((top_count, token_count), jnp.float32)]
+
+    def merge(before, final):
+        return call(
+            functools.partial(merge_kernel, token_count, capacity, top_count, before),
+            "merge",
+            results_shapes if final else [bf16((block_rows, width))],
+            [SMEM] + [VMEM] * (1 + CHIPS + before),
+            8 * row_total * token_count * width,
+            2 * (2 * block_rows + 2 * row_total) * width,
+        )
+
+    def weight(core, partials):
+        specs = [
+            pl.BlockSpec((1,) + shape.shape[1:], lambda step: (core, 0, 0), memory_space=pltpu.VMEM) for shape in kept_shapes
+        ]
+        return call(
+            functools.partial(weight_kernel, levels),
+            "weight",
+            [bf16((width, hidden)), bf16((width, hidden)), bf16((hidden, width))]
+            if partials
+            else [bf16((width + hidden, 2 * hidden))],
+            specs * levels + [VMEM] * partials,
+            3 * levels * row_total * width * hidden,
+            levels * row_total * (2 * width + 3 * hidden) + 6 * width * hidden,
+            (1,),
+        )
+
+    def after(value, *earlier):
+        return lax.optimization_barrier((value,) + earlier)[0]
+
+    moved = []
+
+    def exchange(parts):
+        earlier = moved[-BEHIND] if len(moved) >= BEHIND else None
+        received = [parts[0]]
+        for chip in range(1, CHIPS):
+            part = after(parts[chip], *(earlier[1:] if STRICT else earlier[chip : chip + 1])) if earlier else parts[chip]
+            received.append(flip(part, 2 * chip))
+        moved.append(received)
+        return received
+
+    mats = [w_gate[0], w_up[0], w_down[0]]
+    blocks = {0: block}
+    for step in order[1:]:
+        blocks[step] = climb(block, step)
+    arrived, results, kept = {}, {}, {}
+    last = block
+    for turn in range(levels + AHEAD):
+        if turn == min(WHEN, levels - 1):
+            for mat in mats[:3]:
+                mats.append(flip(mat, 1))
+            last = after(last, *mats[3:])
+        if turn < levels:
+            packed = pack(table, blocks[order[turn]], last)
+            last = packed[0]
+            arrived[order[turn]] = exchange(packed)
+        if turn >= AHEAD:
+            step = order[turn - AHEAD]
+            outs = expert(*arrived[step], *mats, last)
+            last = outs[0]
+            results[step], kept[step] = outs[:CHIPS], outs[CHIPS:]
+    homeward = (sorted(order[1:], key=lambda step: -min(step, levels - step)) if FAR else order[1:]) + order[:1]
+    returned = {step: exchange(results[step]) for step in homeward}
+    saved = [value for step in order for value in kept[step]]
+    sent = []
+    for turn, step in enumerate(homeward):
+        if turn == WPOS:
+            (partial,) = weight(1, 0)(*saved, last)
+            last = partial
+            partial = flip(partial, 1)
+        if turn == levels - 1:
+            grad_mats = weight(0, 1)(*saved, partial, last)
+            last = grad_mats[0]
+        earlier, final = (sent, True) if step == 0 else ([], False)
+        merged = merge(len(earlier), final)(table, blocks[step], *returned[step], *earlier, last)
+        last = merged[0]
+        if step:
+            sent.append(climb(merged[0], levels - step))
+    mixed, grad_tokens, grad_gates = merged
+    return (mixed, grad_tokens, grad_gates.T) + tuple(mat[None] for mat in grad_mats)
 
 
 def solution(mesh):

time: 234 us -> 200 us (0.85)
  waiting for transfers between devices: 98 us -> 46.6 us
  starting transfers between devices: 46.5 us -> 66.6 us
  local copies, waits for them, and re-layouts: 18.2 us -> 7.07 us
  Pallas kernels: 68.2 us -> 77.8 us
    ppermute x6, waiting for transfers between devices: 44.2 us -> 6.54 us  [climb(): return lax.ppermute(value, axes, pairs)]
    ppermute x6, starting transfers between devices: 11.6 us -> 35.2 us  [climb(): return lax.ppermute(value, axes, pairs)]
    ppermute x32 -> x28, waiting for transfers between devices: 53.8 us -> 40 us  [flip(): return lax.ppermute(value, axes, pairs)]
    pallas_call x14, Pallas kernels: 66.3 us -> 75.9 us  [the longest x4 34.2 us: local_plane(): outs = expert(*arrived[step], *mats, last)]
    unnamed x96 -> x83, local copies, waits for them, and re-layouts: 12.7 us -> 7.07 us
    slice x31 -> x0, local copies, waits for them, and re-layouts: 5.47 us -> none  [the longest x23 4.04 us: local_plane(): swapped = flip(jnp.stack([part[1] for part in arrived]), 1)]
    ppermute x32 -> x28, starting transfers between devices: 34.9 us -> 31.4 us  [flip(): return lax.ppermute(value, axes, pairs)]
  transfers between devices with their start and end apart: 38 -> 34, of which waited for: 12 -> 11; matrix products, arithmetic and copies ran while one was open for 1% -> 1% of each run, Pallas kernels for 27% -> 31%
where the time goes in v2:
time: 200 us; the launch traced here: 199 us
  Pallas kernels  77.8 us (39%)
  starting transfers between devices  66.6 us (33%)
  waiting for transfers between devices  46.6 us (23%)
  local copies, waits for them, and re-layouts  7.07 us (4%)
    ppermute x28, waiting for transfers between devices, flip(): return lax.ppermute(value, axes, pairs)  40 us
    ppermute x6, starting transfers between devices, climb(): return lax.ppermute(value, axes, pairs)  35.2 us
    pallas_call x4, Pallas kernels, local_plane(): outs = expert(*arrived[step], *mats, last)  34.2 us
    ppermute x28, starting transfers between devices, flip(): return lax.ppermute(value, axes, pairs)  31.4 us
    pallas_call x4, Pallas kernels, local_plane(): merge(len(earlier), final)  14 us
    pallas_call x4, Pallas kernels, local_plane(): packed = pack(table, blocks[order[turn]], last)  11.8 us
    pallas_call x1, Pallas kernels, local_plane(): grad_mats = weight(0, 1)(*saved, partial, last)  8.08 us
    pallas_call x1, Pallas kernels, local_plane(): partial, = weight(1, 0)(*saved, last)  7.84 us
  transfers between devices with their start and end apart: 34, of which 11 were waited for; matrix products, arithmetic and copies ran while one was open for 1% of the time, Pallas kernels for 31%

profile of v2, /device:TPU:0, one launch (start us, length us, event | category | flops | bytes accessed | tf_op | source)
XLA Modules:
  0.0 199.5 jit_solution(12605626629845736214)
XLA Ops:
  8.2 3.2 %pack.4 = (bf16[2,96,1024]{2,1,0:T(8,128)(2,1)}, bf16[2,96,1024]{2,1,0:T(8,128)(2,1)}, bf16[2,96,1024]{2,1,0:T(8,128)(2,1)}, bf16[2,96,1024]{2,1,0:T(8,128)(2,1)}) custom-call(s32[8]{0:T(128)} %xor_add_fusion.refs_0_, bf16[272,1024]{1,0:T(8,128)(2,1)} %join.1.refs_1_.refs_2_, bf16[272,1024]{1,0:T(8,128)(2,1)} %join.1.refs_1_.refs_2_), custom_call_target="tpu_custom_call" | custom-call | tf_op jit(solution)/shard_map/pack/pallas_call | solution.py:428
  17.5 6.0 %collective-permute-done.6.refs_1_ = bf16[272,1024]{1,0:T(8,128)(2,1)} collective-permute-done((bf16[272,1024]{1,0:T(8,128)(2,1)}, bf16[272,1024]{1,0:T(8,128)(2,1)}, u32[]{:S(2)}, u32[]{:S(2)}) %collective-permute-start.6) | collective-permute-done | bytes 557088 | tf_op jit(solution)/shard_map/ppermute | solution.py:346
  23.5 2.8 %pack.5 = (bf16[2,96,1024]{2,1,0:T(8,128)(2,1)}, bf16[2,96,1024]{2,1,0:T(8,128)(2,1)}, bf16[2,96,1024]{2,1,0:T(8,128)(2,1)}, bf16[2,96,1024]{2,1,0:T(8,128)(2,1)}) custom-call(s32[8]{0:T(128)} %xor_add_fusion.refs_0_, bf16[272,1024]{1,0:T(8,128)(2,1)} %collective-permute-done.6.refs_1_, bf16[2,96,1024]{2,1,0:T(8,128)(2,1)} %get-tuple-element.87.refs_2_.refs_0_), custom_call_target="tpu_custom_call" | custom-call | tf_op jit(solution)/shard_map/pack/pallas_call | solution.py:428
  29.0 3.9 %collective-permute-done.4.refs_2_ = bf16[2,96,1024]{2,1,0:T(8,128)(2,1)S(1)} collective-permute-done((bf16[2,96,1024]{2,1,0:T(8,128)(2,1)}, bf16[2,96,1024]{2,1,0:T(8,128)(2,1)S(1)}, u32[]{:S(2)}, u32[]{:S(2)}) %collective-permute-start.4) | collective-permute-done | bytes 393248 | tf_op jit(solution)/shard_map/ppermute | solution.py:342
  34.5 3.5 %collective-permute-start.7 = (bf16[272,1024]{1,0:T(8,128)(2,1)}, bf16[272,1024]{1,0:T(8,128)(2,1)S(1)}, u32[]{:S(2)}, u32[]{:S(2)}) collective-permute-start(bf16[272,1024]{1,0:T(8,128)(2,1)} %join.1.refs_1_.refs_2_), channel_id=1, source_target_pairs={{0,24},{1,25},{2,26},{3,27},{4,28},{5,29},{6,30},{7,31},{8,0},{9,1... | collective-permute-start | bytes 1671176 | tf_op jit(solution)/shard_map/ppermute | solution.py:346
  38.1 8.5 %expert.4 = (bf16[2,96,1024]{2,1,0:T(8,128)(2,1)}, bf16[2,96,1024]{2,1,0:T(8,128)(2,1)}, bf16[2,96,1024]{2,1,0:T(8,128)(2,1)}, bf16[2,96,1024]{2,1,0:T(8,128)(2,...) custom-call(bf16[2,96,1024]{2,1,0:T(8,128)(2,1)} %get-tuple-element., ...), custom_call_target="tpu_custom_call" | custom-call | tf_op jit(solution)/shard_map/expert/pallas_call | solution.py:433
  54.5 8.4 %expert.5 = (bf16[2,96,1024]{2,1,0:T(8,128)(2,1)}, bf16[2,96,1024]{2,1,0:T(8,128)(2,1)}, bf16[2,96,1024]{2,1,0:T(8,128)(2,1)}, bf16[2,96,1024]{2,1,0:T(8,128)(2,...) custom-call(bf16[2,96,1024]{2,1,0:T(8,128)(2,1)} %get-tuple-element., ...), custom_call_target="tpu_custom_call" | custom-call | tf_op jit(solution)/shard_map/expert/pallas_call | solution.py:433
  63.7 2.9 %pack.7 = (bf16[2,96,1024]{2,1,0:T(8,128)(2,1)}, bf16[2,96,1024]{2,1,0:T(8,128)(2,1)}, bf16[2,96,1024]{2,1,0:T(8,128)(2,1)}, bf16[2,96,1024]{2,1,0:T(8,128)(2,1)}) custom-call(s32[8]{0:T(128)} %xor_add_fusion.refs_0_, bf16[272,1024]{1,0:T(8,128)(2,1)} %copy-done.6, bf16[2,96,1024]{2,1,0:T(8,128)(2,1)} %get-tuple-element.101.refs_2_), custom_call_target="tpu_custom_call" | custom-call | tf_op jit(solution)/shard_map/pack/pallas_call | solution.py:428
  68.8 3.4 %collective-permute-done.14.refs_2_ = bf16[2,96,1024]{2,1,0:T(8,128)(2,1)S(1)} collective-permute-done((bf16[2,96,1024]{2,1,0:T(8,128)(2,1)}, bf16[2,96,1024]{2,1,0:T(8,128)(2,1)S(1)}, u32[]{:S(2)}, u32[]{:S(2)}) %collective-permute-start.14) | collective-permute-done | bytes 393248 | tf_op jit(solution)/shard_map/ppermute | solution.py:342
  73.8 7.0 %collective-permute-done.17.refs_3_ = bf16[2,96,1024]{2,1,0:T(8,128)(2,1)S(1)} collective-permute-done((bf16[2,96,1024]{2,1,0:T(8,128)(2,1)}, bf16[2,96,1024]{2,1,0:T(8,128)(2,1)S(1)}, u32[]{:S(2)}, u32[]{:S(2)}) %collective-permute-start.17) | collective-permute-done | bytes 393248 | tf_op jit(solution)/shard_map/ppermute | solution.py:342
  83.2 5.9 %collective-permute-done.15.refs_2_ = bf16[2,96,1024]{2,1,0:T(8,128)(2,1)S(1)} collective-permute-done((bf16[2,96,1024]{2,1,0:T(8,128)(2,1)}, bf16[2,96,1024]{2,1,0:T(8,128)(2,1)S(1)}, u32[]{:S(2)}, u32[]{:S(2)}) %collective-permute-start.15) | collective-permute-done | bytes 393248 | tf_op jit(solution)/shard_map/ppermute | solution.py:342
  92.1 8.5 %expert.6 = (bf16[2,96,1024]{2,1,0:T(8,128)(2,1)}, bf16[2,96,1024]{2,1,0:T(8,128)(2,1)}, bf16[2,96,1024]{2,1,0:T(8,128)(2,1)}, bf16[2,96,1024]{2,1,0:T(8,128)(2,...) custom-call(bf16[2,96,1024]{2,1,0:T(8,128)(2,1)} %get-tuple-element., ...), custom_call_target="tpu_custom_call" | custom-call | tf_op jit(solution)/shard_map/expert/pallas_call | solution.py:433
  100.6 8.8 %expert.7 = (bf16[2,96,1024]{2,1,0:T(8,128)(2,1)}, bf16[2,96,1024]{2,1,0:T(8,128)(2,1)}, bf16[2,96,1024]{2,1,0:T(8,128)(2,1)}, bf16[2,96,1024]{2,1,0:T(8,128)(2,...) custom-call(bf16[2,96,1024]{2,1,0:T(8,128)(2,1)} %get-tuple-element., ...), custom_call_target="tpu_custom_call" | custom-call | tf_op jit(solution)/shard_map/expert/pallas_call | solution.py:433
  110.4 3.4 %merge.4.refs_20_ = bf16[272,1024]{1,0:T(8,128)(2,1)} custom-call(s32[8]{0:T(128)} %xor_add_fusion.refs_0_, bf16[272,1024]{1,0:T(8,128)(2,1)} %collective-permute-done.6.refs_1_, bf16[2,96,1024]{2,1,0:T(8,128)(2,1)} %get-tuple-element.101.refs_2_, bf16[2,96,1024]{2,1,0:T(8,128)(2,1)} %copy-done.27, bf16[2,96,1024]{2,1,0:T(8,128)(2,1)} %copy-done.26, ...), custom_call_target="tpu_custom_call" | custom-call | tf_op jit(solution)/shard_map/merge/pallas_call | solution.py:449
  113.8 7.8 %weight.2.refs_6_ = bf16[1536,1024]{1,0:T(8,128)(2,1)} custom-call(bf16[2,192,1024]{2,1,0:T(8,128)(2,1)} %get-tuple-element.140.refs_0_, bf16[2,192,1024]{2,1,0:T(8,128)(2,1)} %get-tuple-element.141.refs_1_, bf16[2,192,512]{2,1,0:T(8,128)(2,1)} %get-tuple-element.142.refs_2_, bf16[2,192,512]{2,1,0:T(8,128)(2,1)} %get-tuple-element.143.refs_3_, ...), custom_call_target="tpu_custom_call" | custom-call | tf_op jit(solution)/shard_map/weight/pallas_call | solution.py:442
  125.2 13.5 %collective-permute-start.30 = (bf16[272,1024]{1,0:T(8,128)(2,1)S(1)}, bf16[272,1024]{1,0:T(8,128)(2,1)S(1)}, u32[]{:S(2)}, u32[]{:S(2)}) collective-permute-start(bf16[272,1024]{1,0:T(8,128)(2,1)S(1)} %copy-done.4), channel_id=1, source_target_pairs={{0,24},{1,25},{2,26},{3,27},{4,28},{5,29},{6,30},{7,31},{8,0},{9,1... | collective-permute-start | bytes 1671176 | tf_op jit(solution)/shard_map/ppermute | solution.py:346
  144.2 3.4 %merge.5.refs_6_ = bf16[272,1024]{1,0:T(8,128)(2,1)} custom-call(s32[8]{0:T(128)} %xor_add_fusion.refs_0_, bf16[272,1024]{1,0:T(8,128)(2,1)} %copy-done.5, bf16[2,96,1024]{2,1,0:T(8,128)(2,1)} %get-tuple-element.115.refs_10_.refs_2_, bf16[2,96,1024]{2,1,0:T(8,128)(2,1)} %copy-done.30, bf16[2,96,1024]{2,1,0:T(8,128)(2,1)} %copy-done.29, ...), custom_call_target="tpu_custom_call" | custom-call | tf_op jit(solution)/shard_map/merge/pallas_call | solution.py:449
  147.6 4.3 %collective-permute-done.28.refs_5_ = bf16[2,96,1024]{2,1,0:T(8,128)(2,1)S(1)} collective-permute-done((bf16[2,96,1024]{2,1,0:T(8,128)(2,1)}, bf16[2,96,1024]{2,1,0:T(8,128)(2,1)S(1)}, u32[]{:S(2)}, u32[]{:S(2)}) %collective-permute-start.28) | collective-permute-done | bytes 393248 | tf_op jit(solution)/shard_map/ppermute | solution.py:342
  154.1 5.3 %collective-permute-done.24.refs_4_ = bf16[2,96,1024]{2,1,0:T(8,128)(2,1)S(1)} collective-permute-done((bf16[2,96,1024]{2,1,0:T(8,128)(2,1)}, bf16[2,96,1024]{2,1,0:T(8,128)(2,1)S(1)}, u32[]{:S(2)}, u32[]{:S(2)}) %collective-permute-start.24) | collective-permute-done | bytes 393248 | tf_op jit(solution)/shard_map/ppermute | solution.py:342
  160.9 3.5 %merge.6.refs_21_ = bf16[272,1024]{1,0:T(8,128)(2,1)} custom-call(s32[8]{0:T(128)} %xor_add_fusion.refs_0_, bf16[272,1024]{1,0:T(8,128)(2,1)} %copy-done.6, bf16[2,96,1024]{2,1,0:T(8,128)(2,1)} %get-tuple-element.139.refs_6_.refs_2_, bf16[2,96,1024]{2,1,0:T(8,128)(2,1)} %copy-done.33, bf16[2,96,1024]{2,1,0:T(8,128)(2,1)} %copy-done.32, ...), custom_call_target="tpu_custom_call" | custom-call | tf_op jit(solution)/shard_map/merge/pallas_call | solution.py:449
  164.4 10.8 %collective-permute-start.32 = (bf16[272,1024]{1,0:T(8,128)(2,1)}, bf16[272,1024]{1,0:T(8,128)(2,1)S(1)}, u32[]{:S(2)}, u32[]{:S(2)}) collective-permute-start(bf16[272,1024]{1,0:T(8,128)(2,1)} %merge.6.refs_21_), channel_id=1, source_target_pairs={{0,8},{1,9},{2,10},{3,11},{4,12},{5,13},{6,14},{7,15},{8,16},{9,17... | collective-permute-start | bytes 1671176 | tf_op jit(solution)/shard_map/ppermute | solution.py:346
  178.9 8.1 %weight.3 = (bf16[1024,512]{1,0:T(8,128)(2,1)}, bf16[1024,512]{1,0:T(8,128)(2,1)}, bf16[512,1024]{1,0:T(8,128)(2,1)}) custom-call(bf16[2,192,1024]{2,1,0:T(8,128)(2,1)} %get-tuple-element.140.refs_0_, bf16[2,192,1024]{2,1,0:T(8,128)(2,1)} %get-tuple-element.141.refs_1_, bf16[2,192,512]{2,1,0:T(8,128)(2,1)} %get-tuple-element.142.refs_2_, ...), custom_call_target="tpu_custom_call" | custom-call | tf_op jit(solution)/shard_map/weight/pallas_call | solution.py:446
  188.0 6.6 %collective-permute-done.25.refs_4_ = bf16[2,96,1024]{2,1,0:T(8,128)(2,1)S(1)} collective-permute-done((bf16[2,96,1024]{2,1,0:T(8,128)(2,1)S(1)}, bf16[2,96,1024]{2,1,0:T(8,128)(2,1)S(1)}, u32[]{:S(2)}, u32[]{:S(2)}) %collective-permute-start.25) | collective-permute-done | bytes 393248 | tf_op jit(solution)/shard_map/ppermute | solution.py:342
  195.7 3.8 %merge.7 = (bf16[128,1024]{1,0:T(8,128)(2,1)}, bf16[128,1024]{1,0:T(8,128)(2,1)}, f32[8,128]{1,0:T(8,128)}) custom-call(s32[8]{0:T(128)} %xor_add_fusion.refs_0_, bf16[272,1024]{1,0:T(8,128)(2,1)} %join.1.refs_1_.refs_2_, bf16[2,96,1024]{2,1,0:T(8,128)(2,1)} %get-tuple-element.92.refs_2_, bf16[2,96,1024]{2,1,0:T(8,128)(2,1)} %copy-done.25, ...), custom_call_target="tpu_custom_call" | custom-call | tf_op jit(solution)/shard_map/merge/pallas_call | solution.py:449
  (143 shorter events, 55.5 us)
Async XLA Ops:
  5.0 18.6 %collective-permute-start.6 = (bf16[272,1024]{1,0:T(8,128)(2,1)}, bf16[272,1024]{1,0:T(8,128)(2,1)}, u32[]{:S(2)}, u32[]{:S(2)}) collective-permute-start(bf16[272,1024]{1,0:T(8,128)(2,1)} %join.1.refs_1_.refs_2_), channel_id=1, source_target_pairs={{0,8},{1,9},{2,10},{3,11},{4,12},{5,13},{6,14},{7,15},{8,16},{9,17... | collective-permute-start | bytes 1671176 | tf_op jit(solution)/shard_map/ppermute | solution.py:346
  13.9 19.0 %collective-permute-start.4 = (bf16[2,96,1024]{2,1,0:T(8,128)(2,1)}, bf16[2,96,1024]{2,1,0:T(8,128)(2,1)S(1)}, u32[]{:S(2)}, u32[]{:S(2)}) collective-permute-start(bf16[2,96,1024]{2,1,0:T(8,128)(2,1)} %get-tuple-element.89), channel_id=1, source_target_pairs={{0,4},{1,5},{2,6},{3,7},{4,0},{5,1},{6,2},{7,3},{8,12},{9,13},{10,... | collective-permute-start | bytes 1179656 | tf_op jit(solution)/shard_map/ppermute | solution.py:342
  14.4 20.0 %collective-permute-start.3 = (bf16[2,96,1024]{2,1,0:T(8,128)(2,1)}, bf16[2,96,1024]{2,1,0:T(8,128)(2,1)S(1)}, u32[]{:S(2)}, u32[]{:S(2)}) collective-permute-start(bf16[2,96,1024]{2,1,0:T(8,128)(2,1)} %get-tuple-element.88), channel_id=1, source_target_pairs={{0,2},{1,3},{2,0},{3,1},{4,6},{5,7},{6,4},{7,5},{8,10},{9,11},{10,... | collective-permute-start | bytes 1179656 | tf_op jit(solution)/shard_map/ppermute | solution.py:342
  14.9 32.1 %collective-permute-start.11 = (bf16[272,1024]{1,0:T(8,128)(2,1)}, bf16[272,1024]{1,0:T(8,128)(2,1)S(1)}, u32[]{:S(2)}, u32[]{:S(2)}) collective-permute-start(bf16[272,1024]{1,0:T(8,128)(2,1)} %join.1.refs_1_.refs_2_), channel_id=1, source_target_pairs={{0,16},{1,17},{2,18},{3,19},{4,20},{5,21},{6,22},{7,23},{8,24},{9,... | collective-permute-start | bytes 1671176 | tf_op jit(solution)/shard_map/ppermute | solution.py:346
  26.4 24.3 %collective-permute-start.10 = (bf16[2,96,1024]{2,1,0:T(8,128)(2,1)}, bf16[2,96,1024]{2,1,0:T(8,128)(2,1)S(1)}, u32[]{:S(2)}, u32[]{:S(2)}) collective-permute-start(bf16[2,96,1024]{2,1,0:T(8,128)(2,1)} %get-tuple-element.99), channel_id=1, source_target_pairs={{0,6},{1,7},{2,4},{3,5},{4,2},{5,3},{6,0},{7,1},{8,14},{9,15},{10,... | collective-permute-start | bytes 1179656 | tf_op jit(solution)/shard_map/ppermute | solution.py:342
  32.9 20.3 %collective-permute-start.9 = (bf16[2,96,1024]{2,1,0:T(8,128)(2,1)}, bf16[2,96,1024]{2,1,0:T(8,128)(2,1)S(1)}, u32[]{:S(2)}, u32[]{:S(2)}) collective-permute-start(bf16[2,96,1024]{2,1,0:T(8,128)(2,1)} %get-tuple-element.97), channel_id=1, source_target_pairs={{0,4},{1,5},{2,6},{3,7},{4,0},{5,1},{6,2},{7,3},{8,12},{9,13},{10,... | collective-permute-start | bytes 1179656 | tf_op jit(solution)/shard_map/ppermute | solution.py:342
  34.4 19.3 %collective-permute-start.8 = (bf16[2,96,1024]{2,1,0:T(8,128)(2,1)}, bf16[2,96,1024]{2,1,0:T(8,128)(2,1)S(1)}, u32[]{:S(2)}, u32[]{:S(2)}) collective-permute-start(bf16[2,96,1024]{2,1,0:T(8,128)(2,1)} %get-tuple-element.95), channel_id=1, source_target_pairs={{0,2},{1,3},{2,0},{3,1},{4,6},{5,7},{6,4},{7,5},{8,10},{9,11},{10,... | collective-permute-start | bytes 1179656 | tf_op jit(solution)/shard_map/ppermute | solution.py:342
  34.5 28.4 %collective-permute-start.7 = (bf16[272,1024]{1,0:T(8,128)(2,1)}, bf16[272,1024]{1,0:T(8,128)(2,1)S(1)}, u32[]{:S(2)}, u32[]{:S(2)}) collective-permute-start(bf16[272,1024]{1,0:T(8,128)(2,1)} %join.1.refs_1_.refs_2_), channel_id=1, source_target_pairs={{0,24},{1,25},{2,26},{3,27},{4,28},{5,29},{6,30},{7,31},{8,0},{9,1... | collective-permute-start | bytes 1671176 | tf_op jit(solution)/shard_map/ppermute | solution.py:346
  53.2 19.0 %collective-permute-start.14 = (bf16[2,96,1024]{2,1,0:T(8,128)(2,1)}, bf16[2,96,1024]{2,1,0:T(8,128)(2,1)S(1)}, u32[]{:S(2)}, u32[]{:S(2)}) collective-permute-start(bf16[2,96,1024]{2,1,0:T(8,128)(2,1)} %get-tuple-element.109), channel_id=1, source_target_pairs={{0,4},{1,5},{2,6},{3,7},{4,0},{5,1},{6,2},{7,3},{8,12},{9,13},{10,... | collective-permute-start | bytes 1179656 | tf_op jit(solution)/shard_map/ppermute | solution.py:342
  53.7 20.0 %collective-permute-start.12 = (bf16[2,96,1024]{2,1,0:T(8,128)(2,1)}, bf16[2,96,1024]{2,1,0:T(8,128)(2,1)S(1)}, u32[]{:S(2)}, u32[]{:S(2)}) collective-permute-start(bf16[2,96,1024]{2,1,0:T(8,128)(2,1)} %get-tuple-element.105), channel_id=1, source_target_pairs={{0,2},{1,3},{2,0},{3,1},{4,6},{5,7},{6,4},{7,5},{8,10},{9,11},{10,... | collective-permute-start | bytes 1179656 | tf_op jit(solution)/shard_map/ppermute | solution.py:342
  72.2 16.9 %collective-permute-start.15 = (bf16[2,96,1024]{2,1,0:T(8,128)(2,1)}, bf16[2,96,1024]{2,1,0:T(8,128)(2,1)S(1)}, u32[]{:S(2)}, u32[]{:S(2)}) collective-permute-start(bf16[2,96,1024]{2,1,0:T(8,128)(2,1)} %get-tuple-element.110), channel_id=1, source_target_pairs={{0,4},{1,5},{2,6},{3,7},{4,0},{5,1},{6,2},{7,3},{8,12},{9,13},{10,... | collective-permute-start | bytes 1179656 | tf_op jit(solution)/shard_map/ppermute | solution.py:342
  80.8 28.6 %collective-permute-start.26 = (bf16[2,96,1024]{2,1,0:T(8,128)(2,1)}, bf16[2,96,1024]{2,1,0:T(8,128)(2,1)S(1)}, u32[]{:S(2)}, u32[]{:S(2)}) collective-permute-start(bf16[2,96,1024]{2,1,0:T(8,128)(2,1)} %get-tuple-element.135), channel_id=1, source_target_pairs={{0,6},{1,7},{2,4},{3,5},{4,2},{5,3},{6,0},{7,1},{8,14},{9,15},{10,... | collective-permute-start | bytes 1179656 | tf_op jit(solution)/shard_map/ppermute | solution.py:342
  89.1 20.3 %collective-permute-start.22 = (bf16[2,96,1024]{2,1,0:T(8,128)(2,1)}, bf16[2,96,1024]{2,1,0:T(8,128)(2,1)S(1)}, u32[]{:S(2)}, u32[]{:S(2)}) collective-permute-start(bf16[2,96,1024]{2,1,0:T(8,128)(2,1)} %get-tuple-element.127), channel_id=1, source_target_pairs={{0,4},{1,5},{2,6},{3,7},{4,0},{5,1},{6,2},{7,3},{8,12},{9,13},{10,... | collective-permute-start | bytes 1179656 | tf_op jit(solution)/shard_map/ppermute | solution.py:342
  90.7 18.8 %collective-permute-start.18 = (bf16[2,96,1024]{2,1,0:T(8,128)(2,1)}, bf16[2,96,1024]{2,1,0:T(8,128)(2,1)S(1)}, u32[]{:S(2)}, u32[]{:S(2)}) collective-permute-start(bf16[2,96,1024]{2,1,0:T(8,128)(2,1)} %get-tuple-element.119), channel_id=1, source_target_pairs={{0,2},{1,3},{2,0},{3,1},{4,6},{5,7},{6,4},{7,5},{8,10},{9,11},{10,... | collective-permute-start | bytes 1179656 | tf_op jit(solution)/shard_map/ppermute | solution.py:342
  121.6 55.6 %collective-permute-start.33 = (bf16[1536,1024]{1,0:T(8,128)(2,1)}, bf16[1536,1024]{1,0:T(8,128)(2,1)S(1)}, u32[]{:S(2)}, u32[]{:S(2)}) collective-permute-start(bf16[1536,1024]{1,0:T(8,128)(2,1)} %weight.2.refs_6_), channel_id=1, source_target_pairs={{0,1},{1,0},{2,3},{3,2},{4,5},{5,4},{6,7},{7,6},{8,9},{9,8},{10,11... | collective-permute-start | bytes 9437192 | tf_op jit(solution)/shard_map/ppermute | solution.py:342
  121.7 17.0 %collective-permute-start.27 = (bf16[2,96,1024]{2,1,0:T(8,128)(2,1)S(1)}, bf16[2,96,1024]{2,1,0:T(8,128)(2,1)S(1)}, u32[]{:S(2)}, u32[]{:S(2)}) collective-permute-start(bf16[2,96,1024]{2,1,0:T(8,128)(2,1)S(1)} %copy-done.40), channel_id=1, source_target_pairs={{0,6},{1,7},{2,4},{3,5},{4,2},{5,3},{6,0},{7,1},{8,14},{9,15},{10,... | collective-permute-start | bytes 1179656 | tf_op jit(solution)/shard_map/ppermute | solution.py:342
  122.2 19.6 %collective-permute-start.23 = (bf16[2,96,1024]{2,1,0:T(8,128)(2,1)S(1)}, bf16[2,96,1024]{2,1,0:T(8,128)(2,1)S(1)}, u32[]{:S(2)}, u32[]{:S(2)}) collective-permute-start(bf16[2,96,1024]{2,1,0:T(8,128)(2,1)S(1)} %copy-done.39), channel_id=1, source_target_pairs={{0,4},{1,5},{2,6},{3,7},{4,0},{5,1},{6,2},{7,3},{8,12},{9,13},{10,... | collective-permute-start | bytes 1179656 | tf_op jit(solution)/shard_map/ppermute | solution.py:342
  123.8 19.7 %collective-permute-start.19 = (bf16[2,96,1024]{2,1,0:T(8,128)(2,1)S(1)}, bf16[2,96,1024]{2,1,0:T(8,128)(2,1)S(1)}, u32[]{:S(2)}, u32[]{:S(2)}) collective-permute-start(bf16[2,96,1024]{2,1,0:T(8,128)(2,1)S(1)} %copy-done.38), channel_id=1, source_target_pairs={{0,2},{1,3},{2,0},{3,1},{4,6},{5,7},{6,4},{7,5},{8,10},{9,11},{10,... | collective-permute-start | bytes 1179656 | tf_op jit(solution)/shard_map/ppermute | solution.py:342
  125.2 50.4 %collective-permute-start.30 = (bf16[272,1024]{1,0:T(8,128)(2,1)S(1)}, bf16[272,1024]{1,0:T(8,128)(2,1)S(1)}, u32[]{:S(2)}, u32[]{:S(2)}) collective-permute-start(bf16[272,1024]{1,0:T(8,128)(2,1)S(1)} %copy-done.4), channel_id=1, source_target_pairs={{0,24},{1,25},{2,26},{3,27},{4,28},{5,29},{6,30},{7,31},{8,0},{9,1... | collective-permute-start | bytes 1671176 | tf_op jit(solution)/shard_map/ppermute | solution.py:346
  141.8 17.6 %collective-permute-start.24 = (bf16[2,96,1024]{2,1,0:T(8,128)(2,1)}, bf16[2,96,1024]{2,1,0:T(8,128)(2,1)S(1)}, u32[]{:S(2)}, u32[]{:S(2)}) collective-permute-start(bf16[2,96,1024]{2,1,0:T(8,128)(2,1)} %get-tuple-element.129), channel_id=1, source_target_pairs={{0,4},{1,5},{2,6},{3,7},{4,0},{5,1},{6,2},{7,3},{8,12},{9,13},{10,... | collective-permute-start | bytes 1179656 | tf_op jit(solution)/shard_map/ppermute | solution.py:342
  151.9 35.1 %collective-permute-start.31 = (bf16[272,1024]{1,0:T(8,128)(2,1)}, bf16[272,1024]{1,0:T(8,128)(2,1)S(1)}, u32[]{:S(2)}, u32[]{:S(2)}) collective-permute-start(bf16[272,1024]{1,0:T(8,128)(2,1)} %merge.5.refs_6_), channel_id=1, source_target_pairs={{0,16},{1,17},{2,18},{3,19},{4,20},{5,21},{6,22},{7,23},{8,24},{9,... | collective-permute-start | bytes 1671176 | tf_op jit(solution)/shard_map/ppermute | solution.py:346
  164.4 30.3 %collective-permute-start.32 = (bf16[272,1024]{1,0:T(8,128)(2,1)}, bf16[272,1024]{1,0:T(8,128)(2,1)S(1)}, u32[]{:S(2)}, u32[]{:S(2)}) collective-permute-start(bf16[272,1024]{1,0:T(8,128)(2,1)} %merge.6.refs_21_), channel_id=1, source_target_pairs={{0,8},{1,9},{2,10},{3,11},{4,12},{5,13},{6,14},{7,15},{8,16},{9,17... | collective-permute-start | bytes 1671176 | tf_op jit(solution)/shard_map/ppermute | solution.py:346
  175.7 19.0 %collective-permute-start.25 = (bf16[2,96,1024]{2,1,0:T(8,128)(2,1)S(1)}, bf16[2,96,1024]{2,1,0:T(8,128)(2,1)S(1)}, u32[]{:S(2)}, u32[]{:S(2)}) collective-permute-start(bf16[2,96,1024]{2,1,0:T(8,128)(2,1)S(1)} %copy-done.35), channel_id=1, source_target_pairs={{0,4},{1,5},{2,6},{3,7},{4,0},{5,1},{6,2},{7,3},{8,12},{9,13},{10,... | collective-permute-start | bytes 1179656 | tf_op jit(solution)/shard_map/ppermute | solution.py:342
  177.2 17.4 %collective-permute-start.21 = (bf16[2,96,1024]{2,1,0:T(8,128)(2,1)S(1)}, bf16[2,96,1024]{2,1,0:T(8,128)(2,1)S(1)}, u32[]{:S(2)}, u32[]{:S(2)}) collective-permute-start(bf16[2,96,1024]{2,1,0:T(8,128)(2,1)S(1)} %copy-done.34), channel_id=1, source_target_pairs={{0,2},{1,3},{2,0},{3,1},{4,6},{5,7},{6,4},{7,5},{8,10},{9,11},{10,... | collective-permute-start | bytes 1179656 | tf_op jit(solution)/shard_map/ppermute | solution.py:342
  (51 other events, 570.1 us)

commit v3 on v2

--- a/solution.py
+++ b/solution.py
@@ -138,10 +138,11 @@
 LEADING = (((0,), (0,)), ((), ()))
 TRAILING = (((1,), (1,)), ((), ()))
 CHIPS = 4
-COST = {'join': 1.0, 'pack': 0, 'expert': 0, 'merge': 0, 'weight': 0}
+COST = {'join': 1.0, 'pack': 0, 'expert': 0, 'merge': 150, 'weight': 0}
 WHEN = 0
+CHAINZ = 0
 FAR = 0
-WPOS = 1
+WPOS = 2
 BEHIND = 1
 STRICT = 0
 AHEAD = 1
@@ -352,7 +353,7 @@
     (block,) = call(join_kernel, "join", [bf16((block_rows, width))], [VMEM] * 4, 0, 4 * block_rows * width)(
         tokens, grad_out, expert_ids.T, gates.T, gates
     )
-    order = list(range(levels))
+    order = sorted(range(levels), key=lambda step: min(step, levels - step))
     pack = call(
         functools.partial(pack_kernel, token_count, capacity, top_count),
         "pack",
@@ -416,7 +417,7 @@
     mats = [w_gate[0], w_up[0], w_down[0]]
     blocks = {0: block}
     for step in order[1:]:
-        blocks[step] = climb(block, step)
+        blocks[step] = climb(after(block, blocks[order[1]]) if CHAINZ and step == order[-2] else block, step)
     arrived, results, kept = {}, {}, {}
     last = block
     for turn in range(levels + AHEAD):

time: 200 us -> 181 us (0.905)
  starting transfers between devices: 66.6 us -> 47.6 us
    ppermute x6, starting transfers between devices: 35.2 us -> 15.8 us  [climb(): return lax.ppermute(value, axes, pairs)]
    ppermute x6, waiting for transfers between devices: 6.54 us -> 11.1 us  [climb(): return lax.ppermute(value, axes, pairs)]
    ppermute x28, waiting for transfers between devices: 40 us -> 36.4 us  [flip(): return lax.ppermute(value, axes, pairs)]
    unnamed x83 -> x85, local copies, waits for them, and re-layouts: 7.07 us -> 5.92 us
  transfers between devices with their start and end apart: 34 -> 34, of which waited for: 11 -> 9; matrix products, arithmetic and copies ran while one was open for 1% -> 1% of each run, Pallas kernels for 31% -> 41%
where the time goes in v3:
time: 181 us; the launch traced here: 180 us
  Pallas kernels  77.8 us (43%)
  starting transfers between devices  47.6 us (26%)
  waiting for transfers between devices  47.4 us (26%)
  local copies, waits for them, and re-layouts  5.92 us (3%)
    ppermute x28, waiting for transfers between devices, flip(): return lax.ppermute(value, axes, pairs)  36.4 us
    pallas_call x4, Pallas kernels, local_plane(): outs = expert(*arrived[step], *mats, last)  34.2 us
    ppermute x28, starting transfers between devices, flip(): return lax.ppermute(value, axes, pairs)  31.8 us
    ppermute x6, starting transfers between devices, climb(): return lax.ppermute(value, axes, pairs)  15.8 us
    pallas_call x4, Pallas kernels, local_plane(): merge(len(earlier), final)  14.1 us
    pallas_call x4, Pallas kernels, local_plane(): packed = pack(table, blocks[order[turn]], last)  11.8 us
    ppermute x6, waiting for transfers between devices, climb(): return lax.ppermute(value, axes, pairs)  11.1 us
    pallas_call x1, Pallas kernels, local_plane(): grad_mats = weight(0, 1)(*saved, partial, last)  8.08 us
  transfers between devices with their start and end apart: 34, of which 9 were waited for; matrix products, arithmetic and copies ran while one was open for 1% of the time, Pallas kernels for 41%

profile of v3, /device:TPU:0, one launch (start us, length us, event | category | flops | bytes accessed | tf_op | source)
XLA Modules:
  0.0 180.2 jit_solution(17153652633999009370)
XLA Ops:
  5.0 2.7 %collective-permute-start.6 = (bf16[272,1024]{1,0:T(8,128)(2,1)}, bf16[272,1024]{1,0:T(8,128)(2,1)}, u32[]{:S(2)}, u32[]{:S(2)}) collective-permute-start(bf16[272,1024]{1,0:T(8,128)(2,1)} %join.1.refs_1_.refs_2_), channel_id=1, source_target_pairs={{0,8},{1,9},{2,10},{3,11},{4,12},{5,13},{6,14},{7,15},{8,16},{9,17... | collective-permute-start | bytes 1671176 | tf_op jit(solution)/shard_map/ppermute | solution.py:347
  8.2 3.3 %pack.4 = (bf16[2,96,1024]{2,1,0:T(8,128)(2,1)}, bf16[2,96,1024]{2,1,0:T(8,128)(2,1)}, bf16[2,96,1024]{2,1,0:T(8,128)(2,1)}, bf16[2,96,1024]{2,1,0:T(8,128)(2,1)}) custom-call(s32[8]{0:T(128)} %xor_add_fusion.refs_0_, bf16[272,1024]{1,0:T(8,128)(2,1)} %join.1.refs_1_.refs_2_, bf16[272,1024]{1,0:T(8,128)(2,1)} %join.1.refs_1_.refs_2_), custom_call_target="tpu_custom_call" | custom-call | tf_op jit(solution)/shard_map/pack/pallas_call | solution.py:429
  15.0 3.4 %collective-permute-start.11 = (bf16[272,1024]{1,0:T(8,128)(2,1)}, bf16[272,1024]{1,0:T(8,128)(2,1)S(1)}, u32[]{:S(2)}, u32[]{:S(2)}) collective-permute-start(bf16[272,1024]{1,0:T(8,128)(2,1)} %join.1.refs_1_.refs_2_), channel_id=1, source_target_pairs={{0,24},{1,25},{2,26},{3,27},{4,28},{5,29},{6,30},{7,31},{8,0},{9,1... | collective-permute-start | bytes 1671176 | tf_op jit(solution)/shard_map/ppermute | solution.py:347
  18.4 5.1 %collective-permute-done.6.refs_1_ = bf16[272,1024]{1,0:T(8,128)(2,1)} collective-permute-done((bf16[272,1024]{1,0:T(8,128)(2,1)}, bf16[272,1024]{1,0:T(8,128)(2,1)}, u32[]{:S(2)}, u32[]{:S(2)}) %collective-permute-start.6) | collective-permute-done | bytes 557088 | tf_op jit(solution)/shard_map/ppermute | solution.py:347
  23.5 2.8 %pack.5 = (bf16[2,96,1024]{2,1,0:T(8,128)(2,1)}, bf16[2,96,1024]{2,1,0:T(8,128)(2,1)}, bf16[2,96,1024]{2,1,0:T(8,128)(2,1)}, bf16[2,96,1024]{2,1,0:T(8,128)(2,1)}) custom-call(s32[8]{0:T(128)} %xor_add_fusion.refs_0_, bf16[272,1024]{1,0:T(8,128)(2,1)} %collective-permute-done.6.refs_1_, bf16[2,96,1024]{2,1,0:T(8,128)(2,1)} %get-tuple-element.87.refs_2_.refs_0_), custom_call_target="tpu_custom_call" | custom-call | tf_op jit(solution)/shard_map/pack/pallas_call | solution.py:429
  29.5 4.2 %collective-permute-done.5.refs_3_ = bf16[2,96,1024]{2,1,0:T(8,128)(2,1)S(1)} collective-permute-done((bf16[2,96,1024]{2,1,0:T(8,128)(2,1)}, bf16[2,96,1024]{2,1,0:T(8,128)(2,1)S(1)}, u32[]{:S(2)}, u32[]{:S(2)}) %collective-permute-start.5) | collective-permute-done | bytes 393248 | tf_op jit(solution)/shard_map/ppermute | solution.py:343
  36.1 6.1 %collective-permute-start.7 = (bf16[272,1024]{1,0:T(8,128)(2,1)}, bf16[272,1024]{1,0:T(8,128)(2,1)S(1)}, u32[]{:S(2)}, u32[]{:S(2)}) collective-permute-start(bf16[272,1024]{1,0:T(8,128)(2,1)} %join.1.refs_1_.refs_2_), channel_id=1, source_target_pairs={{0,16},{1,17},{2,18},{3,19},{4,20},{5,21},{6,22},{7,23},{8,24},{9,... | collective-permute-start | bytes 1671176 | tf_op jit(solution)/shard_map/ppermute | solution.py:347
  42.2 8.5 %expert.4 = (bf16[2,96,1024]{2,1,0:T(8,128)(2,1)}, bf16[2,96,1024]{2,1,0:T(8,128)(2,1)}, bf16[2,96,1024]{2,1,0:T(8,128)(2,1)}, bf16[2,96,1024]{2,1,0:T(8,128)(2,...) custom-call(bf16[2,96,1024]{2,1,0:T(8,128)(2,1)} %get-tuple-element., ...), custom_call_target="tpu_custom_call" | custom-call | tf_op jit(solution)/shard_map/expert/pallas_call | solution.py:434
  51.6 2.8 %pack.6 = (bf16[2,96,1024]{2,1,0:T(8,128)(2,1)}, bf16[2,96,1024]{2,1,0:T(8,128)(2,1)}, bf16[2,96,1024]{2,1,0:T(8,128)(2,1)}, bf16[2,96,1024]{2,1,0:T(8,128)(2,1)}) custom-call(s32[8]{0:T(128)} %xor_add_fusion.refs_0_, bf16[272,1024]{1,0:T(8,128)(2,1)} %copy-done.4, bf16[2,96,1024]{2,1,0:T(8,128)(2,1)} %get-tuple-element.92.refs_2_), custom_call_target="tpu_custom_call" | custom-call | tf_op jit(solution)/shard_map/pack/pallas_call | solution.py:429
  58.2 8.5 %expert.5 = (bf16[2,96,1024]{2,1,0:T(8,128)(2,1)}, bf16[2,96,1024]{2,1,0:T(8,128)(2,1)}, bf16[2,96,1024]{2,1,0:T(8,128)(2,1)}, bf16[2,96,1024]{2,1,0:T(8,128)(2,...) custom-call(bf16[2,96,1024]{2,1,0:T(8,128)(2,1)} %get-tuple-element., ...), custom_call_target="tpu_custom_call" | custom-call | tf_op jit(solution)/shard_map/expert/pallas_call | solution.py:434
  67.5 2.8 %pack.7 = (bf16[2,96,1024]{2,1,0:T(8,128)(2,1)}, bf16[2,96,1024]{2,1,0:T(8,128)(2,1)}, bf16[2,96,1024]{2,1,0:T(8,128)(2,1)}, bf16[2,96,1024]{2,1,0:T(8,128)(2,1)}) custom-call(s32[8]{0:T(128)} %xor_add_fusion.refs_0_, bf16[272,1024]{1,0:T(8,128)(2,1)} %copy-done.5, bf16[2,96,1024]{2,1,0:T(8,128)(2,1)} %get-tuple-element.101.refs_2_), custom_call_target="tpu_custom_call" | custom-call | tf_op jit(solution)/shard_map/pack/pallas_call | solution.py:429
  73.9 13.4 %collective-permute-done.15.refs_2_ = bf16[2,96,1024]{2,1,0:T(8,128)(2,1)S(1)} collective-permute-done((bf16[2,96,1024]{2,1,0:T(8,128)(2,1)}, bf16[2,96,1024]{2,1,0:T(8,128)(2,1)S(1)}, u32[]{:S(2)}, u32[]{:S(2)}) %collective-permute-start.15) | collective-permute-done | bytes 393248 | tf_op jit(solution)/shard_map/ppermute | solution.py:343
  88.9 3.7 %collective-permute-done.17.refs_3_ = bf16[2,96,1024]{2,1,0:T(8,128)(2,1)S(1)} collective-permute-done((bf16[2,96,1024]{2,1,0:T(8,128)(2,1)}, bf16[2,96,1024]{2,1,0:T(8,128)(2,1)S(1)}, u32[]{:S(2)}, u32[]{:S(2)}) %collective-permute-start.17) | collective-permute-done | bytes 393248 | tf_op jit(solution)/shard_map/ppermute | solution.py:343
  94.8 8.5 %expert.6 = (bf16[2,96,1024]{2,1,0:T(8,128)(2,1)}, bf16[2,96,1024]{2,1,0:T(8,128)(2,1)}, bf16[2,96,1024]{2,1,0:T(8,128)(2,1)}, bf16[2,96,1024]{2,1,0:T(8,128)(2,...) custom-call(bf16[2,96,1024]{2,1,0:T(8,128)(2,1)} %get-tuple-element., ...), custom_call_target="tpu_custom_call" | custom-call | tf_op jit(solution)/shard_map/expert/pallas_call | solution.py:434
  103.3 8.8 %expert.7 = (bf16[2,96,1024]{2,1,0:T(8,128)(2,1)}, bf16[2,96,1024]{2,1,0:T(8,128)(2,1)}, bf16[2,96,1024]{2,1,0:T(8,128)(2,1)}, bf16[2,96,1024]{2,1,0:T(8,128)(2,...) custom-call(bf16[2,96,1024]{2,1,0:T(8,128)(2,1)} %get-tuple-element., ...), custom_call_target="tpu_custom_call" | custom-call | tf_op jit(solution)/shard_map/expert/pallas_call | solution.py:434
  115.8 3.5 %merge.4.refs_6_ = bf16[272,1024]{1,0:T(8,128)(2,1)} custom-call(s32[8]{0:T(128)} %xor_add_fusion.refs_0_, bf16[272,1024]{1,0:T(8,128)(2,1)} %collective-permute-done.6.refs_1_, bf16[2,96,1024]{2,1,0:T(8,128)(2,1)} %get-tuple-element.101.refs_2_, bf16[2,96,1024]{2,1,0:T(8,128)(2,1)} %copy-done.29, bf16[2,96,1024]{2,1,0:T(8,128)(2,1)} %copy-done.31, ...), custom_call_target="tpu_custom_call" | custom-call | flops 60397977600 | bytes 2686976 | tf_op jit(solution)/shard_map/merge/pallas_call | solution.py:450
  120.3 3.8 %collective-permute-done.27.refs_5_ = bf16[2,96,1024]{2,1,0:T(8,128)(2,1)S(1)} collective-permute-done((bf16[2,96,1024]{2,1,0:T(8,128)(2,1)S(1)}, bf16[2,96,1024]{2,1,0:T(8,128)(2,1)S(1)}, u32[]{:S(2)}, u32[]{:S(2)}) %collective-permute-start.27) | collective-permute-done | bytes 393248 | tf_op jit(solution)/shard_map/ppermute | solution.py:343
  130.3 3.4 %merge.5.refs_20_ = bf16[272,1024]{1,0:T(8,128)(2,1)} custom-call(s32[8]{0:T(128)} %xor_add_fusion.refs_0_, bf16[272,1024]{1,0:T(8,128)(2,1)} %copy-done.4, bf16[2,96,1024]{2,1,0:T(8,128)(2,1)} %get-tuple-element.115.refs_10_.refs_2_, bf16[2,96,1024]{2,1,0:T(8,128)(2,1)} %copy-done.40, bf16[2,96,1024]{2,1,0:T(8,128)(2,1)} %copy-done.38, ...), custom_call_target="tpu_custom_call" | custom-call | flops 60397977600 | bytes 2686976 | tf_op jit(solution)/shard_map/merge/pallas_call | solution.py:450
  135.2 7.7 %weight.2.refs_6_ = bf16[1536,1024]{1,0:T(8,128)(2,1)} custom-call(bf16[2,192,1024]{2,1,0:T(8,128)(2,1)} %get-tuple-element.140.refs_0_, bf16[2,192,1024]{2,1,0:T(8,128)(2,1)} %get-tuple-element.141.refs_1_, bf16[2,192,512]{2,1,0:T(8,128)(2,1)} %get-tuple-element.142.refs_2_, bf16[2,192,512]{2,1,0:T(8,128)(2,1)} %get-tuple-element.143.refs_3_, ...), custom_call_target="tpu_custom_call" | custom-call | tf_op jit(solution)/shard_map/weight/pallas_call | solution.py:443
  144.6 3.4 %merge.6.refs_21_ = bf16[272,1024]{1,0:T(8,128)(2,1)} custom-call(s32[8]{0:T(128)} %xor_add_fusion.refs_0_, bf16[272,1024]{1,0:T(8,128)(2,1)} %copy-done.5, bf16[2,96,1024]{2,1,0:T(8,128)(2,1)} %get-tuple-element.139.refs_6_.refs_2_, bf16[2,96,1024]{2,1,0:T(8,128)(2,1)} %copy-done.41, bf16[2,96,1024]{2,1,0:T(8,128)(2,1)} %copy-done.39, ...), custom_call_target="tpu_custom_call" | custom-call | flops 60397977600 | bytes 2686976 | tf_op jit(solution)/shard_map/merge/pallas_call | solution.py:450
  153.0 8.1 %weight.3 = (bf16[1024,512]{1,0:T(8,128)(2,1)}, bf16[1024,512]{1,0:T(8,128)(2,1)}, bf16[512,1024]{1,0:T(8,128)(2,1)}) custom-call(bf16[2,192,1024]{2,1,0:T(8,128)(2,1)} %get-tuple-element.140.refs_0_, bf16[2,192,1024]{2,1,0:T(8,128)(2,1)} %get-tuple-element.141.refs_1_, bf16[2,192,512]{2,1,0:T(8,128)(2,1)} %get-tuple-element.142.refs_2_, ...), custom_call_target="tpu_custom_call" | custom-call | tf_op jit(solution)/shard_map/weight/pallas_call | solution.py:447
  162.0 7.6 %collective-permute-done.25.refs_4_ = bf16[2,96,1024]{2,1,0:T(8,128)(2,1)S(1)} collective-permute-done((bf16[2,96,1024]{2,1,0:T(8,128)(2,1)S(1)}, bf16[2,96,1024]{2,1,0:T(8,128)(2,1)S(1)}, u32[]{:S(2)}, u32[]{:S(2)}) %collective-permute-start.25) | collective-permute-done | bytes 393248 | tf_op jit(solution)/shard_map/ppermute | solution.py:343
  169.7 6.0 %collective-permute-done.32.refs_8_ = bf16[272,1024]{1,0:T(8,128)(2,1)S(1)} collective-permute-done((bf16[272,1024]{1,0:T(8,128)(2,1)}, bf16[272,1024]{1,0:T(8,128)(2,1)S(1)}, u32[]{:S(2)}, u32[]{:S(2)}) %collective-permute-start.32) | collective-permute-done | bytes 557088 | tf_op jit(solution)/shard_map/ppermute | solution.py:347
  176.4 3.8 %merge.7 = (bf16[128,1024]{1,0:T(8,128)(2,1)}, bf16[128,1024]{1,0:T(8,128)(2,1)}, f32[8,128]{1,0:T(8,128)}) custom-call(s32[8]{0:T(128)} %xor_add_fusion.refs_0_, bf16[272,1024]{1,0:T(8,128)(2,1)} %join.1.refs_1_.refs_2_, bf16[2,96,1024]{2,1,0:T(8,128)(2,1)} %get-tuple-element.92.refs_2_, bf16[2,96,1024]{2,1,0:T(8,128)(2,1)} %copy-done.35, ...), custom_call_target="tpu_custom_call" | custom-call | flops 60397977600 | bytes 2686976 | tf_op jit(solution)/shard_map/merge/pallas_call | solution.py:450
  (145 shorter events, 47.5 us)
Async XLA Ops:
  5.0 18.5 %collective-permute-start.6 = (bf16[272,1024]{1,0:T(8,128)(2,1)}, bf16[272,1024]{1,0:T(8,128)(2,1)}, u32[]{:S(2)}, u32[]{:S(2)}) collective-permute-start(bf16[272,1024]{1,0:T(8,128)(2,1)} %join.1.refs_1_.refs_2_), channel_id=1, source_target_pairs={{0,8},{1,9},{2,10},{3,11},{4,12},{5,13},{6,14},{7,15},{8,16},{9,17... | collective-permute-start | bytes 1671176 | tf_op jit(solution)/shard_map/ppermute | solution.py:347
  13.1 14.9 %collective-permute-start.3 = (bf16[2,96,1024]{2,1,0:T(8,128)(2,1)}, bf16[2,96,1024]{2,1,0:T(8,128)(2,1)S(1)}, u32[]{:S(2)}, u32[]{:S(2)}) collective-permute-start(bf16[2,96,1024]{2,1,0:T(8,128)(2,1)} %get-tuple-element.88), channel_id=1, source_target_pairs={{0,2},{1,3},{2,0},{3,1},{4,6},{5,7},{6,4},{7,5},{8,10},{9,11},{10,... | collective-permute-start | bytes 1179656 | tf_op jit(solution)/shard_map/ppermute | solution.py:343
  14.6 19.1 %collective-permute-start.5 = (bf16[2,96,1024]{2,1,0:T(8,128)(2,1)}, bf16[2,96,1024]{2,1,0:T(8,128)(2,1)S(1)}, u32[]{:S(2)}, u32[]{:S(2)}) collective-permute-start(bf16[2,96,1024]{2,1,0:T(8,128)(2,1)} %get-tuple-element.90), channel_id=1, source_target_pairs={{0,6},{1,7},{2,4},{3,5},{4,2},{5,3},{6,0},{7,1},{8,14},{9,15},{10,... | collective-permute-start | bytes 1179656 | tf_op jit(solution)/shard_map/ppermute | solution.py:343
  15.0 35.7 %collective-permute-start.11 = (bf16[272,1024]{1,0:T(8,128)(2,1)}, bf16[272,1024]{1,0:T(8,128)(2,1)S(1)}, u32[]{:S(2)}, u32[]{:S(2)}) collective-permute-start(bf16[272,1024]{1,0:T(8,128)(2,1)} %join.1.refs_1_.refs_2_), channel_id=1, source_target_pairs={{0,24},{1,25},{2,26},{3,27},{4,28},{5,29},{6,30},{7,31},{8,0},{9,1... | collective-permute-start | bytes 1671176 | tf_op jit(solution)/shard_map/ppermute | solution.py:347
  26.3 28.1 %collective-permute-start.9 = (bf16[2,96,1024]{2,1,0:T(8,128)(2,1)}, bf16[2,96,1024]{2,1,0:T(8,128)(2,1)S(1)}, u32[]{:S(2)}, u32[]{:S(2)}) collective-permute-start(bf16[2,96,1024]{2,1,0:T(8,128)(2,1)} %get-tuple-element.97), channel_id=1, source_target_pairs={{0,4},{1,5},{2,6},{3,7},{4,0},{5,1},{6,2},{7,3},{8,12},{9,13},{10,... | collective-permute-start | bytes 1179656 | tf_op jit(solution)/shard_map/ppermute | solution.py:343
  28.0 27.9 %collective-permute-start.8 = (bf16[2,96,1024]{2,1,0:T(8,128)(2,1)}, bf16[2,96,1024]{2,1,0:T(8,128)(2,1)S(1)}, u32[]{:S(2)}, u32[]{:S(2)}) collective-permute-start(bf16[2,96,1024]{2,1,0:T(8,128)(2,1)} %get-tuple-element.95), channel_id=1, source_target_pairs={{0,2},{1,3},{2,0},{3,1},{4,6},{5,7},{6,4},{7,5},{8,10},{9,11},{10,... | collective-permute-start | bytes 1179656 | tf_op jit(solution)/shard_map/ppermute | solution.py:343
  33.7 23.8 %collective-permute-start.10 = (bf16[2,96,1024]{2,1,0:T(8,128)(2,1)}, bf16[2,96,1024]{2,1,0:T(8,128)(2,1)S(1)}, u32[]{:S(2)}, u32[]{:S(2)}) collective-permute-start(bf16[2,96,1024]{2,1,0:T(8,128)(2,1)} %get-tuple-element.99), channel_id=1, source_target_pairs={{0,6},{1,7},{2,4},{3,5},{4,2},{5,3},{6,0},{7,1},{8,14},{9,15},{10,... | collective-permute-start | bytes 1179656 | tf_op jit(solution)/shard_map/ppermute | solution.py:343
  36.1 30.5 %collective-permute-start.7 = (bf16[272,1024]{1,0:T(8,128)(2,1)}, bf16[272,1024]{1,0:T(8,128)(2,1)S(1)}, u32[]{:S(2)}, u32[]{:S(2)}) collective-permute-start(bf16[272,1024]{1,0:T(8,128)(2,1)} %join.1.refs_1_.refs_2_), channel_id=1, source_target_pairs={{0,16},{1,17},{2,18},{3,19},{4,20},{5,21},{6,22},{7,23},{8,24},{9,... | collective-permute-start | bytes 1671176 | tf_op jit(solution)/shard_map/ppermute | solution.py:347
  54.4 15.9 %collective-permute-start.14 = (bf16[2,96,1024]{2,1,0:T(8,128)(2,1)}, bf16[2,96,1024]{2,1,0:T(8,128)(2,1)S(1)}, u32[]{:S(2)}, u32[]{:S(2)}) collective-permute-start(bf16[2,96,1024]{2,1,0:T(8,128)(2,1)} %get-tuple-element.109), channel_id=1, source_target_pairs={{0,4},{1,5},{2,6},{3,7},{4,0},{5,1},{6,2},{7,3},{8,12},{9,13},{10,... | collective-permute-start | bytes 1179656 | tf_op jit(solution)/shard_map/ppermute | solution.py:343
  56.0 15.7 %collective-permute-start.12 = (bf16[2,96,1024]{2,1,0:T(8,128)(2,1)}, bf16[2,96,1024]{2,1,0:T(8,128)(2,1)S(1)}, u32[]{:S(2)}, u32[]{:S(2)}) collective-permute-start(bf16[2,96,1024]{2,1,0:T(8,128)(2,1)} %get-tuple-element.105), channel_id=1, source_target_pairs={{0,2},{1,3},{2,0},{3,1},{4,6},{5,7},{6,4},{7,5},{8,10},{9,11},{10,... | collective-permute-start | bytes 1179656 | tf_op jit(solution)/shard_map/ppermute | solution.py:343
  57.5 15.7 %collective-permute-start.16 = (bf16[2,96,1024]{2,1,0:T(8,128)(2,1)}, bf16[2,96,1024]{2,1,0:T(8,128)(2,1)S(1)}, u32[]{:S(2)}, u32[]{:S(2)}) collective-permute-start(bf16[2,96,1024]{2,1,0:T(8,128)(2,1)} %get-tuple-element.113), channel_id=1, source_target_pairs={{0,6},{1,7},{2,4},{3,5},{4,2},{5,3},{6,0},{7,1},{8,14},{9,15},{10,... | collective-permute-start | bytes 1179656 | tf_op jit(solution)/shard_map/ppermute | solution.py:343
  70.3 16.9 %collective-permute-start.15 = (bf16[2,96,1024]{2,1,0:T(8,128)(2,1)}, bf16[2,96,1024]{2,1,0:T(8,128)(2,1)S(1)}, u32[]{:S(2)}, u32[]{:S(2)}) collective-permute-start(bf16[2,96,1024]{2,1,0:T(8,128)(2,1)} %get-tuple-element.110), channel_id=1, source_target_pairs={{0,4},{1,5},{2,6},{3,7},{4,0},{5,1},{6,2},{7,3},{8,12},{9,13},{10,... | collective-permute-start | bytes 1179656 | tf_op jit(solution)/shard_map/ppermute | solution.py:343
  71.6 15.6 %collective-permute-start.13 = (bf16[2,96,1024]{2,1,0:T(8,128)(2,1)}, bf16[2,96,1024]{2,1,0:T(8,128)(2,1)S(1)}, u32[]{:S(2)}, u32[]{:S(2)}) collective-permute-start(bf16[2,96,1024]{2,1,0:T(8,128)(2,1)} %get-tuple-element.106), channel_id=1, source_target_pairs={{0,2},{1,3},{2,0},{3,1},{4,6},{5,7},{6,4},{7,5},{8,10},{9,11},{10,... | collective-permute-start | bytes 1179656 | tf_op jit(solution)/shard_map/ppermute | solution.py:343
  73.1 19.5 %collective-permute-start.17 = (bf16[2,96,1024]{2,1,0:T(8,128)(2,1)}, bf16[2,96,1024]{2,1,0:T(8,128)(2,1)S(1)}, u32[]{:S(2)}, u32[]{:S(2)}) collective-permute-start(bf16[2,96,1024]{2,1,0:T(8,128)(2,1)} %get-tuple-element.114), channel_id=1, source_target_pairs={{0,6},{1,7},{2,4},{3,5},{4,2},{5,3},{6,0},{7,1},{8,14},{9,15},{10,... | collective-permute-start | bytes 1179656 | tf_op jit(solution)/shard_map/ppermute | solution.py:343
  87.3 24.9 %collective-permute-start.18 = (bf16[2,96,1024]{2,1,0:T(8,128)(2,1)}, bf16[2,96,1024]{2,1,0:T(8,128)(2,1)S(1)}, u32[]{:S(2)}, u32[]{:S(2)}) collective-permute-start(bf16[2,96,1024]{2,1,0:T(8,128)(2,1)} %get-tuple-element.119), channel_id=1, source_target_pairs={{0,2},{1,3},{2,0},{3,1},{4,6},{5,7},{6,4},{7,5},{8,10},{9,11},{10,... | collective-permute-start | bytes 1179656 | tf_op jit(solution)/shard_map/ppermute | solution.py:343
  87.3 24.8 %collective-permute-start.22 = (bf16[2,96,1024]{2,1,0:T(8,128)(2,1)}, bf16[2,96,1024]{2,1,0:T(8,128)(2,1)S(1)}, u32[]{:S(2)}, u32[]{:S(2)}) collective-permute-start(bf16[2,96,1024]{2,1,0:T(8,128)(2,1)} %get-tuple-element.127), channel_id=1, source_target_pairs={{0,4},{1,5},{2,6},{3,7},{4,0},{5,1},{6,2},{7,3},{8,12},{9,13},{10,... | collective-permute-start | bytes 1179656 | tf_op jit(solution)/shard_map/ppermute | solution.py:343
  92.6 19.5 %collective-permute-start.26 = (bf16[2,96,1024]{2,1,0:T(8,128)(2,1)}, bf16[2,96,1024]{2,1,0:T(8,128)(2,1)S(1)}, u32[]{:S(2)}, u32[]{:S(2)}) collective-permute-start(bf16[2,96,1024]{2,1,0:T(8,128)(2,1)} %get-tuple-element.135), channel_id=1, source_target_pairs={{0,6},{1,7},{2,4},{3,5},{4,2},{5,3},{6,0},{7,1},{8,14},{9,15},{10,... | collective-permute-start | bytes 1179656 | tf_op jit(solution)/shard_map/ppermute | solution.py:343
  113.0 15.2 %collective-permute-start.23 = (bf16[2,96,1024]{2,1,0:T(8,128)(2,1)S(1)}, bf16[2,96,1024]{2,1,0:T(8,128)(2,1)S(1)}, u32[]{:S(2)}, u32[]{:S(2)}) collective-permute-start(bf16[2,96,1024]{2,1,0:T(8,128)(2,1)S(1)} %copy-done.30), channel_id=1, source_target_pairs={{0,4},{1,5},{2,6},{3,7},{4,0},{5,1},{6,2},{7,3},{8,12},{9,13},{10,... | collective-permute-start | bytes 1179656 | tf_op jit(solution)/shard_map/ppermute | solution.py:343
  119.3 31.3 %collective-permute-start.30 = (bf16[272,1024]{1,0:T(8,128)(2,1)}, bf16[272,1024]{1,0:T(8,128)(2,1)S(1)}, u32[]{:S(2)}, u32[]{:S(2)}) collective-permute-start(bf16[272,1024]{1,0:T(8,128)(2,1)} %merge.4.refs_6_), channel_id=1, source_target_pairs={{0,24},{1,25},{2,26},{3,27},{4,28},{5,29},{6,30},{7,31},{8,0},{9,1... | collective-permute-start | bytes 1671176 | tf_op jit(solution)/shard_map/ppermute | solution.py:347
  124.1 18.9 %collective-permute-start.28 = (bf16[2,96,1024]{2,1,0:T(8,128)(2,1)S(1)}, bf16[2,96,1024]{2,1,0:T(8,128)(2,1)S(1)}, u32[]{:S(2)}, u32[]{:S(2)}) collective-permute-start(bf16[2,96,1024]{2,1,0:T(8,128)(2,1)S(1)} %copy-done.26), channel_id=1, source_target_pairs={{0,6},{1,7},{2,4},{3,5},{4,2},{5,3},{6,0},{7,1},{8,14},{9,15},{10,... | collective-permute-start | bytes 1179656 | tf_op jit(solution)/shard_map/ppermute | solution.py:343
  133.7 27.4 %collective-permute-start.31 = (bf16[272,1024]{1,0:T(8,128)(2,1)}, bf16[272,1024]{1,0:T(8,128)(2,1)S(1)}, u32[]{:S(2)}, u32[]{:S(2)}) collective-permute-start(bf16[272,1024]{1,0:T(8,128)(2,1)} %merge.5.refs_20_), channel_id=1, source_target_pairs={{0,8},{1,9},{2,10},{3,11},{4,12},{5,13},{6,14},{7,15},{8,16},{9,17... | collective-permute-start | bytes 1671176 | tf_op jit(solution)/shard_map/ppermute | solution.py:347
  148.0 27.6 %collective-permute-start.32 = (bf16[272,1024]{1,0:T(8,128)(2,1)}, bf16[272,1024]{1,0:T(8,128)(2,1)S(1)}, u32[]{:S(2)}, u32[]{:S(2)}) collective-permute-start(bf16[272,1024]{1,0:T(8,128)(2,1)} %merge.6.refs_21_), channel_id=1, source_target_pairs={{0,16},{1,17},{2,18},{3,19},{4,20},{5,21},{6,22},{7,23},{8,24},{9,... | collective-permute-start | bytes 1671176 | tf_op jit(solution)/shard_map/ppermute | solution.py:347
  150.6 19.1 %collective-permute-start.25 = (bf16[2,96,1024]{2,1,0:T(8,128)(2,1)S(1)}, bf16[2,96,1024]{2,1,0:T(8,128)(2,1)S(1)}, u32[]{:S(2)}, u32[]{:S(2)}) collective-permute-start(bf16[2,96,1024]{2,1,0:T(8,128)(2,1)S(1)} %copy-done.22), channel_id=1, source_target_pairs={{0,4},{1,5},{2,6},{3,7},{4,0},{5,1},{6,2},{7,3},{8,12},{9,13},{10,... | collective-permute-start | bytes 1179656 | tf_op jit(solution)/shard_map/ppermute | solution.py:343
  151.4 18.3 %collective-permute-start.21 = (bf16[2,96,1024]{2,1,0:T(8,128)(2,1)S(1)}, bf16[2,96,1024]{2,1,0:T(8,128)(2,1)S(1)}, u32[]{:S(2)}, u32[]{:S(2)}) collective-permute-start(bf16[2,96,1024]{2,1,0:T(8,128)(2,1)S(1)} %copy-done.21), channel_id=1, source_target_pairs={{0,2},{1,3},{2,0},{3,1},{4,6},{5,7},{6,4},{7,5},{8,10},{9,11},{10,... | collective-permute-start | bytes 1179656 | tf_op jit(solution)/shard_map/ppermute | solution.py:343
  (52 other events, 550.0 us)

commit v4 on v3

--- a/solution.py
+++ b/solution.py
@@ -141,13 +141,10 @@
 COST = {'join': 1.0, 'pack': 0, 'expert': 0, 'merge': 150, 'weight': 0}
 WHEN = 0
 CHAINZ = 0
-FAR = 0
 WPOS = 2
 BEHIND = 1
 STRICT = 0
 AHEAD = 1
-WEIGHT_A = 1
-WEIGHT_B = 2
 VMEM = pl.BlockSpec(memory_space=pltpu.VMEM)
 SMEM = pl.BlockSpec(memory_space=pltpu.SMEM)
 
@@ -434,7 +431,7 @@
             outs = expert(*arrived[step], *mats, last)
             last = outs[0]
             results[step], kept[step] = outs[:CHIPS], outs[CHIPS:]
-    homeward = (sorted(order[1:], key=lambda step: -min(step, levels - step)) if FAR else order[1:]) + order[:1]
+    homeward = order[1:2] + order[:1:-1] + order[:1]
     returned = {step: exchange(results[step]) for step in homeward}
     saved = [value for step in order for value in kept[step]]
     sent = []

time: 181 us -> 175 us (0.967)
  waiting for transfers between devices: 47.4 us -> 41.1 us
    ppermute x6, waiting for transfers between devices: 11.1 us -> 5.12 us  [climb(): return lax.ppermute(value, axes, pairs)]
    unnamed x85 -> x79, local copies, waits for them, and re-layouts: 5.92 us -> 6.19 us
  transfers between devices with their start and end apart: 34 -> 34, of which waited for: 9 -> 8; matrix products, arithmetic and copies ran while one was open for 1% -> 1% of each run, Pallas kernels for 41% -> 42%
where the time goes in v4:
time: 175 us
  Pallas kernels  77.7 us (44%)
  starting transfers between devices  48.1 us (27%)
  waiting for transfers between devices  41.1 us (23%)
  local copies, waits for them, and re-layouts  6.19 us (4%)
    ppermute x28, waiting for transfers between devices, flip(): return lax.ppermute(value, axes, pairs)  36 us
    pallas_call x4, Pallas kernels, local_plane(): outs = expert(*arrived[step], *mats, last)  34.1 us
    ppermute x28, starting transfers between devices, flip(): return lax.ppermute(value, axes, pairs)  32.1 us
    ppermute x6, starting transfers between devices, climb(): return lax.ppermute(value, axes, pairs)  16 us
    pallas_call x4, Pallas kernels, local_plane(): merge(len(earlier), final)  14.1 us
    pallas_call x4, Pallas kernels, local_plane(): packed = pack(table, blocks[order[turn]], last)  11.8 us
    pallas_call x1, Pallas kernels, local_plane(): grad_mats = weight(0, 1)(*saved, partial, last)  8.08 us
    pallas_call x1, Pallas kernels, local_plane(): partial, = weight(1, 0)(*saved, last)  7.68 us
  transfers between devices with their start and end apart: 34, of which 8 were waited for; matrix products, arithmetic and copies ran while one was open for 1% of the time, Pallas kernels for 42%

profile of v4, /device:TPU:0, one launch (start us, length us, event | category | flops | bytes accessed | tf_op | source)
XLA Modules:
  0.0 174.6 jit_solution(13937024593091403174)
XLA Ops:
  5.0 2.7 %collective-permute-start.6 = (bf16[272,1024]{1,0:T(8,128)(2,1)}, bf16[272,1024]{1,0:T(8,128)(2,1)}, u32[]{:S(2)}, u32[]{:S(2)}) collective-permute-start(bf16[272,1024]{1,0:T(8,128)(2,1)} %join.1.refs_1_.refs_2_), channel_id=1, source_target_pairs={{0,8},{1,9},{2,10},{3,11},{4,12},{5,13},{6,14},{7,15},{8,16},{9,17... | collective-permute-start | bytes 1671176 | tf_op jit(solution)/shard_map/ppermute | solution.py:344
  8.2 3.3 %pack.4 = (bf16[2,96,1024]{2,1,0:T(8,128)(2,1)}, bf16[2,96,1024]{2,1,0:T(8,128)(2,1)}, bf16[2,96,1024]{2,1,0:T(8,128)(2,1)}, bf16[2,96,1024]{2,1,0:T(8,128)(2,1)}) custom-call(s32[8]{0:T(128)} %xor_add_fusion.refs_0_, bf16[272,1024]{1,0:T(8,128)(2,1)} %join.1.refs_1_.refs_2_, bf16[272,1024]{1,0:T(8,128)(2,1)} %join.1.refs_1_.refs_2_), custom_call_target="tpu_custom_call" | custom-call | tf_op jit(solution)/shard_map/pack/pallas_call | solution.py:426
  15.0 3.4 %collective-permute-start.7 = (bf16[272,1024]{1,0:T(8,128)(2,1)}, bf16[272,1024]{1,0:T(8,128)(2,1)S(1)}, u32[]{:S(2)}, u32[]{:S(2)}) collective-permute-start(bf16[272,1024]{1,0:T(8,128)(2,1)} %join.1.refs_1_.refs_2_), channel_id=1, source_target_pairs={{0,24},{1,25},{2,26},{3,27},{4,28},{5,29},{6,30},{7,31},{8,0},{9,1... | collective-permute-start | bytes 1671176 | tf_op jit(solution)/shard_map/ppermute | solution.py:344
  18.4 5.1 %collective-permute-done.6.refs_1_ = bf16[272,1024]{1,0:T(8,128)(2,1)} collective-permute-done((bf16[272,1024]{1,0:T(8,128)(2,1)}, bf16[272,1024]{1,0:T(8,128)(2,1)}, u32[]{:S(2)}, u32[]{:S(2)}) %collective-permute-start.6) | collective-permute-done | bytes 557088 | tf_op jit(solution)/shard_map/ppermute | solution.py:344
  23.5 2.8 %pack.5 = (bf16[2,96,1024]{2,1,0:T(8,128)(2,1)}, bf16[2,96,1024]{2,1,0:T(8,128)(2,1)}, bf16[2,96,1024]{2,1,0:T(8,128)(2,1)}, bf16[2,96,1024]{2,1,0:T(8,128)(2,1)}) custom-call(s32[8]{0:T(128)} %xor_add_fusion.refs_0_, bf16[272,1024]{1,0:T(8,128)(2,1)} %collective-permute-done.6.refs_1_, bf16[2,96,1024]{2,1,0:T(8,128)(2,1)} %get-tuple-element.87.refs_2_.refs_0_), custom_call_target="tpu_custom_call" | custom-call | tf_op jit(solution)/shard_map/pack/pallas_call | solution.py:426
  29.5 4.1 %collective-permute-done.5.refs_3_ = bf16[2,96,1024]{2,1,0:T(8,128)(2,1)S(1)} collective-permute-done((bf16[2,96,1024]{2,1,0:T(8,128)(2,1)}, bf16[2,96,1024]{2,1,0:T(8,128)(2,1)S(1)}, u32[]{:S(2)}, u32[]{:S(2)}) %collective-permute-start.5) | collective-permute-done | bytes 393248 | tf_op jit(solution)/shard_map/ppermute | solution.py:340
  36.1 6.2 %collective-permute-start.14 = (bf16[272,1024]{1,0:T(8,128)(2,1)}, bf16[272,1024]{1,0:T(8,128)(2,1)S(1)}, u32[]{:S(2)}, u32[]{:S(2)}) collective-permute-start(bf16[272,1024]{1,0:T(8,128)(2,1)} %join.1.refs_1_.refs_2_), channel_id=1, source_target_pairs={{0,16},{1,17},{2,18},{3,19},{4,20},{5,21},{6,22},{7,23},{8,24},{9,... | collective-permute-start | bytes 1671176 | tf_op jit(solution)/shard_map/ppermute | solution.py:344
  42.3 8.5 %expert.4 = (bf16[2,96,1024]{2,1,0:T(8,128)(2,1)}, bf16[2,96,1024]{2,1,0:T(8,128)(2,1)}, bf16[2,96,1024]{2,1,0:T(8,128)(2,1)}, bf16[2,96,1024]{2,1,0:T(8,128)(2,...) custom-call(bf16[2,96,1024]{2,1,0:T(8,128)(2,1)} %get-tuple-element., ...), custom_call_target="tpu_custom_call" | custom-call | tf_op jit(solution)/shard_map/expert/pallas_call | solution.py:431
  51.6 2.8 %pack.6 = (bf16[2,96,1024]{2,1,0:T(8,128)(2,1)}, bf16[2,96,1024]{2,1,0:T(8,128)(2,1)}, bf16[2,96,1024]{2,1,0:T(8,128)(2,1)}, bf16[2,96,1024]{2,1,0:T(8,128)(2,1)}) custom-call(s32[8]{0:T(128)} %xor_add_fusion.refs_0_, bf16[272,1024]{1,0:T(8,128)(2,1)} %copy-done.4, bf16[2,96,1024]{2,1,0:T(8,128)(2,1)} %get-tuple-element.92.refs_2_), custom_call_target="tpu_custom_call" | custom-call | tf_op jit(solution)/shard_map/pack/pallas_call | solution.py:426
  58.2 8.4 %expert.5 = (bf16[2,96,1024]{2,1,0:T(8,128)(2,1)}, bf16[2,96,1024]{2,1,0:T(8,128)(2,1)}, bf16[2,96,1024]{2,1,0:T(8,128)(2,1)}, bf16[2,96,1024]{2,1,0:T(8,128)(2,...) custom-call(bf16[2,96,1024]{2,1,0:T(8,128)(2,1)} %get-tuple-element., ...), custom_call_target="tpu_custom_call" | custom-call | tf_op jit(solution)/shard_map/expert/pallas_call | solution.py:431
  67.5 2.8 %pack.7 = (bf16[2,96,1024]{2,1,0:T(8,128)(2,1)}, bf16[2,96,1024]{2,1,0:T(8,128)(2,1)}, bf16[2,96,1024]{2,1,0:T(8,128)(2,1)}, bf16[2,96,1024]{2,1,0:T(8,128)(2,1)}) custom-call(s32[8]{0:T(128)} %xor_add_fusion.refs_0_, bf16[272,1024]{1,0:T(8,128)(2,1)} %copy-done.5, bf16[2,96,1024]{2,1,0:T(8,128)(2,1)} %get-tuple-element.107.refs_2_), custom_call_target="tpu_custom_call" | custom-call | tf_op jit(solution)/shard_map/pack/pallas_call | solution.py:426
  73.9 13.3 %collective-permute-done.16.refs_2_ = bf16[2,96,1024]{2,1,0:T(8,128)(2,1)S(1)} collective-permute-done((bf16[2,96,1024]{2,1,0:T(8,128)(2,1)}, bf16[2,96,1024]{2,1,0:T(8,128)(2,1)S(1)}, u32[]{:S(2)}, u32[]{:S(2)}) %collective-permute-start.16) | collective-permute-done | bytes 393248 | tf_op jit(solution)/shard_map/ppermute | solution.py:340
  89.0 3.7 %collective-permute-done.17.refs_3_ = bf16[2,96,1024]{2,1,0:T(8,128)(2,1)S(1)} collective-permute-done((bf16[2,96,1024]{2,1,0:T(8,128)(2,1)}, bf16[2,96,1024]{2,1,0:T(8,128)(2,1)S(1)}, u32[]{:S(2)}, u32[]{:S(2)}) %collective-permute-start.17) | collective-permute-done | bytes 393248 | tf_op jit(solution)/shard_map/ppermute | solution.py:340
  94.9 8.5 %expert.6 = (bf16[2,96,1024]{2,1,0:T(8,128)(2,1)}, bf16[2,96,1024]{2,1,0:T(8,128)(2,1)}, bf16[2,96,1024]{2,1,0:T(8,128)(2,1)}, bf16[2,96,1024]{2,1,0:T(8,128)(2,...) custom-call(bf16[2,96,1024]{2,1,0:T(8,128)(2,1)} %get-tuple-element., ...), custom_call_target="tpu_custom_call" | custom-call | tf_op jit(solution)/shard_map/expert/pallas_call | solution.py:431
  103.4 8.7 %expert.7 = (bf16[2,96,1024]{2,1,0:T(8,128)(2,1)}, bf16[2,96,1024]{2,1,0:T(8,128)(2,1)}, bf16[2,96,1024]{2,1,0:T(8,128)(2,1)}, bf16[2,96,1024]{2,1,0:T(8,128)(2,...) custom-call(bf16[2,96,1024]{2,1,0:T(8,128)(2,1)} %get-tuple-element., ...), custom_call_target="tpu_custom_call" | custom-call | tf_op jit(solution)/shard_map/expert/pallas_call | solution.py:431
  115.7 3.5 %merge.4.refs_6_ = bf16[272,1024]{1,0:T(8,128)(2,1)} custom-call(s32[8]{0:T(128)} %xor_add_fusion.refs_0_, bf16[272,1024]{1,0:T(8,128)(2,1)} %collective-permute-done.6.refs_1_, bf16[2,96,1024]{2,1,0:T(8,128)(2,1)} %get-tuple-element.107.refs_2_, bf16[2,96,1024]{2,1,0:T(8,128)(2,1)} %copy-done.28, bf16[2,96,1024]{2,1,0:T(8,128)(2,1)} %copy-done.29, ...), custom_call_target="tpu_custom_call" | custom-call | flops 60397977600 | bytes 2686976 | tf_op jit(solution)/shard_map/merge/pallas_call | solution.py:447
  120.2 3.8 %collective-permute-done.27.refs_5_ = bf16[2,96,1024]{2,1,0:T(8,128)(2,1)S(1)} collective-permute-done((bf16[2,96,1024]{2,1,0:T(8,128)(2,1)}, bf16[2,96,1024]{2,1,0:T(8,128)(2,1)S(1)}, u32[]{:S(2)}, u32[]{:S(2)}) %collective-permute-start.27) | collective-permute-done | bytes 393248 | tf_op jit(solution)/shard_map/ppermute | solution.py:340
  125.6 2.5 %collective-permute-done.23.refs_4_ = bf16[2,96,1024]{2,1,0:T(8,128)(2,1)S(1)} collective-permute-done((bf16[2,96,1024]{2,1,0:T(8,128)(2,1)}, bf16[2,96,1024]{2,1,0:T(8,128)(2,1)S(1)}, u32[]{:S(2)}, u32[]{:S(2)}) %collective-permute-start.23) | collective-permute-done | bytes 393248 | tf_op jit(solution)/shard_map/ppermute | solution.py:340
  130.3 3.4 %merge.5.refs_20_ = bf16[272,1024]{1,0:T(8,128)(2,1)} custom-call(s32[8]{0:T(128)} %xor_add_fusion.refs_0_, bf16[272,1024]{1,0:T(8,128)(2,1)} %copy-done.5, bf16[2,96,1024]{2,1,0:T(8,128)(2,1)} %get-tuple-element.139.refs_6_.refs_2_, bf16[2,96,1024]{2,1,0:T(8,128)(2,1)} %copy-done.37, bf16[2,96,1024]{2,1,0:T(8,128)(2,1)} %copy-done.35, ...), custom_call_target="tpu_custom_call" | custom-call | flops 60397977600 | bytes 2686976 | tf_op jit(solution)/shard_map/merge/pallas_call | solution.py:447
  134.9 7.7 %weight.2.refs_6_ = bf16[1536,1024]{1,0:T(8,128)(2,1)} custom-call(bf16[2,192,1024]{2,1,0:T(8,128)(2,1)} %get-tuple-element.140.refs_0_, bf16[2,192,1024]{2,1,0:T(8,128)(2,1)} %get-tuple-element.141.refs_1_, bf16[2,192,512]{2,1,0:T(8,128)(2,1)} %get-tuple-element.142.refs_2_, bf16[2,192,512]{2,1,0:T(8,128)(2,1)} %get-tuple-element.143.refs_3_, ...), custom_call_target="tpu_custom_call" | custom-call | tf_op jit(solution)/shard_map/weight/pallas_call | solution.py:440
  144.2 3.4 %merge.6.refs_21_ = bf16[272,1024]{1,0:T(8,128)(2,1)} custom-call(s32[8]{0:T(128)} %xor_add_fusion.refs_0_, bf16[272,1024]{1,0:T(8,128)(2,1)} %copy-done.4, bf16[2,96,1024]{2,1,0:T(8,128)(2,1)} %get-tuple-element.116.refs_10_.refs_2_, bf16[2,96,1024]{2,1,0:T(8,128)(2,1)} %copy-done.38, bf16[2,96,1024]{2,1,0:T(8,128)(2,1)} %copy-done.36, ...), custom_call_target="tpu_custom_call" | custom-call | flops 60397977600 | bytes 2686976 | tf_op jit(solution)/shard_map/merge/pallas_call | solution.py:447
  153.0 8.1 %weight.3 = (bf16[1024,512]{1,0:T(8,128)(2,1)}, bf16[1024,512]{1,0:T(8,128)(2,1)}, bf16[512,1024]{1,0:T(8,128)(2,1)}) custom-call(bf16[2,192,1024]{2,1,0:T(8,128)(2,1)} %get-tuple-element.140.refs_0_, bf16[2,192,1024]{2,1,0:T(8,128)(2,1)} %get-tuple-element.141.refs_1_, bf16[2,192,512]{2,1,0:T(8,128)(2,1)} %get-tuple-element.142.refs_2_, ...), custom_call_target="tpu_custom_call" | custom-call | tf_op jit(solution)/shard_map/weight/pallas_call | solution.py:444
  162.1 7.6 %collective-permute-done.25.refs_4_ = bf16[2,96,1024]{2,1,0:T(8,128)(2,1)S(1)} collective-permute-done((bf16[2,96,1024]{2,1,0:T(8,128)(2,1)S(1)}, bf16[2,96,1024]{2,1,0:T(8,128)(2,1)S(1)}, u32[]{:S(2)}, u32[]{:S(2)}) %collective-permute-start.25) | collective-permute-done | bytes 393248 | tf_op jit(solution)/shard_map/ppermute | solution.py:340
  170.8 3.8 %merge.7 = (bf16[128,1024]{1,0:T(8,128)(2,1)}, bf16[128,1024]{1,0:T(8,128)(2,1)}, f32[8,128]{1,0:T(8,128)}) custom-call(s32[8]{0:T(128)} %xor_add_fusion.refs_0_, bf16[272,1024]{1,0:T(8,128)(2,1)} %join.1.refs_1_.refs_2_, bf16[2,96,1024]{2,1,0:T(8,128)(2,1)} %get-tuple-element.92.refs_2_, bf16[2,96,1024]{2,1,0:T(8,128)(2,1)} %copy-done.32, ...), custom_call_target="tpu_custom_call" | custom-call | flops 60397977600 | bytes 2686976 | tf_op jit(solution)/shard_map/merge/pallas_call | solution.py:447
  (139 shorter events, 45.5 us)
Async XLA Ops:
  5.0 18.5 %collective-permute-start.6 = (bf16[272,1024]{1,0:T(8,128)(2,1)}, bf16[272,1024]{1,0:T(8,128)(2,1)}, u32[]{:S(2)}, u32[]{:S(2)}) collective-permute-start(bf16[272,1024]{1,0:T(8,128)(2,1)} %join.1.refs_1_.refs_2_), channel_id=1, source_target_pairs={{0,8},{1,9},{2,10},{3,11},{4,12},{5,13},{6,14},{7,15},{8,16},{9,17... | collective-permute-start | bytes 1671176 | tf_op jit(solution)/shard_map/ppermute | solution.py:344
  13.0 15.0 %collective-permute-start.3 = (bf16[2,96,1024]{2,1,0:T(8,128)(2,1)}, bf16[2,96,1024]{2,1,0:T(8,128)(2,1)S(1)}, u32[]{:S(2)}, u32[]{:S(2)}) collective-permute-start(bf16[2,96,1024]{2,1,0:T(8,128)(2,1)} %get-tuple-element.88), channel_id=1, source_target_pairs={{0,2},{1,3},{2,0},{3,1},{4,6},{5,7},{6,4},{7,5},{8,10},{9,11},{10,... | collective-permute-start | bytes 1179656 | tf_op jit(solution)/shard_map/ppermute | solution.py:340
  14.5 19.1 %collective-permute-start.5 = (bf16[2,96,1024]{2,1,0:T(8,128)(2,1)}, bf16[2,96,1024]{2,1,0:T(8,128)(2,1)S(1)}, u32[]{:S(2)}, u32[]{:S(2)}) collective-permute-start(bf16[2,96,1024]{2,1,0:T(8,128)(2,1)} %get-tuple-element.90), channel_id=1, source_target_pairs={{0,6},{1,7},{2,4},{3,5},{4,2},{5,3},{6,0},{7,1},{8,14},{9,15},{10,... | collective-permute-start | bytes 1179656 | tf_op jit(solution)/shard_map/ppermute | solution.py:340
  15.0 35.8 %collective-permute-start.7 = (bf16[272,1024]{1,0:T(8,128)(2,1)}, bf16[272,1024]{1,0:T(8,128)(2,1)S(1)}, u32[]{:S(2)}, u32[]{:S(2)}) collective-permute-start(bf16[272,1024]{1,0:T(8,128)(2,1)} %join.1.refs_1_.refs_2_), channel_id=1, source_target_pairs={{0,24},{1,25},{2,26},{3,27},{4,28},{5,29},{6,30},{7,31},{8,0},{9,1... | collective-permute-start | bytes 1671176 | tf_op jit(solution)/shard_map/ppermute | solution.py:344
  26.3 28.1 %collective-permute-start.10 = (bf16[2,96,1024]{2,1,0:T(8,128)(2,1)}, bf16[2,96,1024]{2,1,0:T(8,128)(2,1)S(1)}, u32[]{:S(2)}, u32[]{:S(2)}) collective-permute-start(bf16[2,96,1024]{2,1,0:T(8,128)(2,1)} %get-tuple-element.101), channel_id=1, source_target_pairs={{0,4},{1,5},{2,6},{3,7},{4,0},{5,1},{6,2},{7,3},{8,12},{9,13},{10,... | collective-permute-start | bytes 1179656 | tf_op jit(solution)/shard_map/ppermute | solution.py:340
  28.0 27.9 %collective-permute-start.8 = (bf16[2,96,1024]{2,1,0:T(8,128)(2,1)}, bf16[2,96,1024]{2,1,0:T(8,128)(2,1)S(1)}, u32[]{:S(2)}, u32[]{:S(2)}) collective-permute-start(bf16[2,96,1024]{2,1,0:T(8,128)(2,1)} %get-tuple-element.97), channel_id=1, source_target_pairs={{0,2},{1,3},{2,0},{3,1},{4,6},{5,7},{6,4},{7,5},{8,10},{9,11},{10,... | collective-permute-start | bytes 1179656 | tf_op jit(solution)/shard_map/ppermute | solution.py:340
  33.6 23.9 %collective-permute-start.12 = (bf16[2,96,1024]{2,1,0:T(8,128)(2,1)}, bf16[2,96,1024]{2,1,0:T(8,128)(2,1)S(1)}, u32[]{:S(2)}, u32[]{:S(2)}) collective-permute-start(bf16[2,96,1024]{2,1,0:T(8,128)(2,1)} %get-tuple-element.105), channel_id=1, source_target_pairs={{0,6},{1,7},{2,4},{3,5},{4,2},{5,3},{6,0},{7,1},{8,14},{9,15},{10,... | collective-permute-start | bytes 1179656 | tf_op jit(solution)/shard_map/ppermute | solution.py:340
  36.1 30.6 %collective-permute-start.14 = (bf16[272,1024]{1,0:T(8,128)(2,1)}, bf16[272,1024]{1,0:T(8,128)(2,1)S(1)}, u32[]{:S(2)}, u32[]{:S(2)}) collective-permute-start(bf16[272,1024]{1,0:T(8,128)(2,1)} %join.1.refs_1_.refs_2_), channel_id=1, source_target_pairs={{0,16},{1,17},{2,18},{3,19},{4,20},{5,21},{6,22},{7,23},{8,24},{9,... | collective-permute-start | bytes 1671176 | tf_op jit(solution)/shard_map/ppermute | solution.py:344
  54.4 15.9 %collective-permute-start.11 = (bf16[2,96,1024]{2,1,0:T(8,128)(2,1)}, bf16[2,96,1024]{2,1,0:T(8,128)(2,1)S(1)}, u32[]{:S(2)}, u32[]{:S(2)}) collective-permute-start(bf16[2,96,1024]{2,1,0:T(8,128)(2,1)} %get-tuple-element.102), channel_id=1, source_target_pairs={{0,4},{1,5},{2,6},{3,7},{4,0},{5,1},{6,2},{7,3},{8,12},{9,13},{10,... | collective-permute-start | bytes 1179656 | tf_op jit(solution)/shard_map/ppermute | solution.py:340
  56.0 15.7 %collective-permute-start.9 = (bf16[2,96,1024]{2,1,0:T(8,128)(2,1)}, bf16[2,96,1024]{2,1,0:T(8,128)(2,1)S(1)}, u32[]{:S(2)}, u32[]{:S(2)}) collective-permute-start(bf16[2,96,1024]{2,1,0:T(8,128)(2,1)} %get-tuple-element.98), channel_id=1, source_target_pairs={{0,2},{1,3},{2,0},{3,1},{4,6},{5,7},{6,4},{7,5},{8,10},{9,11},{10,... | collective-permute-start | bytes 1179656 | tf_op jit(solution)/shard_map/ppermute | solution.py:340
  57.5 15.7 %collective-permute-start.13 = (bf16[2,96,1024]{2,1,0:T(8,128)(2,1)}, bf16[2,96,1024]{2,1,0:T(8,128)(2,1)S(1)}, u32[]{:S(2)}, u32[]{:S(2)}) collective-permute-start(bf16[2,96,1024]{2,1,0:T(8,128)(2,1)} %get-tuple-element.106), channel_id=1, source_target_pairs={{0,6},{1,7},{2,4},{3,5},{4,2},{5,3},{6,0},{7,1},{8,14},{9,15},{10,... | collective-permute-start | bytes 1179656 | tf_op jit(solution)/shard_map/ppermute | solution.py:340
  70.4 16.8 %collective-permute-start.16 = (bf16[2,96,1024]{2,1,0:T(8,128)(2,1)}, bf16[2,96,1024]{2,1,0:T(8,128)(2,1)S(1)}, u32[]{:S(2)}, u32[]{:S(2)}) collective-permute-start(bf16[2,96,1024]{2,1,0:T(8,128)(2,1)} %get-tuple-element.113), channel_id=1, source_target_pairs={{0,4},{1,5},{2,6},{3,7},{4,0},{5,1},{6,2},{7,3},{8,12},{9,13},{10,... | collective-permute-start | bytes 1179656 | tf_op jit(solution)/shard_map/ppermute | solution.py:340
  71.7 15.5 %collective-permute-start.15 = (bf16[2,96,1024]{2,1,0:T(8,128)(2,1)}, bf16[2,96,1024]{2,1,0:T(8,128)(2,1)S(1)}, u32[]{:S(2)}, u32[]{:S(2)}) collective-permute-start(bf16[2,96,1024]{2,1,0:T(8,128)(2,1)} %get-tuple-element.111), channel_id=1, source_target_pairs={{0,2},{1,3},{2,0},{3,1},{4,6},{5,7},{6,4},{7,5},{8,10},{9,11},{10,... | collective-permute-start | bytes 1179656 | tf_op jit(solution)/shard_map/ppermute | solution.py:340
  73.2 19.5 %collective-permute-start.17 = (bf16[2,96,1024]{2,1,0:T(8,128)(2,1)}, bf16[2,96,1024]{2,1,0:T(8,128)(2,1)S(1)}, u32[]{:S(2)}, u32[]{:S(2)}) collective-permute-start(bf16[2,96,1024]{2,1,0:T(8,128)(2,1)} %get-tuple-element.115), channel_id=1, source_target_pairs={{0,6},{1,7},{2,4},{3,5},{4,2},{5,3},{6,0},{7,1},{8,14},{9,15},{10,... | collective-permute-start | bytes 1179656 | tf_op jit(solution)/shard_map/ppermute | solution.py:340
  87.2 24.9 %collective-permute-start.18 = (bf16[2,96,1024]{2,1,0:T(8,128)(2,1)}, bf16[2,96,1024]{2,1,0:T(8,128)(2,1)S(1)}, u32[]{:S(2)}, u32[]{:S(2)}) collective-permute-start(bf16[2,96,1024]{2,1,0:T(8,128)(2,1)} %get-tuple-element.119), channel_id=1, source_target_pairs={{0,2},{1,3},{2,0},{3,1},{4,6},{5,7},{6,4},{7,5},{8,10},{9,11},{10,... | collective-permute-start | bytes 1179656 | tf_op jit(solution)/shard_map/ppermute | solution.py:340
  87.2 24.9 %collective-permute-start.22 = (bf16[2,96,1024]{2,1,0:T(8,128)(2,1)}, bf16[2,96,1024]{2,1,0:T(8,128)(2,1)S(1)}, u32[]{:S(2)}, u32[]{:S(2)}) collective-permute-start(bf16[2,96,1024]{2,1,0:T(8,128)(2,1)} %get-tuple-element.127), channel_id=1, source_target_pairs={{0,4},{1,5},{2,6},{3,7},{4,0},{5,1},{6,2},{7,3},{8,12},{9,13},{10,... | collective-permute-start | bytes 1179656 | tf_op jit(solution)/shard_map/ppermute | solution.py:340
  92.7 19.4 %collective-permute-start.26 = (bf16[2,96,1024]{2,1,0:T(8,128)(2,1)}, bf16[2,96,1024]{2,1,0:T(8,128)(2,1)S(1)}, u32[]{:S(2)}, u32[]{:S(2)}) collective-permute-start(bf16[2,96,1024]{2,1,0:T(8,128)(2,1)} %get-tuple-element.135), channel_id=1, source_target_pairs={{0,6},{1,7},{2,4},{3,5},{4,2},{5,3},{6,0},{7,1},{8,14},{9,15},{10,... | collective-permute-start | bytes 1179656 | tf_op jit(solution)/shard_map/ppermute | solution.py:340
  112.9 15.2 %collective-permute-start.23 = (bf16[2,96,1024]{2,1,0:T(8,128)(2,1)}, bf16[2,96,1024]{2,1,0:T(8,128)(2,1)S(1)}, u32[]{:S(2)}, u32[]{:S(2)}) collective-permute-start(bf16[2,96,1024]{2,1,0:T(8,128)(2,1)} %get-tuple-element.128), channel_id=1, source_target_pairs={{0,4},{1,5},{2,6},{3,7},{4,0},{5,1},{6,2},{7,3},{8,12},{9,13},{10,... | collective-permute-start | bytes 1179656 | tf_op jit(solution)/shard_map/ppermute | solution.py:340
  119.2 31.1 %collective-permute-start.30 = (bf16[272,1024]{1,0:T(8,128)(2,1)}, bf16[272,1024]{1,0:T(8,128)(2,1)S(1)}, u32[]{:S(2)}, u32[]{:S(2)}) collective-permute-start(bf16[272,1024]{1,0:T(8,128)(2,1)} %merge.4.refs_6_), channel_id=1, source_target_pairs={{0,24},{1,25},{2,26},{3,27},{4,28},{5,29},{6,30},{7,31},{8,0},{9,1... | collective-permute-start | bytes 1671176 | tf_op jit(solution)/shard_map/ppermute | solution.py:344
  124.0 18.5 %collective-permute-start.28 = (bf16[2,96,1024]{2,1,0:T(8,128)(2,1)S(1)}, bf16[2,96,1024]{2,1,0:T(8,128)(2,1)S(1)}, u32[]{:S(2)}, u32[]{:S(2)}) collective-permute-start(bf16[2,96,1024]{2,1,0:T(8,128)(2,1)S(1)} %copy-done.26), channel_id=1, source_target_pairs={{0,6},{1,7},{2,4},{3,5},{4,2},{5,3},{6,0},{7,1},{8,14},{9,15},{10,... | collective-permute-start | bytes 1179656 | tf_op jit(solution)/shard_map/ppermute | solution.py:340
  133.7 27.4 %collective-permute-start.31 = (bf16[272,1024]{1,0:T(8,128)(2,1)}, bf16[272,1024]{1,0:T(8,128)(2,1)S(1)}, u32[]{:S(2)}, u32[]{:S(2)}) collective-permute-start(bf16[272,1024]{1,0:T(8,128)(2,1)} %merge.5.refs_20_), channel_id=1, source_target_pairs={{0,16},{1,17},{2,18},{3,19},{4,20},{5,21},{6,22},{7,23},{8,24},{9,... | collective-permute-start | bytes 1671176 | tf_op jit(solution)/shard_map/ppermute | solution.py:344
  147.6 22.1 %collective-permute-start.32 = (bf16[272,1024]{1,0:T(8,128)(2,1)}, bf16[272,1024]{1,0:T(8,128)(2,1)S(1)}, u32[]{:S(2)}, u32[]{:S(2)}) collective-permute-start(bf16[272,1024]{1,0:T(8,128)(2,1)} %merge.6.refs_21_), channel_id=1, source_target_pairs={{0,8},{1,9},{2,10},{3,11},{4,12},{5,13},{6,14},{7,15},{8,16},{9,17... | collective-permute-start | bytes 1671176 | tf_op jit(solution)/shard_map/ppermute | solution.py:344
  150.4 19.4 %collective-permute-start.25 = (bf16[2,96,1024]{2,1,0:T(8,128)(2,1)S(1)}, bf16[2,96,1024]{2,1,0:T(8,128)(2,1)S(1)}, u32[]{:S(2)}, u32[]{:S(2)}) collective-permute-start(bf16[2,96,1024]{2,1,0:T(8,128)(2,1)S(1)} %copy-done.22), channel_id=1, source_target_pairs={{0,4},{1,5},{2,6},{3,7},{4,0},{5,1},{6,2},{7,3},{8,12},{9,13},{10,... | collective-permute-start | bytes 1179656 | tf_op jit(solution)/shard_map/ppermute | solution.py:340
  151.4 18.3 %collective-permute-start.21 = (bf16[2,96,1024]{2,1,0:T(8,128)(2,1)S(1)}, bf16[2,96,1024]{2,1,0:T(8,128)(2,1)S(1)}, u32[]{:S(2)}, u32[]{:S(2)}) collective-permute-start(bf16[2,96,1024]{2,1,0:T(8,128)(2,1)S(1)} %copy-done.21), channel_id=1, source_target_pairs={{0,2},{1,3},{2,0},{3,1},{4,6},{5,7},{6,4},{7,5},{8,10},{9,11},{10,... | collective-permute-start | bytes 1179656 | tf_op jit(solution)/shard_map/ppermute | solution.py:340
  (49 other events, 494.8 us)

commit v5 on v4

--- a/solution.py
+++ b/solution.py
@@ -138,7 +138,7 @@
 LEADING = (((0,), (0,)), ((), ()))
 TRAILING = (((1,), (1,)), ((), ()))
 CHIPS = 4
-COST = {'join': 1.0, 'pack': 0, 'expert': 0, 'merge': 150, 'weight': 0}
+COST = {'join': 1.0, 'pack': 0, 'expert': 0, 'merge': 150, 'weight': 25}
 WHEN = 0
 CHAINZ = 0
 WPOS = 2

time: 175 us -> 171 us (0.977)
  local copies, waits for them, and re-layouts: 6.19 us -> 4.31 us
    ppermute x28, waiting for transfers between devices: 36 us -> 31.9 us  [flip(): return lax.ppermute(value, axes, pairs)]
    ppermute x6, waiting for transfers between devices: 5.12 us -> 7.63 us  [climb(): return lax.ppermute(value, axes, pairs)]
    unnamed x79 -> x75, local copies, waits for them, and re-layouts: 6.19 us -> 4.31 us
  transfers between devices with their start and end apart: 34 -> 34, of which waited for: 8 -> 8; matrix products, arithmetic and copies ran while one was open for 1% -> 1% of each run, Pallas kernels for 42% -> 43%
where the time goes in v5:
time: 171 us
  Pallas kernels  77.8 us (45%)
  starting transfers between devices  47.5 us (28%)
  waiting for transfers between devices  39.5 us (23%)
  local copies, waits for them, and re-layouts  4.31 us (3%)
    pallas_call x4, Pallas kernels, local_plane(): outs = expert(*arrived[step], *mats, last)  34.1 us
    ppermute x28, waiting for transfers between devices, flip(): return lax.ppermute(value, axes, pairs)  31.9 us
    ppermute x28, starting transfers between devices, flip(): return lax.ppermute(value, axes, pairs)  31.8 us
    ppermute x6, starting transfers between devices, climb(): return lax.ppermute(value, axes, pairs)  15.8 us
    pallas_call x4, Pallas kernels, local_plane(): merge(len(earlier), final)  14.1 us
    pallas_call x4, Pallas kernels, local_plane(): packed = pack(table, blocks[order[turn]], last)  11.8 us
    pallas_call x1, Pallas kernels, local_plane(): grad_mats = weight(0, 1)(*saved, partial, last)  8.08 us
    pallas_call x1, Pallas kernels, local_plane(): partial, = weight(1, 0)(*saved, last)  7.76 us
  transfers between devices with their start and end apart: 34, of which 8 were waited for; matrix products, arithmetic and copies ran while one was open for 1% of the time, Pallas kernels for 43%

profile of v5, /device:TPU:0, one launch (start us, length us, event | category | flops | bytes accessed | tf_op | source)
XLA Modules:
  0.0 170.7 jit_solution(2387774133367658394)
XLA Ops:
  5.0 2.7 %collective-permute-start.6 = (bf16[272,1024]{1,0:T(8,128)(2,1)}, bf16[272,1024]{1,0:T(8,128)(2,1)}, u32[]{:S(2)}, u32[]{:S(2)}) collective-permute-start(bf16[272,1024]{1,0:T(8,128)(2,1)} %join.1.refs_1_.refs_2_), channel_id=1, source_target_pairs={{0,8},{1,9},{2,10},{3,11},{4,12},{5,13},{6,14},{7,15},{8,16},{9,17... | collective-permute-start | bytes 1671176 | tf_op jit(solution)/shard_map/ppermute | solution.py:344
  8.3 3.3 %pack.4 = (bf16[2,96,1024]{2,1,0:T(8,128)(2,1)}, bf16[2,96,1024]{2,1,0:T(8,128)(2,1)}, bf16[2,96,1024]{2,1,0:T(8,128)(2,1)}, bf16[2,96,1024]{2,1,0:T(8,128)(2,1)}) custom-call(s32[8]{0:T(128)} %xor_add_fusion.refs_0_, bf16[272,1024]{1,0:T(8,128)(2,1)} %join.1.refs_1_.refs_2_, bf16[272,1024]{1,0:T(8,128)(2,1)} %join.1.refs_1_.refs_2_), custom_call_target="tpu_custom_call" | custom-call | tf_op jit(solution)/shard_map/pack/pallas_call | solution.py:426
  15.1 3.3 %collective-permute-start.7 = (bf16[272,1024]{1,0:T(8,128)(2,1)}, bf16[272,1024]{1,0:T(8,128)(2,1)S(1)}, u32[]{:S(2)}, u32[]{:S(2)}) collective-permute-start(bf16[272,1024]{1,0:T(8,128)(2,1)} %join.1.refs_1_.refs_2_), channel_id=1, source_target_pairs={{0,24},{1,25},{2,26},{3,27},{4,28},{5,29},{6,30},{7,31},{8,0},{9,1... | collective-permute-start | bytes 1671176 | tf_op jit(solution)/shard_map/ppermute | solution.py:344
  18.4 5.1 %collective-permute-done.6.refs_1_ = bf16[272,1024]{1,0:T(8,128)(2,1)} collective-permute-done((bf16[272,1024]{1,0:T(8,128)(2,1)}, bf16[272,1024]{1,0:T(8,128)(2,1)}, u32[]{:S(2)}, u32[]{:S(2)}) %collective-permute-start.6) | collective-permute-done | bytes 557088 | tf_op jit(solution)/shard_map/ppermute | solution.py:344
  23.5 2.8 %pack.5 = (bf16[2,96,1024]{2,1,0:T(8,128)(2,1)}, bf16[2,96,1024]{2,1,0:T(8,128)(2,1)}, bf16[2,96,1024]{2,1,0:T(8,128)(2,1)}, bf16[2,96,1024]{2,1,0:T(8,128)(2,1)}) custom-call(s32[8]{0:T(128)} %xor_add_fusion.refs_0_, bf16[272,1024]{1,0:T(8,128)(2,1)} %collective-permute-done.6.refs_1_, bf16[2,96,1024]{2,1,0:T(8,128)(2,1)} %get-tuple-element.87.refs_2_.refs_0_), custom_call_target="tpu_custom_call" | custom-call | tf_op jit(solution)/shard_map/pack/pallas_call | solution.py:426
  29.5 4.2 %collective-permute-done.5.refs_3_ = bf16[2,96,1024]{2,1,0:T(8,128)(2,1)S(1)} collective-permute-done((bf16[2,96,1024]{2,1,0:T(8,128)(2,1)}, bf16[2,96,1024]{2,1,0:T(8,128)(2,1)S(1)}, u32[]{:S(2)}, u32[]{:S(2)}) %collective-permute-start.5) | collective-permute-done | bytes 393248 | tf_op jit(solution)/shard_map/ppermute | solution.py:340
  36.2 6.1 %collective-permute-start.14 = (bf16[272,1024]{1,0:T(8,128)(2,1)}, bf16[272,1024]{1,0:T(8,128)(2,1)S(1)}, u32[]{:S(2)}, u32[]{:S(2)}) collective-permute-start(bf16[272,1024]{1,0:T(8,128)(2,1)} %join.1.refs_1_.refs_2_), channel_id=1, source_target_pairs={{0,16},{1,17},{2,18},{3,19},{4,20},{5,21},{6,22},{7,23},{8,24},{9,... | collective-permute-start | bytes 1671176 | tf_op jit(solution)/shard_map/ppermute | solution.py:344
  42.3 8.5 %expert.4 = (bf16[2,96,1024]{2,1,0:T(8,128)(2,1)}, bf16[2,96,1024]{2,1,0:T(8,128)(2,1)}, bf16[2,96,1024]{2,1,0:T(8,128)(2,1)}, bf16[2,96,1024]{2,1,0:T(8,128)(2,...) custom-call(bf16[2,96,1024]{2,1,0:T(8,128)(2,1)} %get-tuple-element., ...), custom_call_target="tpu_custom_call" | custom-call | tf_op jit(solution)/shard_map/expert/pallas_call | solution.py:431
  51.6 2.8 %pack.6 = (bf16[2,96,1024]{2,1,0:T(8,128)(2,1)}, bf16[2,96,1024]{2,1,0:T(8,128)(2,1)}, bf16[2,96,1024]{2,1,0:T(8,128)(2,1)}, bf16[2,96,1024]{2,1,0:T(8,128)(2,1)}) custom-call(s32[8]{0:T(128)} %xor_add_fusion.refs_0_, bf16[272,1024]{1,0:T(8,128)(2,1)} %copy-done.3, bf16[2,96,1024]{2,1,0:T(8,128)(2,1)} %get-tuple-element.92.refs_2_), custom_call_target="tpu_custom_call" | custom-call | tf_op jit(solution)/shard_map/pack/pallas_call | solution.py:426
  58.2 8.5 %expert.5 = (bf16[2,96,1024]{2,1,0:T(8,128)(2,1)}, bf16[2,96,1024]{2,1,0:T(8,128)(2,1)}, bf16[2,96,1024]{2,1,0:T(8,128)(2,1)}, bf16[2,96,1024]{2,1,0:T(8,128)(2,...) custom-call(bf16[2,96,1024]{2,1,0:T(8,128)(2,1)} %get-tuple-element., ...), custom_call_target="tpu_custom_call" | custom-call | tf_op jit(solution)/shard_map/expert/pallas_call | solution.py:431
  67.6 2.9 %pack.7 = (bf16[2,96,1024]{2,1,0:T(8,128)(2,1)}, bf16[2,96,1024]{2,1,0:T(8,128)(2,1)}, bf16[2,96,1024]{2,1,0:T(8,128)(2,1)}, bf16[2,96,1024]{2,1,0:T(8,128)(2,1)}) custom-call(s32[8]{0:T(128)} %xor_add_fusion.refs_0_, bf16[272,1024]{1,0:T(8,128)(2,1)} %copy-done.4, bf16[2,96,1024]{2,1,0:T(8,128)(2,1)} %get-tuple-element.107.refs_2_), custom_call_target="tpu_custom_call" | custom-call | tf_op jit(solution)/shard_map/pack/pallas_call | solution.py:426
  73.9 13.4 %collective-permute-done.16.refs_2_ = bf16[2,96,1024]{2,1,0:T(8,128)(2,1)S(1)} collective-permute-done((bf16[2,96,1024]{2,1,0:T(8,128)(2,1)}, bf16[2,96,1024]{2,1,0:T(8,128)(2,1)S(1)}, u32[]{:S(2)}, u32[]{:S(2)}) %collective-permute-start.16) | collective-permute-done | bytes 393248 | tf_op jit(solution)/shard_map/ppermute | solution.py:340
  89.0 3.8 %collective-permute-done.17.refs_3_ = bf16[2,96,1024]{2,1,0:T(8,128)(2,1)S(1)} collective-permute-done((bf16[2,96,1024]{2,1,0:T(8,128)(2,1)}, bf16[2,96,1024]{2,1,0:T(8,128)(2,1)S(1)}, u32[]{:S(2)}, u32[]{:S(2)}) %collective-permute-start.17) | collective-permute-done | bytes 393248 | tf_op jit(solution)/shard_map/ppermute | solution.py:340
  94.9 8.5 %expert.6 = (bf16[2,96,1024]{2,1,0:T(8,128)(2,1)}, bf16[2,96,1024]{2,1,0:T(8,128)(2,1)}, bf16[2,96,1024]{2,1,0:T(8,128)(2,1)}, bf16[2,96,1024]{2,1,0:T(8,128)(2,...) custom-call(bf16[2,96,1024]{2,1,0:T(8,128)(2,1)} %get-tuple-element., ...), custom_call_target="tpu_custom_call" | custom-call | tf_op jit(solution)/shard_map/expert/pallas_call | solution.py:431
  103.4 8.6 %expert.7 = (bf16[2,96,1024]{2,1,0:T(8,128)(2,1)}, bf16[2,96,1024]{2,1,0:T(8,128)(2,1)}, bf16[2,96,1024]{2,1,0:T(8,128)(2,1)}, bf16[2,96,1024]{2,1,0:T(8,128)(2,...) custom-call(bf16[2,96,1024]{2,1,0:T(8,128)(2,1)} %get-tuple-element., ...), custom_call_target="tpu_custom_call" | custom-call | tf_op jit(solution)/shard_map/expert/pallas_call | solution.py:431
  115.7 3.5 %merge.4.refs_6_ = bf16[272,1024]{1,0:T(8,128)(2,1)} custom-call(s32[8]{0:T(128)} %xor_add_fusion.refs_0_, bf16[272,1024]{1,0:T(8,128)(2,1)} %collective-permute-done.6.refs_1_, bf16[2,96,1024]{2,1,0:T(8,128)(2,1)} %get-tuple-element.107.refs_2_, bf16[2,96,1024]{2,1,0:T(8,128)(2,1)} %copy-done.27, bf16[2,96,1024]{2,1,0:T(8,128)(2,1)} %copy-done.28, ...), custom_call_target="tpu_custom_call" | custom-call | flops 60397977600 | bytes 2686976 | tf_op jit(solution)/shard_map/merge/pallas_call | solution.py:447
  120.2 4.0 %collective-permute-done.27.refs_5_ = bf16[2,96,1024]{2,1,0:T(8,128)(2,1)S(1)} collective-permute-done((bf16[2,96,1024]{2,1,0:T(8,128)(2,1)}, bf16[2,96,1024]{2,1,0:T(8,128)(2,1)S(1)}, u32[]{:S(2)}, u32[]{:S(2)}) %collective-permute-start.27) | collective-permute-done | bytes 393248 | tf_op jit(solution)/shard_map/ppermute | solution.py:340
  125.6 2.6 %collective-permute-done.23.refs_4_ = bf16[2,96,1024]{2,1,0:T(8,128)(2,1)S(1)} collective-permute-done((bf16[2,96,1024]{2,1,0:T(8,128)(2,1)}, bf16[2,96,1024]{2,1,0:T(8,128)(2,1)S(1)}, u32[]{:S(2)}, u32[]{:S(2)}) %collective-permute-start.23) | collective-permute-done | bytes 393248 | tf_op jit(solution)/shard_map/ppermute | solution.py:340
  130.3 3.4 %merge.5.refs_20_ = bf16[272,1024]{1,0:T(8,128)(2,1)} custom-call(s32[8]{0:T(128)} %xor_add_fusion.refs_0_, bf16[272,1024]{1,0:T(8,128)(2,1)} %copy-done.4, bf16[2,96,1024]{2,1,0:T(8,128)(2,1)} %get-tuple-element.139.refs_6_.refs_2_, bf16[2,96,1024]{2,1,0:T(8,128)(2,1)} %copy-done.36, bf16[2,96,1024]{2,1,0:T(8,128)(2,1)} %copy-done.35, ...), custom_call_target="tpu_custom_call" | custom-call | flops 60397977600 | bytes 2686976 | tf_op jit(solution)/shard_map/merge/pallas_call | solution.py:447
  134.9 7.8 %weight.2.refs_6_ = bf16[1536,1024]{1,0:T(8,128)(2,1)} custom-call(bf16[2,192,1024]{2,1,0:T(8,128)(2,1)} %get-tuple-element.140.refs_0_, bf16[2,192,1024]{2,1,0:T(8,128)(2,1)} %get-tuple-element.141.refs_1_, bf16[2,192,512]{2,1,0:T(8,128)(2,1)} %get-tuple-element.142.refs_2_, bf16[2,192,512]{2,1,0:T(8,128)(2,1)} %get-tuple-element.143.refs_3_, ...), custom_call_target="tpu_custom_call" | custom-call | flops 60397977600 | bytes 8650752 | tf_op jit(solution)/shard_map/weight/pallas_call | solution.py:440
  145.0 3.4 %merge.6.refs_21_ = bf16[272,1024]{1,0:T(8,128)(2,1)} custom-call(s32[8]{0:T(128)} %xor_add_fusion.refs_0_, bf16[272,1024]{1,0:T(8,128)(2,1)} %copy-done.3, bf16[2,96,1024]{2,1,0:T(8,128)(2,1)} %get-tuple-element.116.refs_10_.refs_2_, bf16[2,96,1024]{2,1,0:T(8,128)(2,1)} %copy-done.34, bf16[2,96,1024]{2,1,0:T(8,128)(2,1)} %copy-done.32, ...), custom_call_target="tpu_custom_call" | custom-call | flops 60397977600 | bytes 2686976 | tf_op jit(solution)/shard_map/merge/pallas_call | solution.py:447
  151.5 8.1 %weight.3 = (bf16[1024,512]{1,0:T(8,128)(2,1)}, bf16[1024,512]{1,0:T(8,128)(2,1)}, bf16[512,1024]{1,0:T(8,128)(2,1)}) custom-call(bf16[2,192,1024]{2,1,0:T(8,128)(2,1)} %get-tuple-element.140.refs_0_, bf16[2,192,1024]{2,1,0:T(8,128)(2,1)} %get-tuple-element.141.refs_1_, bf16[2,192,512]{2,1,0:T(8,128)(2,1)} %get-tuple-element.142.refs_2_, ...), custom_call_target="tpu_custom_call" | custom-call | flops 60397977600 | bytes 8650752 | tf_op jit(solution)/shard_map/weight/pallas_call | solution.py:444
  159.6 3.9 %collective-permute-done.25.refs_4_ = bf16[2,96,1024]{2,1,0:T(8,128)(2,1)S(1)} collective-permute-done((bf16[2,96,1024]{2,1,0:T(8,128)(2,1)S(1)}, bf16[2,96,1024]{2,1,0:T(8,128)(2,1)S(1)}, u32[]{:S(2)}, u32[]{:S(2)}) %collective-permute-start.25) | collective-permute-done | bytes 393248 | tf_op jit(solution)/shard_map/ppermute | solution.py:340
  166.9 3.8 %merge.7 = (bf16[128,1024]{1,0:T(8,128)(2,1)}, bf16[128,1024]{1,0:T(8,128)(2,1)}, f32[8,128]{1,0:T(8,128)}) custom-call(s32[8]{0:T(128)} %xor_add_fusion.refs_0_, bf16[272,1024]{1,0:T(8,128)(2,1)} %join.1.refs_1_.refs_2_, bf16[2,96,1024]{2,1,0:T(8,128)(2,1)} %get-tuple-element.92.refs_2_, bf16[2,96,1024]{2,1,0:T(8,128)(2,1)} %copy-done.29, ...), custom_call_target="tpu_custom_call" | custom-call | flops 60397977600 | bytes 2686976 | tf_op jit(solution)/shard_map/merge/pallas_call | solution.py:447
  (135 shorter events, 44.9 us)
Async XLA Ops:
  5.0 18.5 %collective-permute-start.6 = (bf16[272,1024]{1,0:T(8,128)(2,1)}, bf16[272,1024]{1,0:T(8,128)(2,1)}, u32[]{:S(2)}, u32[]{:S(2)}) collective-permute-start(bf16[272,1024]{1,0:T(8,128)(2,1)} %join.1.refs_1_.refs_2_), channel_id=1, source_target_pairs={{0,8},{1,9},{2,10},{3,11},{4,12},{5,13},{6,14},{7,15},{8,16},{9,17... | collective-permute-start | bytes 1671176 | tf_op jit(solution)/shard_map/ppermute | solution.py:344
  14.6 19.1 %collective-permute-start.5 = (bf16[2,96,1024]{2,1,0:T(8,128)(2,1)}, bf16[2,96,1024]{2,1,0:T(8,128)(2,1)S(1)}, u32[]{:S(2)}, u32[]{:S(2)}) collective-permute-start(bf16[2,96,1024]{2,1,0:T(8,128)(2,1)} %get-tuple-element.90), channel_id=1, source_target_pairs={{0,6},{1,7},{2,4},{3,5},{4,2},{5,3},{6,0},{7,1},{8,14},{9,15},{10,... | collective-permute-start | bytes 1179656 | tf_op jit(solution)/shard_map/ppermute | solution.py:340
  15.1 35.7 %collective-permute-start.7 = (bf16[272,1024]{1,0:T(8,128)(2,1)}, bf16[272,1024]{1,0:T(8,128)(2,1)S(1)}, u32[]{:S(2)}, u32[]{:S(2)}) collective-permute-start(bf16[272,1024]{1,0:T(8,128)(2,1)} %join.1.refs_1_.refs_2_), channel_id=1, source_target_pairs={{0,24},{1,25},{2,26},{3,27},{4,28},{5,29},{6,30},{7,31},{8,0},{9,1... | collective-permute-start | bytes 1671176 | tf_op jit(solution)/shard_map/ppermute | solution.py:344
  26.3 28.1 %collective-permute-start.10 = (bf16[2,96,1024]{2,1,0:T(8,128)(2,1)}, bf16[2,96,1024]{2,1,0:T(8,128)(2,1)S(1)}, u32[]{:S(2)}, u32[]{:S(2)}) collective-permute-start(bf16[2,96,1024]{2,1,0:T(8,128)(2,1)} %get-tuple-element.101), channel_id=1, source_target_pairs={{0,4},{1,5},{2,6},{3,7},{4,0},{5,1},{6,2},{7,3},{8,12},{9,13},{10,... | collective-permute-start | bytes 1179656 | tf_op jit(solution)/shard_map/ppermute | solution.py:340
  28.0 28.0 %collective-permute-start.8 = (bf16[2,96,1024]{2,1,0:T(8,128)(2,1)}, bf16[2,96,1024]{2,1,0:T(8,128)(2,1)S(1)}, u32[]{:S(2)}, u32[]{:S(2)}) collective-permute-start(bf16[2,96,1024]{2,1,0:T(8,128)(2,1)} %get-tuple-element.97), channel_id=1, source_target_pairs={{0,2},{1,3},{2,0},{3,1},{4,6},{5,7},{6,4},{7,5},{8,10},{9,11},{10,... | collective-permute-start | bytes 1179656 | tf_op jit(solution)/shard_map/ppermute | solution.py:340
  33.7 23.7 %collective-permute-start.12 = (bf16[2,96,1024]{2,1,0:T(8,128)(2,1)}, bf16[2,96,1024]{2,1,0:T(8,128)(2,1)S(1)}, u32[]{:S(2)}, u32[]{:S(2)}) collective-permute-start(bf16[2,96,1024]{2,1,0:T(8,128)(2,1)} %get-tuple-element.105), channel_id=1, source_target_pairs={{0,6},{1,7},{2,4},{3,5},{4,2},{5,3},{6,0},{7,1},{8,14},{9,15},{10,... | collective-permute-start | bytes 1179656 | tf_op jit(solution)/shard_map/ppermute | solution.py:340
  36.2 30.5 %collective-permute-start.14 = (bf16[272,1024]{1,0:T(8,128)(2,1)}, bf16[272,1024]{1,0:T(8,128)(2,1)S(1)}, u32[]{:S(2)}, u32[]{:S(2)}) collective-permute-start(bf16[272,1024]{1,0:T(8,128)(2,1)} %join.1.refs_1_.refs_2_), channel_id=1, source_target_pairs={{0,16},{1,17},{2,18},{3,19},{4,20},{5,21},{6,22},{7,23},{8,24},{9,... | collective-permute-start | bytes 1671176 | tf_op jit(solution)/shard_map/ppermute | solution.py:344
  54.4 16.0 %collective-permute-start.11 = (bf16[2,96,1024]{2,1,0:T(8,128)(2,1)}, bf16[2,96,1024]{2,1,0:T(8,128)(2,1)S(1)}, u32[]{:S(2)}, u32[]{:S(2)}) collective-permute-start(bf16[2,96,1024]{2,1,0:T(8,128)(2,1)} %get-tuple-element.102), channel_id=1, source_target_pairs={{0,4},{1,5},{2,6},{3,7},{4,0},{5,1},{6,2},{7,3},{8,12},{9,13},{10,... | collective-permute-start | bytes 1179656 | tf_op jit(solution)/shard_map/ppermute | solution.py:340
  56.0 15.7 %collective-permute-start.9 = (bf16[2,96,1024]{2,1,0:T(8,128)(2,1)}, bf16[2,96,1024]{2,1,0:T(8,128)(2,1)S(1)}, u32[]{:S(2)}, u32[]{:S(2)}) collective-permute-start(bf16[2,96,1024]{2,1,0:T(8,128)(2,1)} %get-tuple-element.98), channel_id=1, source_target_pairs={{0,2},{1,3},{2,0},{3,1},{4,6},{5,7},{6,4},{7,5},{8,10},{9,11},{10,... | collective-permute-start | bytes 1179656 | tf_op jit(solution)/shard_map/ppermute | solution.py:340
  57.5 15.7 %collective-permute-start.13 = (bf16[2,96,1024]{2,1,0:T(8,128)(2,1)}, bf16[2,96,1024]{2,1,0:T(8,128)(2,1)S(1)}, u32[]{:S(2)}, u32[]{:S(2)}) collective-permute-start(bf16[2,96,1024]{2,1,0:T(8,128)(2,1)} %get-tuple-element.106), channel_id=1, source_target_pairs={{0,6},{1,7},{2,4},{3,5},{4,2},{5,3},{6,0},{7,1},{8,14},{9,15},{10,... | collective-permute-start | bytes 1179656 | tf_op jit(solution)/shard_map/ppermute | solution.py:340
  70.4 16.9 %collective-permute-start.16 = (bf16[2,96,1024]{2,1,0:T(8,128)(2,1)}, bf16[2,96,1024]{2,1,0:T(8,128)(2,1)S(1)}, u32[]{:S(2)}, u32[]{:S(2)}) collective-permute-start(bf16[2,96,1024]{2,1,0:T(8,128)(2,1)} %get-tuple-element.113), channel_id=1, source_target_pairs={{0,4},{1,5},{2,6},{3,7},{4,0},{5,1},{6,2},{7,3},{8,12},{9,13},{10,... | collective-permute-start | bytes 1179656 | tf_op jit(solution)/shard_map/ppermute | solution.py:340
  71.7 15.6 %collective-permute-start.15 = (bf16[2,96,1024]{2,1,0:T(8,128)(2,1)}, bf16[2,96,1024]{2,1,0:T(8,128)(2,1)S(1)}, u32[]{:S(2)}, u32[]{:S(2)}) collective-permute-start(bf16[2,96,1024]{2,1,0:T(8,128)(2,1)} %get-tuple-element.111), channel_id=1, source_target_pairs={{0,2},{1,3},{2,0},{3,1},{4,6},{5,7},{6,4},{7,5},{8,10},{9,11},{10,... | collective-permute-start | bytes 1179656 | tf_op jit(solution)/shard_map/ppermute | solution.py:340
  73.2 19.5 %collective-permute-start.17 = (bf16[2,96,1024]{2,1,0:T(8,128)(2,1)}, bf16[2,96,1024]{2,1,0:T(8,128)(2,1)S(1)}, u32[]{:S(2)}, u32[]{:S(2)}) collective-permute-start(bf16[2,96,1024]{2,1,0:T(8,128)(2,1)} %get-tuple-element.115), channel_id=1, source_target_pairs={{0,6},{1,7},{2,4},{3,5},{4,2},{5,3},{6,0},{7,1},{8,14},{9,15},{10,... | collective-permute-start | bytes 1179656 | tf_op jit(solution)/shard_map/ppermute | solution.py:340
  87.3 24.7 %collective-permute-start.18 = (bf16[2,96,1024]{2,1,0:T(8,128)(2,1)}, bf16[2,96,1024]{2,1,0:T(8,128)(2,1)S(1)}, u32[]{:S(2)}, u32[]{:S(2)}) collective-permute-start(bf16[2,96,1024]{2,1,0:T(8,128)(2,1)} %get-tuple-element.119), channel_id=1, source_target_pairs={{0,2},{1,3},{2,0},{3,1},{4,6},{5,7},{6,4},{7,5},{8,10},{9,11},{10,... | collective-permute-start | bytes 1179656 | tf_op jit(solution)/shard_map/ppermute | solution.py:340
  87.4 24.7 %collective-permute-start.22 = (bf16[2,96,1024]{2,1,0:T(8,128)(2,1)}, bf16[2,96,1024]{2,1,0:T(8,128)(2,1)S(1)}, u32[]{:S(2)}, u32[]{:S(2)}) collective-permute-start(bf16[2,96,1024]{2,1,0:T(8,128)(2,1)} %get-tuple-element.127), channel_id=1, source_target_pairs={{0,4},{1,5},{2,6},{3,7},{4,0},{5,1},{6,2},{7,3},{8,12},{9,13},{10,... | collective-permute-start | bytes 1179656 | tf_op jit(solution)/shard_map/ppermute | solution.py:340
  92.7 19.4 %collective-permute-start.26 = (bf16[2,96,1024]{2,1,0:T(8,128)(2,1)}, bf16[2,96,1024]{2,1,0:T(8,128)(2,1)S(1)}, u32[]{:S(2)}, u32[]{:S(2)}) collective-permute-start(bf16[2,96,1024]{2,1,0:T(8,128)(2,1)} %get-tuple-element.135), channel_id=1, source_target_pairs={{0,6},{1,7},{2,4},{3,5},{4,2},{5,3},{6,0},{7,1},{8,14},{9,15},{10,... | collective-permute-start | bytes 1179656 | tf_op jit(solution)/shard_map/ppermute | solution.py:340
  112.9 15.3 %collective-permute-start.23 = (bf16[2,96,1024]{2,1,0:T(8,128)(2,1)}, bf16[2,96,1024]{2,1,0:T(8,128)(2,1)S(1)}, u32[]{:S(2)}, u32[]{:S(2)}) collective-permute-start(bf16[2,96,1024]{2,1,0:T(8,128)(2,1)} %get-tuple-element.128), channel_id=1, source_target_pairs={{0,4},{1,5},{2,6},{3,7},{4,0},{5,1},{6,2},{7,3},{8,12},{9,13},{10,... | collective-permute-start | bytes 1179656 | tf_op jit(solution)/shard_map/ppermute | solution.py:340
  119.2 29.3 %collective-permute-start.30 = (bf16[272,1024]{1,0:T(8,128)(2,1)}, bf16[272,1024]{1,0:T(8,128)(2,1)}, u32[]{:S(2)}, u32[]{:S(2)}) collective-permute-start(bf16[272,1024]{1,0:T(8,128)(2,1)} %merge.4.refs_6_), channel_id=1, source_target_pairs={{0,24},{1,25},{2,26},{3,27},{4,28},{5,29},{6,30},{7,31},{8,0},{9,1... | collective-permute-start | bytes 1671176 | tf_op jit(solution)/shard_map/ppermute | solution.py:344
  124.2 18.4 %collective-permute-start.28 = (bf16[2,96,1024]{2,1,0:T(8,128)(2,1)S(1)}, bf16[2,96,1024]{2,1,0:T(8,128)(2,1)S(1)}, u32[]{:S(2)}, u32[]{:S(2)}) collective-permute-start(bf16[2,96,1024]{2,1,0:T(8,128)(2,1)S(1)} %copy-done.24), channel_id=1, source_target_pairs={{0,6},{1,7},{2,4},{3,5},{4,2},{5,3},{6,0},{7,1},{8,14},{9,15},{10,... | collective-permute-start | bytes 1179656 | tf_op jit(solution)/shard_map/ppermute | solution.py:340
  133.7 25.9 %collective-permute-start.31 = (bf16[272,1024]{1,0:T(8,128)(2,1)}, bf16[272,1024]{1,0:T(8,128)(2,1)}, u32[]{:S(2)}, u32[]{:S(2)}) collective-permute-start(bf16[272,1024]{1,0:T(8,128)(2,1)} %merge.5.refs_20_), channel_id=1, source_target_pairs={{0,16},{1,17},{2,18},{3,19},{4,20},{5,21},{6,22},{7,23},{8,24},{9,... | collective-permute-start | bytes 1671176 | tf_op jit(solution)/shard_map/ppermute | solution.py:344
  142.7 16.9 %collective-permute-start.29 = (bf16[2,96,1024]{2,1,0:T(8,128)(2,1)S(1)}, bf16[2,96,1024]{2,1,0:T(8,128)(2,1)S(1)}, u32[]{:S(2)}, u32[]{:S(2)}) collective-permute-start(bf16[2,96,1024]{2,1,0:T(8,128)(2,1)S(1)} %copy-done.21), channel_id=1, source_target_pairs={{0,6},{1,7},{2,4},{3,5},{4,2},{5,3},{6,0},{7,1},{8,14},{9,15},{10,... | collective-permute-start | bytes 1179656 | tf_op jit(solution)/shard_map/ppermute | solution.py:340
  143.8 19.7 %collective-permute-start.25 = (bf16[2,96,1024]{2,1,0:T(8,128)(2,1)S(1)}, bf16[2,96,1024]{2,1,0:T(8,128)(2,1)S(1)}, u32[]{:S(2)}, u32[]{:S(2)}) collective-permute-start(bf16[2,96,1024]{2,1,0:T(8,128)(2,1)S(1)} %copy-done.20), channel_id=1, source_target_pairs={{0,4},{1,5},{2,6},{3,7},{4,0},{5,1},{6,2},{7,3},{8,12},{9,13},{10,... | collective-permute-start | bytes 1179656 | tf_op jit(solution)/shard_map/ppermute | solution.py:340
  148.5 15.1 %collective-permute-start.21 = (bf16[2,96,1024]{2,1,0:T(8,128)(2,1)S(1)}, bf16[2,96,1024]{2,1,0:T(8,128)(2,1)S(1)}, u32[]{:S(2)}, u32[]{:S(2)}) collective-permute-start(bf16[2,96,1024]{2,1,0:T(8,128)(2,1)S(1)} %copy-done.19), channel_id=1, source_target_pairs={{0,2},{1,3},{2,0},{3,1},{4,6},{5,7},{6,4},{7,5},{8,10},{9,11},{10,... | collective-permute-start | bytes 1179656 | tf_op jit(solution)/shard_map/ppermute | solution.py:340
  149.9 16.2 %collective-permute-start.32 = (bf16[272,1024]{1,0:T(8,128)(2,1)}, bf16[272,1024]{1,0:T(8,128)(2,1)S(1)}, u32[]{:S(2)}, u32[]{:S(2)}) collective-permute-start(bf16[272,1024]{1,0:T(8,128)(2,1)} %merge.6.refs_21_), channel_id=1, source_target_pairs={{0,8},{1,9},{2,10},{3,11},{4,12},{5,13},{6,14},{7,15},{8,16},{9,17... | collective-permute-start | bytes 1671176 | tf_op jit(solution)/shard_map/ppermute | solution.py:344
  (47 other events, 471.9 us)
